TPU v7x, 128 devices: a whole 4x4x4 slice. The times are simulated.
128 devices in a mesh: seq: 16 (over y, x_lo, core), rows: 8 (over x_hi, z).
Axes of the slice: x: 4 (x_hi: 2, x_lo: 2; x = x_hi * 2 + x_lo), y: 4, z: 4, core: 2. Of those that a mesh axis runs over, the one named last changes fastest.
Arguments:
- inputs: bfloat16 [8, 2048, 1024], P('rows', 'seq'), may hold values from -6 to 6
- cotangent: bfloat16 [8, 2048, 1024], P('rows', 'seq'), may hold values from -6 to 6
- group_order: int32 [32], replicated, may hold values from 0 to 31, each once
- ln_gain: float32 [1024], replicated, may hold values from 0.1 to 1.9
- ln_bias: float32 [1024], replicated, may hold values from -3 to 3
- w_qkv: bfloat16 [1024, 3072], replicated, may hold values from -0.1875 to 0.1875
- b_qkv: float32 [3072], replicated, may hold values from -0.3 to 0.3
- w_out: bfloat16 [1024, 1024], replicated, may hold values from -3 to 3
- w_gate: bfloat16 [1024, 2816], replicated, may hold values from -0.1875 to 0.1875
- w_up: bfloat16 [1024, 2816], replicated, may hold values from -0.1875 to 0.1875
- w_down: bfloat16 [2816, 1024], replicated, may hold values from -0.109375 to 0.109375
Outputs:
- output: bfloat16 [8, 2048, 1024], P('rows', 'seq')
- input_grad: bfloat16 [8, 2048, 1024], P('rows', 'seq')
- grad_qkv: float32 [1024, 3072], P(('seq', 'rows'))
- grad_out: float32 [1024, 1024], P(('seq', 'rows'))
- grad_gate: float32 [1024, 2816], P(('seq', 'rows'))
- grad_up: float32 [1024, 2816], P(('seq', 'rows'))
- grad_down: float32 [2816, 1024], P(('seq', 'rows'))
- grad_qkv_bias: float32 [3072], P(('seq', 'rows'))
- grad_ln_gain: float32 [1024], P(('seq', 'rows'))
- grad_ln_bias: float32 [1024], P(('seq', 'rows'))
Inputs may be any that keep to these rules, and one draw needn't show every extreme that they name: `group_order`: a permutation of the group numbers 0 to 31.
All inputs are finite; a program needn't handle non-finite values.
Results may differ from a plain program's by a relative error of at most 0.014.
Values may be sent and summed in bfloat16 or wider, within the bound.
No kernel may reach another device: no remote copies, remote signals or barrier semaphores. Data moves between devices by JAX's collectives and lax.ppermute only.
A program may use at most 192 MiB of HBM per device.

v0:
```python
import jax
import jax.numpy as jnp
import numpy as np
from jax import lax
from jax.experimental import pallas as pl
from jax.experimental.pallas import tpu as pltpu
from jax.sharding import PartitionSpec as P

HEADS = 16
HEAD_DIM = 64
ROT = 16
GROUP = 64
LENGTH = 2048
WIDTH = 1024
FF = 2816
FF_LOCAL = 176
BLOCK = 256
SEQ = 16
ROWS = 8
HERE = 128
epsilon = 1e-05
f32 = jnp.float32
bf16 = jnp.bfloat16
SMEM = pl.BlockSpec(memory_space=pltpu.SMEM)
VMEM = pl.BlockSpec(memory_space=pltpu.VMEM)
ANY = pl.BlockSpec(memory_space=pl.ANY)


def dot_nn(a, b):
    return lax.dot_general(a, b, (((1,), (0,)), ((), ())), preferred_element_type=f32)


def dot_nt(a, b):
    return lax.dot_general(a, b, (((1,), (1,)), ((), ())), preferred_element_type=f32)


def dot_tn(a, b):
    return lax.dot_general(a, b, (((0,), (0,)), ((), ())), preferred_element_type=f32)


def params(mib):
    return pltpu.CompilerParams(vmem_limit_bytes=mib * 1024 * 1024)


def cost(gflop, mib, exps=0):
    return pl.CostEstimate(
        flops=int(gflop * 1e9), bytes_accessed=int(mib * 2**20), transcendentals=int(exps)
    )


def normalise(rows):
    rows = rows.astype(f32)
    mean = jnp.mean(rows, 1, keepdims=True)
    centred = rows - mean
    inv_std = lax.rsqrt(jnp.mean(centred * centred, 1, keepdims=True) + epsilon)
    return centred * inv_std, inv_std


def gated(gate, up, grad_act):
    sig = 1.0 / (1.0 + jnp.exp(-gate))
    silu = gate * sig
    grad_g = grad_act * up * (sig * (1.0 + gate - silu))
    grad_u = grad_act * silu
    return (silu * up).astype(bf16), grad_g.astype(bf16), grad_u.astype(bf16)


def rotary_tables():
    half = ROT // 2
    lane = np.arange(2 * HEAD_DIM) % HEAD_DIM
    frequency = np.where(lane < ROT, 10000.0 ** (-(lane % half) * (2.0 / ROT)), 0.0)
    groups = np.arange(LENGTH // GROUP)[:, None] * GROUP * frequency
    inside = np.arange(GROUP)[:, None] * frequency
    parts = (np.cos(groups), np.sin(groups), np.cos(inside), np.sin(inside))
    return [jnp.asarray(part, f32) for part in parts]


def own_kernel(x, dy, gain, bias, wg, wu, wd, out, grad, hid):
    @pl.when(pl.program_id(0) == 0)
    def _():
        unit, _ = normalise(x[...])
        hid[...] = (unit * gain[...] + bias[...]).astype(bf16)
        out[...] = x[...].astype(f32)
        grad[...] = jnp.zeros_like(grad)

    gate = dot_nn(hid[...], wg[...])
    up = dot_nn(hid[...], wu[...])
    act, grad_g, grad_u = gated(gate, up, dot_nt(dy[...], wd[...]))
    out[...] += dot_nn(act, wd[...])
    grad[...] += dot_nt(grad_g, wg[...]) + dot_nt(grad_u, wu[...])


def own_rows(x, dy, gain, bias, w_gate, w_up, w_down):
    whole = pl.BlockSpec((HERE, WIDTH), lambda j: (0, 0))
    vector = pl.BlockSpec((1, WIDTH), lambda j: (0, 0))
    columns = pl.BlockSpec((WIDTH, BLOCK), lambda j: (0, j))
    return pl.pallas_call(
        own_kernel,
        grid=(FF // BLOCK,),
        out_shape=[jax.ShapeDtypeStruct((HERE, WIDTH), f32)] * 2,
        in_specs=[whole, whole, vector, vector, columns, columns]
        + [pl.BlockSpec((BLOCK, WIDTH), lambda j: (j, 0))],
        out_specs=[whole, whole],
        scratch_shapes=[pltpu.VMEM((HERE, WIDTH), bf16)],
        compiler_params=params(60),
        cost_estimate=cost(4.5, 18),
        name="own_rows",
    )(x, dy, gain, bias, w_gate, w_up, w_down)


def project_kernel(pieces, n_refs, slot, order, *refs):
    inputs, refs = refs[:n_refs], refs[n_refs:]
    w_qkv, b_qkv, w_o, gain, bias, cos_g, sin_g, cos_i, sin_i = refs[:9]
    unit_out, hid_out, dy_out, packed = refs[9:13]
    x_all, dy_all, unit, hid, piece_sems, out_sems = refs[13:]
    copies = []
    for i, (which, ref, at, rows, chip, offset) in enumerate(pieces):
        to = pl.multiple_of(slot[chip] * HERE + offset, 16)
        copy = pltpu.make_async_copy(
            inputs[ref].at[pl.ds(at, rows), :],
            (x_all, dy_all)[which].at[pl.ds(to, rows), :],
            piece_sems.at[i],
        )
        copy.start()
        copies.append(copy)
    for copy in copies:
        copy.wait()
    dy_copy = pltpu.make_async_copy(dy_all, dy_out, out_sems.at[2, 0])
    dy_copy.start()
    lanes = 2 * HEAD_DIM
    lane = lax.broadcasted_iota(jnp.int32, (1, lanes), 1)
    low = lane % HEAD_DIM < ROT // 2
    scale = jnp.where(lane < HEAD_DIM, HEAD_DIM**-0.5, 1.0)

    def out_copies(i):
        rows = pl.ds(pl.multiple_of(i * BLOCK, BLOCK), BLOCK)
        return [
            pltpu.make_async_copy(unit.at[rows, :], unit_out.at[rows, :], out_sems.at[0, i]),
            pltpu.make_async_copy(hid.at[rows, :], hid_out.at[rows, :], out_sems.at[1, i]),
        ]

    def step(i, carry):
        rows = pl.ds(pl.multiple_of(i * BLOCK, BLOCK), BLOCK)
        unit_f, _ = normalise(x_all[rows, :])
        hidden = (unit_f * gain[...] + bias[...]).astype(bf16)
        unit[rows, :] = unit_f.astype(bf16)
        hid[rows, :] = hidden
        for copy in out_copies(i):
            copy.start()
        qkv = dot_nn(hidden, w_qkv[...]) + b_qkv[...]
        grad_att = dot_nt(dy_all[rows, :], w_o[...])
        raw = qkv[:, :lanes]
        before, after = pltpu.roll(raw, ROT // 2, 1), pltpu.roll(raw, lanes - ROT // 2, 1)
        for g in range(BLOCK // GROUP):
            at = pl.ds(order[i * (BLOCK // GROUP) + g], 1)
            cg, sg = cos_g[at, :], sin_g[at, :]
            cosine = cg * cos_i[...] - sg * sin_i[...]
            sine = sg * cos_i[...] + cg * sin_i[...]
            part = slice(g * GROUP, (g + 1) * GROUP)
            turned = raw[part] * cosine + jnp.where(low, -after[part], before[part]) * sine
            packed[pl.ds(pl.multiple_of(i * BLOCK + g * GROUP, GROUP), GROUP), :lanes] = (
                turned * scale
            ).astype(bf16)
        packed[rows, lanes:] = jnp.concatenate(
            [qkv[:, lanes : lanes + HEAD_DIM], grad_att], 1
        ).astype(bf16)
        return carry

    lax.fori_loop(0, LENGTH // BLOCK, step, 0, unroll=2)
    for i in range(LENGTH // BLOCK):
        for copy in out_copies(i):
            copy.wait()
    dy_copy.wait()


def project(slot, order, arrays, pieces, w_qkv, b_qkv, w_o, gain, bias, tables):
    big = (LENGTH, WIDTH)
    return pl.pallas_call(
        lambda *refs: project_kernel(pieces, len(arrays), *refs),
        out_shape=[jax.ShapeDtypeStruct(big, bf16)] * 3
        + [jax.ShapeDtypeStruct((LENGTH, 4 * HEAD_DIM), bf16)],
        in_specs=[SMEM] * 2 + [ANY] * len(arrays) + [VMEM] * 9,
        out_specs=[ANY] * 3 + [VMEM],
        scratch_shapes=[pltpu.VMEM(big, bf16)] * 4
        + [
            pltpu.SemaphoreType.DMA((len(pieces),)),
            pltpu.SemaphoreType.DMA((3, LENGTH // BLOCK)),
        ],
        compiler_params=params(28),
        cost_estimate=cost(2, 20),
        name="project",
    )(slot, order, *arrays, w_qkv, b_qkv, w_o, gain, bias, *tables)


def attention_kernel(order, packed, cos_g, sin_g, cos_i, sin_i, out_ref, rows_in, dkv, res, turn):
    groups = LENGTH // GROUP
    for g in range(groups):
        at = pl.multiple_of(order[g] * GROUP, GROUP)
        rows_in[pl.ds(at, GROUP), :] = packed[g * GROUP : (g + 1) * GROUP, :]
    q = rows_in[:, :HEAD_DIM]
    k = rows_in[:, HEAD_DIM : 2 * HEAD_DIM]
    v = rows_in[:, 2 * HEAD_DIM : 3 * HEAD_DIM]
    do = rows_in[:, 3 * HEAD_DIM :]
    k_t = k.astype(f32).T.astype(bf16)
    v_t = v.astype(f32).T.astype(bf16)
    dkv[...] = jnp.zeros_like(dkv)
    row = lax.broadcasted_iota(jnp.int32, (BLOCK, BLOCK), 0)
    col = lax.broadcasted_iota(jnp.int32, (BLOCK, BLOCK), 1)
    visible = row <= col
    for i in range(LENGTH // BLOCK):
        lo, n = i * BLOCK, (i + 1) * BLOCK
        q_i, do_i = q[lo:n], do[lo:n]
        scores = dot_nt(k[:n], q_i)
        last = jnp.where(visible, scores[lo:], -1e30)
        scores = last if i == 0 else jnp.concatenate([scores[:lo], last], 0)
        top = jnp.max(scores, 0, keepdims=True)
        weights = jnp.exp(scores - top)
        inverse = 1.0 / jnp.sum(weights, 0, keepdims=True)
        weights_b = weights.astype(bf16)
        att_t = dot_nn(v_t[:, :n], weights_b) * inverse
        grad_p = dot_nt(v[:n], do_i)
        do_f = do_i.astype(f32)
        delta = jnp.sum(att_t * do_f.T, 0, keepdims=True)
        grad_s = (weights * (grad_p - delta)).astype(bf16)
        dq_t = dot_nn(k_t[:, :n], grad_s) * (inverse * HEAD_DIM**-0.5)
        scale = column(inverse)
        dkv[:n, :HEAD_DIM] += dot_nn(grad_s, (q_i.astype(f32) * scale).astype(bf16))
        dkv[:n, HEAD_DIM:] += dot_nn(weights_b, (do_f * scale).astype(bf16))
        res[lo:n, :] = jnp.concatenate([att_t.T, dq_t.T], 1)
    lanes = 2 * HEAD_DIM
    low = lax.broadcasted_iota(jnp.int32, (1, lanes), 1) % HEAD_DIM < ROT // 2
    for g in range(groups):
        part = slice(g * GROUP, (g + 1) * GROUP)
        cg, sg = cos_g[g : g + 1, :], sin_g[g : g + 1, :]
        cosine = cg * cos_i[...] - sg * sin_i[...]
        sine = sg * cos_i[...] + cg * sin_i[...]
        grads = jnp.concatenate([res[part, HEAD_DIM:], dkv[part, :HEAD_DIM]], 1)
        after = pltpu.roll(grads, lanes - ROT // 2, 1)
        before = pltpu.roll(grads, ROT // 2, 1)
        turn[part, :lanes] = (
            grads * cosine + jnp.where(low, after, -before) * sine
        ).astype(bf16)
        turn[part, lanes:] = jnp.concatenate(
            [dkv[part, HEAD_DIM:], res[part, :HEAD_DIM]], 1
        ).astype(bf16)
    for g in range(groups):
        at = pl.multiple_of(order[g] * GROUP, GROUP)
        out_ref[g * GROUP : (g + 1) * GROUP, :] = turn[pl.ds(at, GROUP), :]


def attention(order, packed, tables):
    lanes = 2 * HEAD_DIM
    return pl.pallas_call(
        attention_kernel,
        out_shape=jax.ShapeDtypeStruct((LENGTH, 2 * lanes), bf16),
        in_specs=[SMEM] + [VMEM] * 5,
        out_specs=VMEM,
        scratch_shapes=[
            pltpu.VMEM((LENGTH, 2 * lanes), bf16),
            pltpu.VMEM((LENGTH, lanes), f32),
            pltpu.VMEM((LENGTH, lanes), f32),
            pltpu.VMEM((LENGTH, 2 * lanes), bf16),
        ],
        compiler_params=params(28),
        cost_estimate=cost(15, 8, LENGTH * LENGTH // 2),
        name="attention",
    )(order, packed, *tables)


def column(row):
    return jnp.broadcast_to(row, (8, row.shape[1])).T[:, :1]


def weights_kernel(
    unit_in, hid_in, dy_in, heads, w_qkv, w_g, w_u, w_d, gain, bias, block,
    unit, hid, dy, acts, grads_g, grads_u, stage, sems,
):
    blocks = LENGTH // BLOCK

    def copies(i):
        rows = pl.ds(pl.multiple_of(i * BLOCK, BLOCK), BLOCK)
        return [
            pltpu.make_async_copy(src.at[rows, :], to.at[rows, :], sems.at[j, i])
            for j, (src, to) in enumerate(((hid_in, hid), (dy_in, dy), (unit_in, unit)))
        ]

    for j in range(3):
        for i in range(blocks):
            copies(i)[j].start()

    def step(i, totals):
        rows = pl.ds(pl.multiple_of(i * BLOCK, BLOCK), BLOCK)
        for copy in copies(i)[:2]:
            copy.wait()
        gate = dot_nn(hid[rows, :], w_g[...])
        up = dot_nn(hid[rows, :], w_u[...])
        act, grad_g, grad_u = gated(gate, up, dot_nt(dy[rows, :], w_d[...]))
        acts[rows, :] = act
        grads_g[rows, :] = grad_g
        grads_u[rows, :] = grad_u
        return (
            totals[0] + jnp.sum(grad_g.astype(f32), 0, keepdims=True),
            totals[1] + jnp.sum(grad_u.astype(f32), 0, keepdims=True),
        )

    zero = jnp.zeros((1, FF_LOCAL), f32)
    totals = lax.fori_loop(0, blocks, step, (zero, zero), unroll=2)
    for i in range(blocks):
        copies(i)[2].wait()
    gain_col, bias_col = column(gain[...]), column(bias[...])
    grads_all = heads[...]
    total_h = jnp.sum(grads_all.astype(f32), 0, keepdims=True)
    inner = [dot_tn(grads, unit[...]).T for grads in (grads_g[...], grads_u[...], grads_all)]
    terms, gain_part, bias_part = [], 0.0, 0.0
    for one, weights, total in zip(inner, (w_g, w_u, w_qkv), totals + (total_h,)):
        wide = weights[...].astype(f32)
        terms.append(one * gain_col + bias_col * total)
        gain_part += jnp.sum(one * wide, 1, keepdims=True)
        bias_part += jnp.sum(wide * total, 1, keepdims=True)
    row8 = lax.broadcasted_iota(jnp.int32, (8, 256), 0)
    lane8 = lax.broadcasted_iota(jnp.int32, (8, 256), 1)
    spread = jnp.where((lane8 // 24 == row8) & (lane8 < 192), total_h, 0.0).astype(bf16)
    pick_row = lax.broadcasted_iota(jnp.int32, (256, 256), 0)
    pick_lane = lax.broadcasted_iota(jnp.int32, (256, 256), 1)
    pick = ((pick_row % 24 + 192 == pick_lane) & (pick_row < 192)).astype(bf16)
    extra = dot_nn(spread, pick)
    lane = lax.broadcasted_iota(jnp.int32, (1, 256), 1)
    last = jnp.where(lane < 192, terms[2], 0.0).reshape(HERE, 8, 256) + extra[None]
    stage[:, :384] = jnp.concatenate(
        terms[:2] + [gain_part, bias_part, jnp.zeros((WIDTH, 30), f32)], 1
    )
    stage[:, 384:] = last.reshape(WIDTH, 256)
    down_all = dot_tn(acts[...], dy[...])
    out_all = dot_tn(grads_all[:, 3 * HEAD_DIM :], dy[...])
    for r in range(ROWS):
        for s in range(0, SEQ, 2):
            first, second = (s * ROWS + r) * 8, ((s + 1) * ROWS + r) * 8
            block[r, s * 8 : s * 8 + 16, :] = jnp.concatenate(
                [stage[first : first + 8, :], stage[second : second + 8, :]], 0
            ).astype(bf16)
        both = jnp.concatenate(
            [out_all[r * 8 : r * 8 + 8], down_all[r * 22 : (r + 1) * 22], jnp.zeros((2, WIDTH), f32)],
            0,
        ).astype(bf16)
        block[r, HERE : HERE + 32, :] = both[:, :640]
        block[r, HERE + 32 :, :384] = both[:, 640:]
        block[r, HERE + 32 :, 384:] = jnp.zeros((32, 256), bf16)


def weight_grads(unit, hid, dy, heads, w_qkv, w_g, w_u, w_d, gain, bias):
    big = (LENGTH, WIDTH)
    return pl.pallas_call(
        weights_kernel,
        out_shape=jax.ShapeDtypeStruct((ROWS, 192, 640), bf16),
        in_specs=[ANY] * 3 + [VMEM] * 7,
        out_specs=VMEM,
        scratch_shapes=[pltpu.VMEM(big, bf16)] * 3
        + [pltpu.VMEM((LENGTH, FF_LOCAL), bf16)] * 3
        + [pltpu.VMEM((WIDTH, 640), f32), pltpu.SemaphoreType.DMA((3, LENGTH // BLOCK))],
        compiler_params=params(40),
        cost_estimate=cost(8, 20),
        name="weight_grads",
    )(unit, hid, dy, heads, w_qkv, w_g, w_u, w_d, gain, bias)


def final_kernel(heads, x, dy, part, grad, gain, w_out, w_qkv, out, input_grad, att, rows, total):
    step = pl.program_id(0)

    @pl.when(step == 0)
    def _():
        for h in range(HEADS):
            here = heads[h * HERE : (h + 1) * HERE, :]
            at = h * HEAD_DIM
            for i in range(3):
                lo = i * WIDTH + at
                rows[:, lo : lo + HEAD_DIM] = here[:, i * HEAD_DIM : (i + 1) * HEAD_DIM]
            att[:, at : at + HEAD_DIM] = here[:, 3 * HEAD_DIM :]

    columns = pl.ds(pl.multiple_of(step * BLOCK, BLOCK), BLOCK)
    out[:, columns] = (part[:, columns] + dot_nn(att[...], w_out[...])).astype(bf16)
    total[:, columns] = grad[:, columns] + dot_nt(rows[...], w_qkv[...])

    @pl.when(step == pl.num_programs(0) - 1)
    def _():
        unit, inv_std = normalise(x[...])
        grad_unit = total[...] * gain[...]
        grad_norm = inv_std * (
            grad_unit
            - jnp.mean(grad_unit, 1, keepdims=True)
            - unit * jnp.mean(grad_unit * unit, 1, keepdims=True)
        )
        input_grad[...] = (dy[...].astype(f32) + grad_norm).astype(bf16)


def final_rows(heads, x, dy, part, grad, gain, w_out, w_qkv):
    fixed = lambda shape: pl.BlockSpec(shape, lambda j: (0,) * len(shape))
    own = fixed((HERE, WIDTH))
    return pl.pallas_call(
        final_kernel,
        grid=(WIDTH // BLOCK,),
        out_shape=[jax.ShapeDtypeStruct((HERE, WIDTH), bf16)] * 2,
        in_specs=[fixed((LENGTH, 256)), own, own, own, own, fixed((1, WIDTH))]
        + [pl.BlockSpec((WIDTH, BLOCK), lambda j: (0, j))]
        + [pl.BlockSpec((BLOCK, 3 * WIDTH), lambda j: (j, 0))],
        out_specs=[own, own],
        scratch_shapes=[
            pltpu.VMEM((HERE, WIDTH), bf16),
            pltpu.VMEM((HERE, 3 * WIDTH), bf16),
            pltpu.VMEM((HERE, WIDTH), f32),
        ],
        compiler_params=params(24),
        cost_estimate=cost(1.1, 10),
        name="final_rows",
    )(heads, x, dy, part, grad, gain, w_out, w_qkv)


def sum_kernel(got, send, down, out):
    total = got[0].astype(f32)
    for r in range(1, ROWS):
        total += got[r].astype(f32)
    send[...] = total[:HERE].astype(bf16)
    first, second = total[HERE : HERE + 32], total[HERE + 32 :, :384]
    out[:, :640] = first[:8]
    out[:, 640:] = second[:8]
    down[:, :640] = first[8:30]
    down[:, 640:] = second[8:30]


def sum_rows(got):
    return pl.pallas_call(
        sum_kernel,
        out_shape=[
            jax.ShapeDtypeStruct((HERE, 640), bf16),
            jax.ShapeDtypeStruct((22, WIDTH), f32),
            jax.ShapeDtypeStruct((8, WIDTH), f32),
        ],
        in_specs=[VMEM],
        out_specs=[VMEM] * 3,
        compiler_params=params(16),
        cost_estimate=cost(0.001, 2),
        name="sum_rows",
    )(got)


def layout_kernel(mine, qkv, gate, up, vectors, extra):
    total = jnp.zeros((8, 256), f32)
    more = jnp.zeros((8, 128), f32)
    for s in range(SEQ):
        here = mine[s * 8 : (s + 1) * 8, :].astype(f32)
        gate[:, s * FF_LOCAL : (s + 1) * FF_LOCAL] = here[:, :FF_LOCAL]
        up[:, s * FF_LOCAL : (s + 1) * FF_LOCAL] = here[:, FF_LOCAL : 2 * FF_LOCAL]
        for i in range(3):
            lo = i * WIDTH + s * HEAD_DIM
            qkv[:, lo : lo + HEAD_DIM] = here[:, 384 + i * HEAD_DIM : 384 + (i + 1) * HEAD_DIM]
        total += here[:, 384:]
        more += here[:, 256:384]
        extra[s * 8 : (s + 1) * 8, :] = here[:, 576:600]
    vectors[:, 0:1] = total[:, 216:217] + more[:, 96:97]
    vectors[:, 1:2] = total[:, 217:218] + more[:, 97:98]


def last_layout(mine):
    return pl.pallas_call(
        layout_kernel,
        out_shape=[
            jax.ShapeDtypeStruct((8, 3 * WIDTH), f32),
            jax.ShapeDtypeStruct((8, FF), f32),
            jax.ShapeDtypeStruct((8, FF), f32),
            jax.ShapeDtypeStruct((8, 2), f32),
            jax.ShapeDtypeStruct((HERE, 24), f32),
        ],
        in_specs=[VMEM],
        out_specs=[VMEM] * 5,
        compiler_params=params(16),
        cost_estimate=cost(0.001, 1),
        name="last_layout",
    )(mine)


PLACES = [(across, up) for across in (0, 1) for up in (-1, 0, 1, 2)]
CORE = [(i, i ^ 1) for i in range(SEQ)]
PAIR = [(i, i ^ 2) for i in range(SEQ)]
UP = [(i, (i + 4) % SEQ) for i in range(SEQ)]
DOWN = [(i, (i + 12) % SEQ) for i in range(SEQ)]


def send(value, to):
    return lax.ppermute(value, "seq", to)


def gather(x, dy, early):
    half = HERE
    own = jnp.concatenate([x, dy], 0)
    below = send(own, UP)
    above = send(own, DOWN)
    pair = send(own, PAIR)
    below, pair, early = lax.optimization_barrier((below, pair, early))
    far = send(below, UP)
    across_above = send(pair, DOWN)
    across_below = send(below, PAIR)
    cuts = (0, 80, 160, 256)
    last = [
        send(block[cuts[i] : cuts[i + 1]], to)
        for i, (block, to) in enumerate(((across_below, UP), (across_above, DOWN), (far, PAIR)))
    ]
    arrays = [own, below, above, pair, far, across_above, across_below] + last
    chips = [(0, 0), (0, -1), (0, 1), (1, 0), (0, 2), (1, 1), (1, -1)]
    pieces = []
    for a, chip in enumerate(chips):
        pieces += [(0, a, 0, half, chip, 0), (1, a, half, half, chip, 0)]
    end = (1, 2)
    pieces += [(0, 7, 0, 80, end, 0), (0, 8, 0, 48, end, 80), (1, 8, 48, 32, end, 0), (1, 9, 0, 96, end, 32)]
    n = len(arrays)
    swapped = [send(a, CORE) for a in arrays]
    table = []
    for core in range(2):
        for which, a, at, rows, chip, offset in pieces:
            table.append((which, a + core * n, at, rows, PLACES.index(chip) + core * 8, offset))
    return arrays + swapped, table, early


def shards(x, dy, order, ln_gain, ln_bias, w_qkv, b_qkv, w_out, w_gate, w_up, w_down):
    x, dy = x[0], dy[0]
    s = lax.axis_index("seq")
    r = lax.axis_index("rows")
    slot = jnp.stack(
        [
            ((s // 4 + up) % 4) * 4 + ((s // 2 % 2) ^ across) * 2 + (s % 2 ^ core)
            for core in range(2)
            for across, up in PLACES
        ]
    ).astype(jnp.int32)
    gain, bias = ln_gain[None, :], ln_bias[None, :]

    def cut(array, at, size, axis):
        return lax.dynamic_slice_in_dim(array, at, size, axis)

    head, unit_at = s * HEAD_DIM, s * FF_LOCAL
    w_qkv_s = jnp.concatenate(
        [cut(w_qkv, head + i * WIDTH, HEAD_DIM, 1) for i in range(3)]
        + [jnp.zeros((WIDTH, HEAD_DIM), bf16)],
        1,
    )
    b_qkv_s = jnp.concatenate(
        [cut(b_qkv, head + i * WIDTH, HEAD_DIM, 0) for i in range(3)] + [jnp.zeros((HEAD_DIM,), f32)]
    )[None, :]
    w_out_s = cut(w_out, head, HEAD_DIM, 0)
    w_gate_s = cut(w_gate, unit_at, FF_LOCAL, 1)
    w_up_s = cut(w_up, unit_at, FF_LOCAL, 1)
    w_down_s = cut(w_down, unit_at, FF_LOCAL, 0)
    early = (slot, w_qkv_s, b_qkv_s, w_gate_s, w_up_s, w_down_s, w_out_s)
    arrays, pieces, early = gather(x, dy, early)
    slot, w_qkv_s, b_qkv_s, w_gate_s, w_up_s, w_down_s, w_out_s = early

    tables = rotary_tables()
    unit, hid, dy_all, packed = project(
        slot, order, arrays, pieces, w_qkv_s, b_qkv_s, w_out_s, gain, bias, tables
    )
    heads = attention(order, packed, tables)
    heads_here = lax.all_to_all(heads, "seq", 0, 0, tiled=True)
    block = weight_grads(
        unit, hid, dy_all, heads, w_qkv_s, w_gate_s, w_up_s, w_down_s, gain, bias
    )
    block, heads_here = lax.optimization_barrier((block, heads_here))
    got = lax.all_to_all(block, "rows", 0, 0, tiled=True)
    x_late, _ = lax.optimization_barrier((x, heads_here))
    part, grad = own_rows(x_late, dy, gain, bias, w_gate, w_up, w_down)
    output, input_grad = final_rows(heads_here, x, dy, part, grad, gain, w_out, w_qkv)
    got, output, input_grad = lax.optimization_barrier((got, output, input_grad))
    outgoing, o_down, o_out = sum_rows(got)
    mine = lax.all_to_all(outgoing, "seq", 0, 0, tiled=True)
    o_qkv, o_gate, o_up, vectors, extra = last_layout(mine)
    totals = extra.reshape(SEQ, 3, HEAD_DIM).transpose(1, 0, 2).reshape(3 * WIDTH)
    o_bqkv = lax.dynamic_slice_in_dim(totals, (s * ROWS + r) * 24, 24, 0)
    return (
        output[None],
        input_grad[None],
        o_qkv,
        o_out,
        o_gate,
        o_up,
        o_down,
        o_bqkv,
        vectors[:, 0],
        vectors[:, 1],
    )


def solution(mesh):
    rows = P("rows", "seq", None)
    both = P(("seq", "rows"), None)
    flat = P(("seq", "rows"))
    return jax.shard_map(
        shards,
        mesh=mesh,
        in_specs=(rows, rows) + (P(),) * 9,
        out_specs=(rows, rows, both, both, both, both, both, flat, flat, flat),
        check_vma=False,
    )
```

profile of v0, /device:TPU:1, one launch (start us, length us, event | category | flops | bytes accessed | tf_op | source)
XLA Modules:
  0.0 153.1 jit_solution(474316335145487668)
XLA Ops:
  0.7 1.1 pad_maximum_fusion.refs_2_
  1.8 1.5 collective-permute-start.9
  3.3 2.8 %collective-permute-start.2 = (bf16[256,1024]{1,0:T(8,128)(2,1)S(1)}, bf16[256,1024]{1,0:T(8,128)(2,1)S(1)}, u32[]{:S(2)}, u32[]{:S(2)}) collective-permute-start(bf16[256,1024]{1,0:T(8,128)(2,1)S(1)} %pad_maximum_fusion.refs_2_), channel_id=1, source_target_pairs={{0,96},{8,104},{16,112},{24,120},{32,0},{40,8},{48,16},{56,24},{64... | collective-permute-start | bytes 1572872 | tf_op jit(solution)/shard_map/ppermute | solution.py:487
  6.2 1.2 collective-permute-start.1
  7.4 0.9 constant_dynamic-slice_fusion.refs_24_
  8.3 1.8 %constant_dynamic-slice_fusion.1.w_d = bf16[176,1024]{1,0:T(8,128)(2,1)} fusion(bf16[2816,1024]{1,0:T(8,128)(2,1)} %wd.1, s32[]{:T(128)S(6)} %select_n.182), kind=kLoop, calls=%fused_computation.5 | loop fusion | bytes 720900 | tf_op jit(solution)/shard_map/dynamic_slice | solution.py:535
  10.0 1.4 constant_dynamic-slice_fusion.6
  11.4 0.8 fusion
  12.3 2.8 %constant_dynamic-slice_fusion.2 = (bf16[1024,176]{1,0:T(8,128)(2,1)}, bf16[1024,176]{1,0:T(8,128)(2,1)}) fusion(bf16[1024,2816]{1,0:T(8,128)(2,1)} %wu.1, s32[]{:T(128)S(6)} %select_n.182, bf16[1024,2816]{1,0:T(8,128)(2,1)} %wg.1), kind=kLoop, calls=%fused_computation.6 | loop fusion | bytes 1441796 | tf_op jit(solution)/shard_map/dynamic_slice | solution.py:535
  15.1 0.3 maximum_maximum_fusion.refs_22_.w_qkv
  15.7 3.7 %collective-permute-done.1.refs_5_ = bf16[256,1024]{1,0:T(8,128)(2,1)S(1)} collective-permute-done((bf16[256,1024]{1,0:T(8,128)(2,1)S(1)}, bf16[256,1024]{1,0:T(8,128)(2,1)S(1)}, u32[]{:S(2)}, u32[]{:S(2)}) %collective-permute-start.1) | collective-permute-done | bytes 524320 | tf_op jit(solution)/shard_map/ppermute | solution.py:487
  19.3 2.1 %collective-permute-done.refs_3_ = bf16[256,1024]{1,0:T(8,128)(2,1)S(1)} collective-permute-done((bf16[256,1024]{1,0:T(8,128)(2,1)S(1)}, bf16[256,1024]{1,0:T(8,128)(2,1)S(1)}, u32[]{:S(2)}, u32[]{:S(2)}) %collective-permute-start) | collective-permute-done | bytes 524320 | tf_op jit(solution)/shard_map/ppermute | solution.py:487
  21.4 1.5 collective-permute-start.11
  23.0 0.3 collective-permute-start.5
  23.3 1.7 %collective-permute-start.3 = (bf16[256,1024]{1,0:T(8,128)(2,1)S(1)}, bf16[256,1024]{1,0:T(8,128)(2,1)S(1)}, u32[]{:S(2)}, u32[]{:S(2)}) collective-permute-start(bf16[256,1024]{1,0:T(8,128)(2,1)S(1)} %collective-permute-done.refs_3_), channel_id=1, source_target_pairs={{0,32},{8,40},{16,48},{24,56},{32,64},{40,72},{48,80},{56,88},{64,... | collective-permute-start | bytes 1572872 | tf_op jit(solution)/shard_map/ppermute | solution.py:487
  24.9 8.4 %collective-permute-done.4.refs_7_ = bf16[256,1024]{1,0:T(8,128)(2,1)S(1)} collective-permute-done((bf16[256,1024]{1,0:T(8,128)(2,1)S(1)}, bf16[256,1024]{1,0:T(8,128)(2,1)S(1)}, u32[]{:S(2)}, u32[]{:S(2)}) %collective-permute-start.4) | collective-permute-done | bytes 524320 | tf_op jit(solution)/shard_map/ppermute | solution.py:487
  33.3 2.4 %collective-permute-start.10 = (bf16[256,1024]{1,0:T(8,128)(2,1)S(1)}, bf16[256,1024]{1,0:T(8,128)(2,1)S(1)}, u32[]{:S(2)}, u32[]{:S(2)}) collective-permute-start(bf16[256,1024]{1,0:T(8,128)(2,1)S(1)} %collective-permute-done.refs_3_), channel_id=1, source_target_pairs={{0,8},{8,0},{16,24},{24,16},{32,40},{40,32},{48,56},{56,48},{64,72... | collective-permute-start | bytes 1572872 | tf_op jit(solution)/shard_map/ppermute | solution.py:487
  35.8 1.3 collective-permute-start.7
  37.1 0.3 collective-permute-start.14
  37.6 1.2 collective-permute-start.13
  38.8 0.5 collective-permute-start.6
  39.4 2.3 %collective-permute-done.7.refs_10_ = bf16[80,1024]{1,0:T(8,128)(2,1)S(1)} collective-permute-done((bf16[80,1024]{1,0:T(8,128)(2,1)S(1)}, bf16[80,1024]{1,0:T(8,128)(2,1)S(1)}, u32[]{:S(2)}, u32[]{:S(2)}) %collective-permute-start.7) | collective-permute-done | bytes 163872 | tf_op jit(solution)/shard_map/ppermute | solution.py:487
  41.9 4.0 %collective-permute-done.6.refs_9_ = bf16[80,1024]{1,0:T(8,128)(2,1)S(1)} collective-permute-done((bf16[80,1024]{1,0:T(8,128)(2,1)S(1)}, bf16[80,1024]{1,0:T(8,128)(2,1)S(1)}, u32[]{:S(2)}, u32[]{:S(2)}) %collective-permute-start.6) | collective-permute-done | bytes 163872 | tf_op jit(solution)/shard_map/ppermute | solution.py:487
  46.0 0.8 collective-permute-start.17
  46.7 0.6 collective-permute-done.8.refs_11_
  47.3 1.7 %collective-permute-start.18 = (bf16[96,1024]{1,0:T(8,128)(2,1)S(1)}, bf16[96,1024]{1,0:T(8,128)(2,1)S(1)}, u32[]{:S(2)}, u32[]{:S(2)}) collective-permute-start(bf16[96,1024]{1,0:T(8,128)(2,1)S(1)} %collective-permute-done.8.refs_11_), channel_id=1, source_target_pairs={{0,8},{8,0},{16,24},{24,16},{32,40},{40,32},{48,56},{56,48},{64,72... | collective-permute-start | bytes 589832 | tf_op jit(solution)/shard_map/ppermute | solution.py:487
  49.0 1.4 collective-permute-done.16.refs_19_
  50.5 10.8 %project.1 = (bf16[2048,1024]{1,0:T(8,128)(2,1)S(1)}, bf16[2048,1024]{1,0:T(8,128)(2,1)S(1)}, bf16[2048,1024]{1,0:T(8,128)(2,1)S(1)}, bf16[2048,256]{1,0:T(8,128)(2,1)S(1)}) custom-call(s32[16]{0:T(128)S(1)} %stack.67.refs_0_, s32[32]{0:T(128)S(1)} %copy-done.17, bf16[256,1024]{1,0:T(8,128)(2,1)S(1)} %pad_maximum_fusion.refs_2_, ...), custom_call_target="tpu_custom_call" | custom-call | flops 2000000000 | bytes 20971520 | tf_op jit(solution)/shard_map/project/pallas_call | solution.py:177
  61.3 2.0 %copy-done.18 = bf16[2048,1024]{1,0:T(8,128)(2,1)} copy-done((bf16[2048,1024]{1,0:T(8,128)(2,1)}, bf16[2048,1024]{1,0:T(8,128)(2,1)S(1)}, u32[]{:S(2)}) %copy-start.18) | copy-done | bytes 4194328
  63.3 15.1 %attention.1.heads = bf16[2048,256]{1,0:T(8,128)(2,1)} custom-call(s32[32]{0:T(128)S(1)} %copy-done.17, bf16[2048,256]{1,0:T(8,128)(2,1)S(1)} %get-tuple-element.50.packed, f32[32,128]{1,0:T(8,128)S(1)} %copy-done.15, f32[32,128]{1,0:T(8,128)S(1)} %copy-done.14, f32[64,128]{1,0:T(8,128)S(1)} %copy-done.13, f32[64,128]{1,0:T(8,128)S(1)} %copy-done.12), custom_call_target="tpu_custom_call" | custom-call | flops 15000000512 | bytes 8388608 | tf_op jit(solution)/shard_map/attention/pallas_call | solution.py:252
  78.4 4.3 %all-to-all-start = ((bf16[16,128,256]{2,1,0:T(8,128)(2,1)}), bf16[16,128,256]{2,1,0:T(8,128)(2,1)S(1)}, u32[]{:S(2)}, u32[]{:S(2)}) async-start(bf16[16,128,256]{2,1,0:T(8,128)(2,1)} %bitcast.21), calls=%async_computation | async-start | bytes 2097152 | tf_op jit(solution)/shard_map/all_to_all | solution.py:559
  82.7 2.2 %copy-done.19 = bf16[2048,1024]{1,0:T(8,128)(2,1)S(1)} copy-done((bf16[2048,1024]{1,0:T(8,128)(2,1)S(1)}, bf16[2048,1024]{1,0:T(8,128)(2,1)}, u32[]{:S(2)}) %copy-start.19) | copy-done | bytes 4194328
  84.9 2.2 %copy-done.21 = bf16[2048,1024]{1,0:T(8,128)(2,1)S(1)} copy-done((bf16[2048,1024]{1,0:T(8,128)(2,1)S(1)}, bf16[2048,1024]{1,0:T(8,128)(2,1)}, u32[]{:S(2)}) %copy-start.21) | copy-done | bytes 4194328
  87.0 14.5 %weight_grads.1 = bf16[8,192,640]{2,1,0:T(8,128)(2,1)S(1)} custom-call(bf16[2048,1024]{1,0:T(8,128)(2,1)S(1)} %copy-done.19, bf16[2048,1024]{1,0:T(8,128)(2,1)S(1)} %copy-done.21, bf16[2048,1024]{1,0:T(8,128)(2,1)} %copy-done.22, bf16[2048,256]{1,0:T(8,128)(2,1)} %attention.1.heads, bf16[1024,256]{1,0:T(8,128)(2,1)S(1)} %maximum_maximum_fusion.refs_22_.w_qkv, ...), custom_call_target="tpu_custom_call" | custom-call | flops 8000000000 | bytes 20971520 | tf_op jit(solution)/shard_map/weight_grads/pallas_call | solution.py:351
  101.6 1.3 copy-done.4
  102.9 7.5 %all-to-all-start.1 = ((bf16[8,192,640]{2,1,0:T(8,128)(2,1)}), bf16[8,192,640]{2,1,0:T(8,128)(2,1)S(1)}, u32[]{:S(2)}, u32[]{:S(2)}) async-start(bf16[8,192,640]{2,1,0:T(8,128)(2,1)} %copy-done.4), calls=%async_computation.1 | async-start | bytes 3932160 | tf_op jit(solution)/shard_map/all_to_all | solution.py:564
  110.4 16.3 %own_rows.1 = (f32[128,1024]{1,0:T(8,128)}, f32[128,1024]{1,0:T(8,128)}) custom-call(bf16[128,1024]{1,0:T(8,128)(2,1)} %bitcast.33, bf16[128,1024]{1,0:T(8,128)(2,1)} %bitcast.30, f32[1,1024]{1,0:T(1,128)} %bitcast.36, f32[1,1024]{1,0:T(1,128)} %bitcast.40, bf16[1024,2816]{1,0:T(8,128)(2,1)} %wg.1, bf16[1024,2816]{1,0:T(8,128)(2,1)} %wu.1, bf16[2816,1024]{1,0:T(8,128)(2,1)} %wd.1), custom_call_target="tpu_custom_call" | custom-call | flops 4499999744 | bytes 18874368 | tf_op jit(solution)/shard_map/own_rows/pallas_call | solution.py:96
  126.7 2.8 %copy-done = bf16[1024,3072]{1,0:T(8,128)(2,1)S(1)} copy-done((bf16[1024,3072]{1,0:T(8,128)(2,1)S(1)}, bf16[1024,3072]{1,0:T(8,128)(2,1)}, u32[]{:S(2)}) %copy-start) | copy-done | bytes 6291480
  129.5 1.6 %copy-done.1 = bf16[1024,1024]{1,0:T(8,128)(2,1)S(1)} copy-done((bf16[1024,1024]{1,0:T(8,128)(2,1)S(1)}, bf16[1024,1024]{1,0:T(8,128)(2,1)}, u32[]{:S(2)}) %copy-start.1) | copy-done | bytes 2097176
  131.1 1.0 copy-done.7
  132.1 1.0 copy-done.8
  133.2 4.9 %final_rows.1 = (bf16[128,1024]{1,0:T(8,128)(2,1)}, bf16[128,1024]{1,0:T(8,128)(2,1)}) custom-call(bf16[2048,256]{1,0:T(8,128)(2,1)S(1)} %bitcast.28, bf16[128,1024]{1,0:T(8,128)(2,1)S(1)} %bitcast.34, bf16[128,1024]{1,0:T(8,128)(2,1)S(1)} %bitcast.31, f32[128,1024]{1,0:T(8,128)S(1)} %copy-done.7, f32[128,1024]{1,0:T(8,128)S(1)} %copy-done.8, ...), custom_call_target="tpu_custom_call" | custom-call | flops 1100000000 | bytes 10485760 | tf_op jit(solution)/shard_map/final_rows/pallas_call | solution.py:397
  138.1 0.9 sum_rows.1
  139.0 5.4 %all-to-all-start.2 = ((bf16[16,8,640]{2,1,0:T(8,128)(2,1)}), bf16[16,8,640]{2,1,0:T(8,128)(2,1)S(1)}, u32[]{:S(2)}, u32[]{:S(2)}) async-start(bf16[16,8,640]{2,1,0:T(8,128)(2,1)} %bitcast.25), calls=%async_computation.2 | async-start | bytes 327680 | tf_op jit(solution)/shard_map/all_to_all | solution.py:570
  144.4 6.4 %all-to-all-done.2 = bf16[16,8,640]{2,1,0:T(8,128)(2,1)S(1)} async-done(((bf16[16,8,640]{2,1,0:T(8,128)(2,1)}), bf16[16,8,640]{2,1,0:T(8,128)(2,1)S(1)}, u32[]{:S(2)}, u32[]{:S(2)}) %all-to-all-start.2) | async-done | bytes 163872 | tf_op jit(solution)/shard_map/all_to_all | solution.py:570
  150.9 0.8 last_layout.1
  151.7 0.7 slice_reduce_fusion
  152.5 0.6 dynamic_slice.43
  (69 shorter events, 1.2 us)
Async XLA Ops:
  0.6 49.8 %copy-start.12 = (f32[64,128]{1,0:T(8,128)S(1)}, f32[64,128]{1,0:T(8,128)}, u32[]{:S(2)}) copy-start(f32[64,128]{1,0:T(8,128)} %constant.249.clone.refs_30_.sin_i) | copy-start | bytes 98308
  0.7 49.8 %copy-start.13 = (f32[64,128]{1,0:T(8,128)S(1)}, f32[64,128]{1,0:T(8,128)}, u32[]{:S(2)}) copy-start(f32[64,128]{1,0:T(8,128)} %constant.248.clone.refs_29_.cos_i) | copy-start | bytes 98308
  0.7 49.8 %copy-start.14 = (f32[32,128]{1,0:T(8,128)S(1)}, f32[32,128]{1,0:T(8,128)}, u32[]{:S(2)}) copy-start(f32[32,128]{1,0:T(8,128)} %constant.247.clone.refs_28_.sin_g) | copy-start | bytes 49156
  0.7 49.8 %copy-start.15 = (f32[32,128]{1,0:T(8,128)S(1)}, f32[32,128]{1,0:T(8,128)}, u32[]{:S(2)}) copy-start(f32[32,128]{1,0:T(8,128)} %constant.246.clone.refs_27_.cos_g) | copy-start | bytes 49156
  0.7 49.8 %copy-start.17 = (s32[32]{0:T(128)S(1)}, s32[32]{0:T(128)}, u32[]{:S(2)}) copy-start(s32[32]{0:T(128)} %order.1) | copy-start | bytes 388
  0.7 49.8 %copy-start.16 = (f32[1024]{0:T(1024)S(1)}, f32[1024]{0:T(1024)}, u32[]{:S(2)}) copy-start(f32[1024]{0:T(1024)} %param.19) | copy-start | bytes 12292
  0.7 49.8 %copy-start.10 = (f32[1024]{0:T(1024)S(1)}, f32[1024]{0:T(1024)}, u32[]{:S(2)}) copy-start(f32[1024]{0:T(1024)} %param.18) | copy-start | bytes 12292
  1.8 21.4 %collective-permute-start.9 = (bf16[256,1024]{1,0:T(8,128)(2,1)S(1)}, bf16[256,1024]{1,0:T(8,128)(2,1)S(1)}, u32[]{:S(2)}, u32[]{:S(2)}) collective-permute-start(bf16[256,1024]{1,0:T(8,128)(2,1)S(1)} %pad_maximum_fusion.refs_2_), channel_id=1, source_target_pairs={{0,8},{8,0},{16,24},{24,16},{32,40},{40,32},{48,56},{56,48},{64,72... | collective-permute-start | bytes 1572872 | tf_op jit(solution)/shard_map/ppermute | solution.py:487
  3.3 18.1 %collective-permute-start.2 = (bf16[256,1024]{1,0:T(8,128)(2,1)S(1)}, bf16[256,1024]{1,0:T(8,128)(2,1)S(1)}, u32[]{:S(2)}, u32[]{:S(2)}) collective-permute-start(bf16[256,1024]{1,0:T(8,128)(2,1)S(1)} %pad_maximum_fusion.refs_2_), channel_id=1, source_target_pairs={{0,96},{8,104},{16,112},{24,120},{32,0},{40,8},{48,16},{56,24},{64... | collective-permute-start | bytes 1572872 | tf_op jit(solution)/shard_map/ppermute | solution.py:487
  6.2 13.2 %collective-permute-start.1 = (bf16[256,1024]{1,0:T(8,128)(2,1)S(1)}, bf16[256,1024]{1,0:T(8,128)(2,1)S(1)}, u32[]{:S(2)}, u32[]{:S(2)}) collective-permute-start(bf16[256,1024]{1,0:T(8,128)(2,1)S(1)} %pad_maximum_fusion.refs_2_), channel_id=1, source_target_pairs={{0,16},{8,24},{16,0},{24,8},{32,48},{40,56},{48,32},{56,40},{64,80... | collective-permute-start | bytes 1572872 | tf_op jit(solution)/shard_map/ppermute | solution.py:487
  7.4 14.1 %collective-permute-start = (bf16[256,1024]{1,0:T(8,128)(2,1)S(1)}, bf16[256,1024]{1,0:T(8,128)(2,1)S(1)}, u32[]{:S(2)}, u32[]{:S(2)}) collective-permute-start(bf16[256,1024]{1,0:T(8,128)(2,1)S(1)} %pad_maximum_fusion.refs_2_), channel_id=1, source_target_pairs={{0,32},{8,40},{16,48},{24,56},{32,64},{40,72},{48,80},{56,88},{64,... | collective-permute-start | bytes 1572872 | tf_op jit(solution)/shard_map/ppermute | solution.py:487
  21.4 11.9 %collective-permute-start.4 = (bf16[256,1024]{1,0:T(8,128)(2,1)S(1)}, bf16[256,1024]{1,0:T(8,128)(2,1)S(1)}, u32[]{:S(2)}, u32[]{:S(2)}) collective-permute-start(bf16[256,1024]{1,0:T(8,128)(2,1)S(1)} %collective-permute-done.1.refs_5_), channel_id=1, source_target_pairs={{0,96},{8,104},{16,112},{24,120},{32,0},{40,8},{48,16},{56,24},{64... | collective-permute-start | bytes 1572872 | tf_op jit(solution)/shard_map/ppermute | solution.py:487
  21.4 14.4 %collective-permute-start.11 = (bf16[256,1024]{1,0:T(8,128)(2,1)S(1)}, bf16[256,1024]{1,0:T(8,128)(2,1)S(1)}, u32[]{:S(2)}, u32[]{:S(2)}) collective-permute-start(bf16[256,1024]{1,0:T(8,128)(2,1)S(1)} %collective-permute-done.2.refs_4_), channel_id=1, source_target_pairs={{0,8},{8,0},{16,24},{24,16},{32,40},{40,32},{48,56},{56,48},{64,72... | collective-permute-start | bytes 1572872 | tf_op jit(solution)/shard_map/ppermute | solution.py:487
  22.9 14.1 %collective-permute-start.12 = (bf16[256,1024]{1,0:T(8,128)(2,1)S(1)}, bf16[256,1024]{1,0:T(8,128)(2,1)S(1)}, u32[]{:S(2)}, u32[]{:S(2)}) collective-permute-start(bf16[256,1024]{1,0:T(8,128)(2,1)S(1)} %collective-permute-done.1.refs_5_), channel_id=1, source_target_pairs={{0,8},{8,0},{16,24},{24,16},{32,40},{40,32},{48,56},{56,48},{64,72... | collective-permute-start | bytes 1572872 | tf_op jit(solution)/shard_map/ppermute | solution.py:487
  23.0 14.3 %collective-permute-start.5 = (bf16[256,1024]{1,0:T(8,128)(2,1)S(1)}, bf16[256,1024]{1,0:T(8,128)(2,1)S(1)}, u32[]{:S(2)}, u32[]{:S(2)}) collective-permute-start(bf16[256,1024]{1,0:T(8,128)(2,1)S(1)} %collective-permute-done.refs_3_), channel_id=1, source_target_pairs={{0,16},{8,24},{16,0},{24,8},{32,48},{40,56},{48,32},{56,40},{64,80... | collective-permute-start | bytes 1572872 | tf_op jit(solution)/shard_map/ppermute | solution.py:487
  23.3 14.3 %collective-permute-start.3 = (bf16[256,1024]{1,0:T(8,128)(2,1)S(1)}, bf16[256,1024]{1,0:T(8,128)(2,1)S(1)}, u32[]{:S(2)}, u32[]{:S(2)}) collective-permute-start(bf16[256,1024]{1,0:T(8,128)(2,1)S(1)} %collective-permute-done.refs_3_), channel_id=1, source_target_pairs={{0,32},{8,40},{16,48},{24,56},{32,64},{40,72},{48,80},{56,88},{64,... | collective-permute-start | bytes 1572872 | tf_op jit(solution)/shard_map/ppermute | solution.py:487
  33.3 5.5 %collective-permute-start.10 = (bf16[256,1024]{1,0:T(8,128)(2,1)S(1)}, bf16[256,1024]{1,0:T(8,128)(2,1)S(1)}, u32[]{:S(2)}, u32[]{:S(2)}) collective-permute-start(bf16[256,1024]{1,0:T(8,128)(2,1)S(1)} %collective-permute-done.refs_3_), channel_id=1, source_target_pairs={{0,8},{8,0},{16,24},{24,16},{32,40},{40,32},{48,56},{56,48},{64,72... | collective-permute-start | bytes 1572872 | tf_op jit(solution)/shard_map/ppermute | solution.py:487
  35.8 5.9 %collective-permute-start.7 = (bf16[80,1024]{1,0:T(8,128)(2,1)S(1)}, bf16[80,1024]{1,0:T(8,128)(2,1)S(1)}, u32[]{:S(2)}, u32[]{:S(2)}) collective-permute-start(bf16[80,1024]{1,0:T(8,128)(2,1)S(1)} %slice.21), channel_id=1, source_target_pairs={{0,96},{8,104},{16,112},{24,120},{32,0},{40,8},{48,16},{56,24},{64... | collective-permute-start | bytes 491528 | tf_op jit(solution)/shard_map/ppermute | solution.py:487
  37.1 13.3 %collective-permute-start.14 = (bf16[256,1024]{1,0:T(8,128)(2,1)S(1)}, bf16[256,1024]{1,0:T(8,128)(2,1)S(1)}, u32[]{:S(2)}, u32[]{:S(2)}) collective-permute-start(bf16[256,1024]{1,0:T(8,128)(2,1)S(1)} %collective-permute-done.4.refs_7_), channel_id=1, source_target_pairs={{0,8},{8,0},{16,24},{24,16},{32,40},{40,32},{48,56},{56,48},{64,72... | collective-permute-start | bytes 1572872 | tf_op jit(solution)/shard_map/ppermute | solution.py:487
  37.4 13.1 %collective-permute-start.15 = (bf16[256,1024]{1,0:T(8,128)(2,1)S(1)}, bf16[256,1024]{1,0:T(8,128)(2,1)S(1)}, u32[]{:S(2)}, u32[]{:S(2)}) collective-permute-start(bf16[256,1024]{1,0:T(8,128)(2,1)S(1)} %collective-permute-done.5.refs_8_), channel_id=1, source_target_pairs={{0,8},{8,0},{16,24},{24,16},{32,40},{40,32},{48,56},{56,48},{64,72... | collective-permute-start | bytes 1572872 | tf_op jit(solution)/shard_map/ppermute | solution.py:487
  37.6 12.8 %collective-permute-start.13 = (bf16[256,1024]{1,0:T(8,128)(2,1)S(1)}, bf16[256,1024]{1,0:T(8,128)(2,1)S(1)}, u32[]{:S(2)}, u32[]{:S(2)}) collective-permute-start(bf16[256,1024]{1,0:T(8,128)(2,1)S(1)} %collective-permute-done.3.refs_6_), channel_id=1, source_target_pairs={{0,8},{8,0},{16,24},{24,16},{32,40},{40,32},{48,56},{56,48},{64,72... | collective-permute-start | bytes 1572872 | tf_op jit(solution)/shard_map/ppermute | solution.py:487
  38.8 7.1 %collective-permute-start.6 = (bf16[80,1024]{1,0:T(8,128)(2,1)S(1)}, bf16[80,1024]{1,0:T(8,128)(2,1)S(1)}, u32[]{:S(2)}, u32[]{:S(2)}) collective-permute-start(bf16[80,1024]{1,0:T(8,128)(2,1)S(1)} %slice.20), channel_id=1, source_target_pairs={{0,32},{8,40},{16,48},{24,56},{32,64},{40,72},{48,80},{56,88},{64,... | collective-permute-start | bytes 491528 | tf_op jit(solution)/shard_map/ppermute | solution.py:487
  41.7 5.6 %collective-permute-start.8 = (bf16[96,1024]{1,0:T(8,128)(2,1)S(1)}, bf16[96,1024]{1,0:T(8,128)(2,1)S(1)}, u32[]{:S(2)}, u32[]{:S(2)}) collective-permute-start(bf16[96,1024]{1,0:T(8,128)(2,1)S(1)} %slice.22), channel_id=1, source_target_pairs={{0,16},{8,24},{16,0},{24,8},{32,48},{40,56},{48,32},{56,40},{64,80... | collective-permute-start | bytes 589832 | tf_op jit(solution)/shard_map/ppermute | solution.py:487
  46.0 3.0 %collective-permute-start.17 = (bf16[80,1024]{1,0:T(8,128)(2,1)S(1)}, bf16[80,1024]{1,0:T(8,128)(2,1)S(1)}, u32[]{:S(2)}, u32[]{:S(2)}) collective-permute-start(bf16[80,1024]{1,0:T(8,128)(2,1)S(1)} %collective-permute-done.7.refs_10_), channel_id=1, source_target_pairs={{0,8},{8,0},{16,24},{24,16},{32,40},{40,32},{48,56},{56,48},{64,72... | collective-permute-start | bytes 491528 | tf_op jit(solution)/shard_map/ppermute | solution.py:487
  47.3 3.1 %collective-permute-start.18 = (bf16[96,1024]{1,0:T(8,128)(2,1)S(1)}, bf16[96,1024]{1,0:T(8,128)(2,1)S(1)}, u32[]{:S(2)}, u32[]{:S(2)}) collective-permute-start(bf16[96,1024]{1,0:T(8,128)(2,1)S(1)} %collective-permute-done.8.refs_11_), channel_id=1, source_target_pairs={{0,8},{8,0},{16,24},{24,16},{32,40},{40,32},{48,56},{56,48},{64,72... | collective-permute-start | bytes 589832 | tf_op jit(solution)/shard_map/ppermute | solution.py:487
  49.0 1.4 collective-permute-start.16
  61.3 2.0 %copy-start.18 = (bf16[2048,1024]{1,0:T(8,128)(2,1)}, bf16[2048,1024]{1,0:T(8,128)(2,1)S(1)}, u32[]{:S(2)}) copy-start(bf16[2048,1024]{1,0:T(8,128)(2,1)S(1)} %get-tuple-element.47.unit_in) | copy-start | bytes 12582916
  63.3 15.1 %copy-start.20 = (bf16[2048,1024]{1,0:T(8,128)(2,1)}, bf16[2048,1024]{1,0:T(8,128)(2,1)S(1)}, u32[]{:S(2)}) copy-start(bf16[2048,1024]{1,0:T(8,128)(2,1)S(1)} %get-tuple-element.48.hid_in) | copy-start | bytes 12582916
  63.3 15.1 %copy-start.22 = (bf16[2048,1024]{1,0:T(8,128)(2,1)}, bf16[2048,1024]{1,0:T(8,128)(2,1)S(1)}, u32[]{:S(2)}) copy-start(bf16[2048,1024]{1,0:T(8,128)(2,1)S(1)} %get-tuple-element.49.dy_in) | copy-start | bytes 12582916
  63.3 19.4 %copy-start.5 = (bf16[1024,176]{1,0:T(8,128)(2,1)S(1)}, bf16[1024,176]{1,0:T(8,128)(2,1)}, u32[]{:S(2)}) copy-start(bf16[1024,176]{1,0:T(8,128)(2,1)} %get-tuple-element.52.w_u) | copy-start | bytes 1081348
  63.3 19.4 %copy-start.6 = (bf16[1024,176]{1,0:T(8,128)(2,1)S(1)}, bf16[1024,176]{1,0:T(8,128)(2,1)}, u32[]{:S(2)}) copy-start(bf16[1024,176]{1,0:T(8,128)(2,1)} %get-tuple-element.51.w_g) | copy-start | bytes 1081348
  63.3 19.4 %copy-start.9 = (bf16[176,1024]{1,0:T(8,128)(2,1)S(1)}, bf16[176,1024]{1,0:T(8,128)(2,1)}, u32[]{:S(2)}) copy-start(bf16[176,1024]{1,0:T(8,128)(2,1)} %constant_dynamic-slice_fusion.1.w_d) | copy-start | bytes 1081348
  78.4 24.5 %all-to-all-start = ((bf16[16,128,256]{2,1,0:T(8,128)(2,1)}), bf16[16,128,256]{2,1,0:T(8,128)(2,1)S(1)}, u32[]{:S(2)}, u32[]{:S(2)}) async-start(bf16[16,128,256]{2,1,0:T(8,128)(2,1)} %bitcast.21), calls=%async_computation | async-start | bytes 2097152 | tf_op jit(solution)/shard_map/all_to_all | solution.py:559
  82.7 2.2 %copy-start.19 = (bf16[2048,1024]{1,0:T(8,128)(2,1)S(1)}, bf16[2048,1024]{1,0:T(8,128)(2,1)}, u32[]{:S(2)}) copy-start(bf16[2048,1024]{1,0:T(8,128)(2,1)} %copy-done.18) | copy-start | bytes 12582916
  84.9 2.2 %copy-start.21 = (bf16[2048,1024]{1,0:T(8,128)(2,1)S(1)}, bf16[2048,1024]{1,0:T(8,128)(2,1)}, u32[]{:S(2)}) copy-start(bf16[2048,1024]{1,0:T(8,128)(2,1)} %copy-done.20) | copy-start | bytes 12582916
  101.5 1.3 copy-start.4
  102.9 35.3 %all-to-all-start.1 = ((bf16[8,192,640]{2,1,0:T(8,128)(2,1)}), bf16[8,192,640]{2,1,0:T(8,128)(2,1)S(1)}, u32[]{:S(2)}, u32[]{:S(2)}) async-start(bf16[8,192,640]{2,1,0:T(8,128)(2,1)} %copy-done.4), calls=%async_computation.1 | async-start | bytes 3932160 | tf_op jit(solution)/shard_map/all_to_all | solution.py:564
  110.4 16.4 %copy-start.2 = (bf16[1,128,1024]{2,1,0:T(8,128)(2,1)S(1)}, bf16[1,128,1024]{2,1,0:T(8,128)(2,1)}, u32[]{:S(2)}) copy-start(bf16[1,128,1024]{2,1,0:T(8,128)(2,1)} %param.16) | copy-start | bytes 786436
  110.4 16.4 %copy-start.3 = (bf16[1,128,1024]{2,1,0:T(8,128)(2,1)S(1)}, bf16[1,128,1024]{2,1,0:T(8,128)(2,1)}, u32[]{:S(2)}) copy-start(bf16[1,128,1024]{2,1,0:T(8,128)(2,1)} %param.15) | copy-start | bytes 786436
  110.4 16.3 %copy-start.11 = (f32[1024]{0:T(1024)S(1)}, f32[1024]{0:T(1024)}, u32[]{:S(2)}) copy-start(f32[1024]{0:T(1024)} %param.18) | copy-start | bytes 12292
  126.7 2.8 %copy-start = (bf16[1024,3072]{1,0:T(8,128)(2,1)S(1)}, bf16[1024,3072]{1,0:T(8,128)(2,1)}, u32[]{:S(2)}) copy-start(bf16[1024,3072]{1,0:T(8,128)(2,1)} %w_qkv.1) | copy-start | bytes 18874372
  129.5 1.6 %copy-start.1 = (bf16[1024,1024]{1,0:T(8,128)(2,1)S(1)}, bf16[1024,1024]{1,0:T(8,128)(2,1)}, u32[]{:S(2)}) copy-start(bf16[1024,1024]{1,0:T(8,128)(2,1)} %w_out.1) | copy-start | bytes 6291460
  131.1 1.0 copy-start.7
  132.1 1.0 copy-start.8
  139.0 11.8 %all-to-all-start.2 = ((bf16[16,8,640]{2,1,0:T(8,128)(2,1)}), bf16[16,8,640]{2,1,0:T(8,128)(2,1)S(1)}, u32[]{:S(2)}, u32[]{:S(2)}) async-start(bf16[16,8,640]{2,1,0:T(8,128)(2,1)} %bitcast.25), calls=%async_computation.2 | async-start | bytes 327680 | tf_op jit(solution)/shard_map/all_to_all | solution.py:570
where the time goes:
time: 154 us; the launch traced here: 153 us
  Pallas kernels  63.3 us (41%)
  starting transfers between devices  34.9 us (23%)
  waiting for transfers between devices  28.9 us (19%)
  local copies, waits for them, and re-layouts  23.5 us (15%)
    ppermute x19, waiting for transfers between devices, send(): return lax.ppermute(value, 'seq', to)  22.5 us
    ppermute x19, starting transfers between devices, send(): return lax.ppermute(value, 'seq', to)  17.7 us
    pallas_call x1, Pallas kernels, own_rows(): pl.pallas_call(own_kernel, grid=(FF // BLOCK,), out_shape=[jax.ShapeDtype...  16.3 us
    pallas_call x1, Pallas kernels, attention(): pl.pallas_call(attention_kernel, out_shape=jax.ShapeDtypeStruct((LENGTH,...  15.1 us
    pallas_call x1, Pallas kernels, weight_grads(): pl.pallas_call(weights_kernel, out_shape=jax.ShapeDtypeStruct((ROWS, 192,...  14.5 us
    unnamed x46, local copies, waits for them, and re-layouts  14.2 us
    pallas_call x1, Pallas kernels, project(): pl.pallas_call(lambda *refs: project_kernel(pieces, len(arrays), *refs),...  10.8 us
    dynamic_slice x5, local copies, waits for them, and re-layouts, cut(): return lax.dynamic_slice_in_dim(array, at, size, axis)  7.66 us
  transfers between devices with their start and end apart: 22, of which 8 were waited for; matrix products, arithmetic and copies ran while one was open for 5% of the time, Pallas kernels for 23%

commit v1 on v0

v1 whole, which is shorter than its diff:
```python
import jax
import jax.numpy as jnp
import numpy as np
from jax import lax
from jax.experimental import pallas as pl
from jax.experimental.pallas import tpu as pltpu
from jax.sharding import PartitionSpec as P

HEADS = 16
HEAD_DIM = 64
ROT = 16
GROUP = 64
LENGTH = 2048
WIDTH = 1024
FF = 2816
FF_LOCAL = 176
BLOCK = 256
SEQ = 16
ROWS = 8
HERE = 128
epsilon = 1e-05
f32 = jnp.float32
bf16 = jnp.bfloat16
SMEM = pl.BlockSpec(memory_space=pltpu.SMEM)
VMEM = pl.BlockSpec(memory_space=pltpu.VMEM)
ANY = pl.BlockSpec(memory_space=pl.ANY)


def dot_nn(a, b):
    return lax.dot_general(a, b, (((1,), (0,)), ((), ())), preferred_element_type=f32)


def dot_nt(a, b):
    return lax.dot_general(a, b, (((1,), (1,)), ((), ())), preferred_element_type=f32)


def dot_tn(a, b):
    return lax.dot_general(a, b, (((0,), (0,)), ((), ())), preferred_element_type=f32)


def params(mib):
    return pltpu.CompilerParams(vmem_limit_bytes=mib * 1024 * 1024)


def cost(gflop, mib, exps=0):
    return pl.CostEstimate(
        flops=int(gflop * 1e9), bytes_accessed=int(mib * 2**20), transcendentals=int(exps)
    )


def normalise(rows):
    rows = rows.astype(f32)
    mean = jnp.mean(rows, 1, keepdims=True)
    centred = rows - mean
    inv_std = lax.rsqrt(jnp.mean(centred * centred, 1, keepdims=True) + epsilon)
    return centred * inv_std, inv_std


def gated(gate, up, grad_act):
    sig = 1.0 / (1.0 + jnp.exp(-gate))
    silu = gate * sig
    grad_g = grad_act * up * (sig * (1.0 + gate - silu))
    grad_u = grad_act * silu
    return (silu * up).astype(bf16), grad_g.astype(bf16), grad_u.astype(bf16)


def rotary_tables():
    half = ROT // 2
    lane = np.arange(2 * HEAD_DIM) % HEAD_DIM
    frequency = np.where(lane < ROT, 10000.0 ** (-(lane % half) * (2.0 / ROT)), 0.0)
    groups = np.arange(LENGTH // GROUP)[:, None] * GROUP * frequency
    inside = np.arange(GROUP)[:, None] * frequency
    parts = (np.cos(groups), np.sin(groups), np.cos(inside), np.sin(inside))
    return jnp.asarray(np.concatenate(parts), f32)


def group_rotation(table, group):
    count = LENGTH // GROUP
    cos_g, sin_g = table[pl.ds(group, 1), :], table[pl.ds(group + count, 1), :]
    cos_i = table[2 * count : 2 * count + GROUP, :]
    sin_i = table[2 * count + GROUP :, :]
    return cos_g * cos_i - sin_g * sin_i, sin_g * cos_i + cos_g * sin_i


def own_kernel(x, dy, gain, bias, wg, wu, wd, out, grad, hid):
    @pl.when(pl.program_id(0) == 0)
    def _():
        unit, _ = normalise(x[...])
        hid[...] = (unit * gain[...] + bias[...]).astype(bf16)
        out[...] = x[...].astype(f32)
        grad[...] = jnp.zeros_like(grad)

    gate = dot_nn(hid[...], wg[...])
    up = dot_nn(hid[...], wu[...])
    act, grad_g, grad_u = gated(gate, up, dot_nt(dy[...], wd[...]))
    out[...] += dot_nn(act, wd[...])
    grad[...] += dot_nt(grad_g, wg[...]) + dot_nt(grad_u, wu[...])


def own_rows(x, dy, gain, bias, w_gate, w_up, w_down):
    whole = pl.BlockSpec((HERE, WIDTH), lambda j: (0, 0))
    vector = pl.BlockSpec((1, WIDTH), lambda j: (0, 0))
    columns = pl.BlockSpec((WIDTH, BLOCK), lambda j: (0, j))
    return pl.pallas_call(
        own_kernel,
        grid=(FF // BLOCK,),
        out_shape=[jax.ShapeDtypeStruct((HERE, WIDTH), f32)] * 2,
        in_specs=[whole, whole, vector, vector, columns, columns]
        + [pl.BlockSpec((BLOCK, WIDTH), lambda j: (j, 0))],
        out_specs=[whole, whole],
        scratch_shapes=[pltpu.VMEM((HERE, WIDTH), bf16)],
        compiler_params=params(60),
        cost_estimate=cost(0.001, 0.001),
        name="own_rows",
    )(x, dy, gain, bias, w_gate, w_up, w_down)


def heads_kernel(
    slot, order, x, dy, w_q, w_k, w_v, w_o, b_q, b_k, b_v, gain, bias,
    table, out, hid, cosine, sine,
):
    lanes = 2 * HEAD_DIM
    lane = lax.broadcasted_iota(jnp.int32, (1, lanes), 1)
    low = lane % HEAD_DIM < ROT // 2
    scale = jnp.where(lane < HEAD_DIM, HEAD_DIM**-0.5, 1.0)

    @pl.when(pl.program_id(0) == 0)
    def _():
        unit, _ = normalise(x[...])
        hid[...] = (unit * gain[...] + bias[...]).astype(bf16)
        for g in range(HERE // GROUP):
            rows = slice(g * GROUP, (g + 1) * GROUP)
            group = order[slot[0] * (HERE // GROUP) + g]
            cosine[rows, :], sine[rows, :] = group_rotation(table, group)

    q = dot_nn(hid[...], w_q[...]) + b_q[...]
    k = dot_nn(hid[...], w_k[...]) + b_k[...]
    v = dot_nn(hid[...], w_v[...]) + b_v[...]
    grad_att = dot_nt(dy[...], w_o[...])
    for h in range(BLOCK // HEAD_DIM):
        part = slice(h * HEAD_DIM, (h + 1) * HEAD_DIM)
        raw = jnp.concatenate([q[:, part], k[:, part]], 1)
        before, after = pltpu.roll(raw, ROT // 2, 1), pltpu.roll(raw, lanes - ROT // 2, 1)
        turned = (raw * cosine[...] + jnp.where(low, -after, before) * sine[...]) * scale
        rows = slice(h * HERE, (h + 1) * HERE)
        out[rows, :lanes] = turned.astype(bf16)
        out[rows, lanes:] = jnp.concatenate([v[:, part], grad_att[:, part]], 1).astype(bf16)


def own_heads(slot, order, x, dy, w_qkv, w_out, b_qkv, gain, bias, table):
    fixed = lambda shape: pl.BlockSpec(shape, lambda j: (0,) * len(shape))
    own, vector = fixed((HERE, WIDTH)), fixed((1, WIDTH))
    steps = WIDTH // BLOCK

    def part(rows, i):
        return pl.BlockSpec((rows, BLOCK), lambda j: (0, i * steps + j))

    return pl.pallas_call(
        heads_kernel,
        grid=(steps,),
        out_shape=jax.ShapeDtypeStruct((LENGTH, 4 * HEAD_DIM), bf16),
        in_specs=[SMEM] * 2
        + [own, own, part(WIDTH, 0), part(WIDTH, 1), part(WIDTH, 2)]
        + [pl.BlockSpec((BLOCK, WIDTH), lambda j: (j, 0)), part(1, 0), part(1, 1), part(1, 2)]
        + [vector, vector, fixed(table.shape)],
        out_specs=pl.BlockSpec((4 * HERE, 4 * HEAD_DIM), lambda j: (j, 0)),
        scratch_shapes=[
            pltpu.VMEM((HERE, WIDTH), bf16),
            pltpu.VMEM((HERE, 2 * HEAD_DIM), f32),
            pltpu.VMEM((HERE, 2 * HEAD_DIM), f32),
        ],
        compiler_params=params(60),
        cost_estimate=cost(1.1, 9),
        name="own_heads",
    )(slot, order, x, dy, w_qkv, w_qkv, w_qkv, w_out, b_qkv, b_qkv, b_qkv, gain, bias, table)


def attention_kernel(*refs):
    order, packed, table, out_ref, rows_in, dkv, res, turn = refs[-8:]
    groups = LENGTH // GROUP
    for g in range(groups):
        at = pl.multiple_of(order[g] * GROUP, GROUP)
        rows_in[pl.ds(at, GROUP), :] = packed[g * GROUP : (g + 1) * GROUP, :]
    q = rows_in[:, :HEAD_DIM]
    k = rows_in[:, HEAD_DIM : 2 * HEAD_DIM]
    v = rows_in[:, 2 * HEAD_DIM : 3 * HEAD_DIM]
    do = rows_in[:, 3 * HEAD_DIM :]
    k_t = k.astype(f32).T.astype(bf16)
    v_t = v.astype(f32).T.astype(bf16)
    dkv[...] = jnp.zeros_like(dkv)
    row = lax.broadcasted_iota(jnp.int32, (BLOCK, BLOCK), 0)
    col = lax.broadcasted_iota(jnp.int32, (BLOCK, BLOCK), 1)
    visible = row <= col
    for i in range(LENGTH // BLOCK):
        lo, n = i * BLOCK, (i + 1) * BLOCK
        q_i, do_i = q[lo:n], do[lo:n]
        scores = dot_nt(k[:n], q_i)
        last = jnp.where(visible, scores[lo:], -1e30)
        scores = last if i == 0 else jnp.concatenate([scores[:lo], last], 0)
        top = jnp.max(scores, 0, keepdims=True)
        weights = jnp.exp(scores - top)
        inverse = 1.0 / jnp.sum(weights, 0, keepdims=True)
        weights_b = weights.astype(bf16)
        att_t = dot_nn(v_t[:, :n], weights_b) * inverse
        grad_p = dot_nt(v[:n], do_i)
        do_f = do_i.astype(f32)
        delta = jnp.sum(att_t * do_f.T, 0, keepdims=True)
        grad_s = (weights * (grad_p - delta)).astype(bf16)
        dq_t = dot_nn(k_t[:, :n], grad_s) * (inverse * HEAD_DIM**-0.5)
        scale = column(inverse)
        dkv[:n, :HEAD_DIM] += dot_nn(grad_s, (q_i.astype(f32) * scale).astype(bf16))
        dkv[:n, HEAD_DIM:] += dot_nn(weights_b, (do_f * scale).astype(bf16))
        res[lo:n, :] = jnp.concatenate([att_t.T, dq_t.T], 1)
    lanes = 2 * HEAD_DIM
    low = lax.broadcasted_iota(jnp.int32, (1, lanes), 1) % HEAD_DIM < ROT // 2
    for g in range(groups):
        part = slice(g * GROUP, (g + 1) * GROUP)
        cosine, sine = group_rotation(table, g)
        grads = jnp.concatenate([res[part, HEAD_DIM:], dkv[part, :HEAD_DIM]], 1)
        after = pltpu.roll(grads, lanes - ROT // 2, 1)
        before = pltpu.roll(grads, ROT // 2, 1)
        turn[part, :lanes] = (
            grads * cosine + jnp.where(low, after, -before) * sine
        ).astype(bf16)
        turn[part, lanes:] = jnp.concatenate(
            [dkv[part, HEAD_DIM:], res[part, :HEAD_DIM]], 1
        ).astype(bf16)
    for g in range(groups):
        at = pl.multiple_of(order[g] * GROUP, GROUP)
        out_ref[g * GROUP : (g + 1) * GROUP, :] = turn[pl.ds(at, GROUP), :]


def attention(order, packed, table, first=()):
    lanes = 2 * HEAD_DIM
    return pl.pallas_call(
        attention_kernel,
        out_shape=jax.ShapeDtypeStruct((LENGTH, 2 * lanes), bf16),
        in_specs=[ANY] * len(first) + [SMEM] + [VMEM] * 2,
        out_specs=VMEM,
        scratch_shapes=[
            pltpu.VMEM((LENGTH, 2 * lanes), bf16),
            pltpu.VMEM((LENGTH, lanes), f32),
            pltpu.VMEM((LENGTH, lanes), f32),
            pltpu.VMEM((LENGTH, 2 * lanes), bf16),
        ],
        compiler_params=params(60),
        cost_estimate=cost(15, 8, LENGTH * LENGTH // 2),
        name="attention",
    )(*first, order, packed, table)


def cut_kernel(slot, w_qkv, w_gate, w_up, out_qkv, out_gate, out_up, wide_qkv, wide_gu, sems):
    here = slot[0]
    first = here * FF_LOCAL
    tile = jnp.minimum(first // 128, (FF - 384) // 128) * 128
    copies = []
    for i in range(3):
        lanes = pl.ds(pl.multiple_of(here // 2 * 128 + i * WIDTH, 128), 128)
        to = wide_qkv.at[:, i * 128 : (i + 1) * 128]
        copies.append(pltpu.make_async_copy(w_qkv.at[:, lanes], to, sems.at[i]))
    for i, source in enumerate((w_gate, w_up)):
        lanes = pl.ds(pl.multiple_of(tile, 128), 384)
        copies.append(pltpu.make_async_copy(source.at[:, lanes], wide_gu.at[i], sems.at[3 + i]))
    for copy in copies:
        copy.start()
    row = lax.broadcasted_iota(jnp.int32, (384, 256), 0)
    lane = lax.broadcasted_iota(jnp.int32, (384, 256), 1)
    source = lane // HEAD_DIM * 128 + here % 2 * HEAD_DIM + lane % HEAD_DIM
    pick_qkv = ((row == source) & (lane < 3 * HEAD_DIM)).astype(bf16)
    pick_gu = (row == lane + (first - tile)).astype(bf16)[:, :FF_LOCAL]
    for copy in copies:
        copy.wait()
    out_qkv[...] = dot_nn(wide_qkv[...], pick_qkv).astype(bf16)
    out_gate[...] = dot_nn(wide_gu[0], pick_gu).astype(bf16)
    out_up[...] = dot_nn(wide_gu[1], pick_gu).astype(bf16)


def cut_weights(slot, w_qkv, w_gate, w_up):
    return pl.pallas_call(
        cut_kernel,
        out_shape=[
            jax.ShapeDtypeStruct((WIDTH, 256), bf16),
            jax.ShapeDtypeStruct((WIDTH, FF_LOCAL), bf16),
            jax.ShapeDtypeStruct((WIDTH, FF_LOCAL), bf16),
        ],
        in_specs=[SMEM] + [ANY] * 3,
        out_specs=[VMEM] * 3,
        scratch_shapes=[
            pltpu.VMEM((WIDTH, 384), bf16),
            pltpu.VMEM((2, WIDTH, 384), bf16),
            pltpu.SemaphoreType.DMA((5,)),
        ],
        compiler_params=params(60),
        cost_estimate=cost(0.001, 0.001),
        name="cut_weights",
    )(slot, w_qkv, w_gate, w_up)


def column(row):
    return jnp.broadcast_to(row, (8, row.shape[1])).T[:, :1]


def weights_kernel(pieces, n_refs, slot, *refs):
    inputs, refs = refs[:n_refs], refs[n_refs:]
    heads_in, w_qkv, w_g, w_u, w_d_in, gain, bias, block_out = refs[:8]
    x_all, dy, unit, heads, acts, grads_g, grads_u, stage, w_d, block = refs[8:18]
    piece_sems, head_sems, out_sems, weight_sem = refs[18:]
    here = slot[0]
    w_d_copy = pltpu.make_async_copy(
        w_d_in.at[pl.ds(pl.multiple_of(here * FF_LOCAL, 16), FF_LOCAL), :], w_d, weight_sem
    )
    w_d_copy.start()
    copies = []
    for i, (which, ref, at, rows, chip, offset) in enumerate(pieces):
        copy = pltpu.make_async_copy(
            inputs[ref].at[pl.ds(at, rows), :],
            (x_all, dy)[which].at[pl.ds(chip * HERE + offset, rows), :],
            piece_sems.at[i],
        )
        copy.start()
        copies.append(copy)
    for i in range(SEQ):
        copy = pltpu.make_async_copy(
            heads_in.at[pl.ds(pl.multiple_of(slot[i] * HERE, HERE), HERE), :],
            heads.at[pl.ds(i * HERE, HERE), :],
            head_sems.at[i],
        )
        copy.start()
        copies.append(copy)
    for copy in copies + [w_d_copy]:
        copy.wait()
    totals = [0.0, 0.0]
    for i in range(LENGTH // BLOCK):
        rows = slice(i * BLOCK, (i + 1) * BLOCK)
        unit_f, _ = normalise(x_all[rows, :])
        hid = (unit_f * gain[...] + bias[...]).astype(bf16)
        unit[rows, :] = unit_f.astype(bf16)
        gate = dot_nn(hid, w_g[...])
        up = dot_nn(hid, w_u[...])
        act, grad_g, grad_u = gated(gate, up, dot_nt(dy[rows, :], w_d[...]))
        acts[rows, :] = act
        grads_g[rows, :] = grad_g
        grads_u[rows, :] = grad_u
        totals[0] += jnp.sum(grad_g.astype(f32), 0, keepdims=True)
        totals[1] += jnp.sum(grad_u.astype(f32), 0, keepdims=True)
    gain_col, bias_col = column(gain[...]), column(bias[...])
    grads_all = heads[:, : 3 * HEAD_DIM]
    total_h = jnp.sum(grads_all.astype(f32), 0, keepdims=True)
    inner = [dot_tn(grads, unit[...]).T for grads in (grads_g[...], grads_u[...], grads_all)]
    terms, gain_part, bias_part = [], 0.0, 0.0
    for one, weights, total in zip(inner, (w_g, w_u, w_qkv), totals + [total_h]):
        wide = weights[:, : one.shape[1]].astype(f32)
        terms.append(one * gain_col + bias_col * total)
        gain_part += jnp.sum(one * wide, 1, keepdims=True)
        bias_part += jnp.sum(wide * total, 1, keepdims=True)
    at_row = lax.broadcasted_iota(jnp.int32, (192, HERE), 0)
    owner = (at_row // HEAD_DIM * WIDTH + here * HEAD_DIM + at_row % HEAD_DIM) // 24
    mine = owner == lax.broadcasted_iota(jnp.int32, (192, HERE), 1)
    at_row = lax.broadcasted_iota(jnp.int32, (192, 256), 0)
    place = (at_row // HEAD_DIM * WIDTH + here * HEAD_DIM + at_row % HEAD_DIM) % 24 + 192
    pick = (place == lax.broadcasted_iota(jnp.int32, (192, 256), 1)).astype(bf16)
    extra = dot_tn(jnp.where(mine, column(total_h), 0.0).astype(bf16), pick)
    first_row = lax.broadcasted_iota(jnp.int32, (1, 8, 1), 1) == 0
    last = jnp.concatenate([terms[2], jnp.zeros((WIDTH, 64), f32)], 1).reshape(HERE, 8, 256)
    last += jnp.where(first_row, extra[:, None, :], 0.0)
    stage[:, :384] = jnp.concatenate(
        terms[:2] + [gain_part, bias_part, jnp.zeros((WIDTH, 30), f32)], 1
    )
    stage[:, 384:] = last.reshape(WIDTH, 256)
    down_all = dot_tn(acts[...], dy[...])
    out_all = dot_tn(heads[:, 3 * HEAD_DIM :], dy[...])
    outs = []
    for r in range(ROWS):
        for s in range(0, SEQ, 2):
            first, second = (s * ROWS + r) * 8, ((s + 1) * ROWS + r) * 8
            block[r, s * 8 : s * 8 + 16, :] = jnp.concatenate(
                [stage[first : first + 8, :], stage[second : second + 8, :]], 0
            ).astype(bf16)
        both = jnp.concatenate(
            [out_all[r * 8 : r * 8 + 8], down_all[r * 22 : (r + 1) * 22], jnp.zeros((2, WIDTH), f32)],
            0,
        ).astype(bf16)
        block[r, HERE : HERE + 32, :] = both[:, :640]
        block[r, HERE + 32 :, :384] = both[:, 640:]
        block[r, HERE + 32 :, 384:] = jnp.zeros((32, 256), bf16)
        outs.append(pltpu.make_async_copy(block.at[r], block_out.at[r], out_sems.at[r]))
        outs[r].start()
    for copy in outs:
        copy.wait()


def weight_grads(slot, arrays, pieces, heads, w_qkv, w_g, w_u, w_d, gain, bias):
    big = (LENGTH, WIDTH)
    return pl.pallas_call(
        lambda *refs: weights_kernel(pieces, len(arrays), *refs),
        out_shape=jax.ShapeDtypeStruct((ROWS, 192, 640), bf16),
        in_specs=[SMEM] + [ANY] * (len(arrays) + 1) + [VMEM] * 3 + [ANY] + [VMEM] * 2,
        out_specs=ANY,
        scratch_shapes=[pltpu.VMEM(big, bf16)] * 3
        + [pltpu.VMEM((LENGTH, 4 * HEAD_DIM), bf16)]
        + [pltpu.VMEM((LENGTH, FF_LOCAL), bf16)] * 3
        + [
            pltpu.VMEM((WIDTH, 640), f32),
            pltpu.VMEM((FF_LOCAL, WIDTH), bf16),
            pltpu.VMEM((ROWS, 192, 640), bf16),
            pltpu.SemaphoreType.DMA((len(pieces),)),
            pltpu.SemaphoreType.DMA((SEQ,)),
            pltpu.SemaphoreType.DMA((ROWS,)),
            pltpu.SemaphoreType.DMA,
        ],
        compiler_params=params(60),
        cost_estimate=cost(8, 20),
        name="weight_grads",
    )(slot, *arrays, heads, w_qkv, w_g, w_u, w_d, gain, bias)


def final_kernel(heads, x, dy, part, grad, gain, w_out, w_qkv, out, input_grad, att, rows, total):
    step = pl.program_id(0)

    @pl.when(step == 0)
    def _():
        for h in range(HEADS):
            here = heads[h * HERE : (h + 1) * HERE, :]
            at = h * HEAD_DIM
            for i in range(3):
                lo = i * WIDTH + at
                rows[:, lo : lo + HEAD_DIM] = here[:, i * HEAD_DIM : (i + 1) * HEAD_DIM]
            att[:, at : at + HEAD_DIM] = here[:, 3 * HEAD_DIM :]

    columns = pl.ds(pl.multiple_of(step * BLOCK, BLOCK), BLOCK)
    out[:, columns] = (part[:, columns] + dot_nn(att[...], w_out[...])).astype(bf16)
    total[:, columns] = grad[:, columns] + dot_nt(rows[...], w_qkv[...])

    @pl.when(step == pl.num_programs(0) - 1)
    def _():
        unit, inv_std = normalise(x[...])
        grad_unit = total[...] * gain[...]
        grad_norm = inv_std * (
            grad_unit
            - jnp.mean(grad_unit, 1, keepdims=True)
            - unit * jnp.mean(grad_unit * unit, 1, keepdims=True)
        )
        input_grad[...] = (dy[...].astype(f32) + grad_norm).astype(bf16)


def final_rows(heads, x, dy, part, grad, gain, w_out, w_qkv):
    fixed = lambda shape: pl.BlockSpec(shape, lambda j: (0,) * len(shape))
    own = fixed((HERE, WIDTH))
    return pl.pallas_call(
        final_kernel,
        grid=(WIDTH // BLOCK,),
        out_shape=[jax.ShapeDtypeStruct((HERE, WIDTH), bf16)] * 2,
        in_specs=[fixed((LENGTH, 256)), own, own, own, own, fixed((1, WIDTH))]
        + [pl.BlockSpec((WIDTH, BLOCK), lambda j: (0, j))]
        + [pl.BlockSpec((BLOCK, 3 * WIDTH), lambda j: (j, 0))],
        out_specs=[own, own],
        scratch_shapes=[
            pltpu.VMEM((HERE, WIDTH), bf16),
            pltpu.VMEM((HERE, 3 * WIDTH), bf16),
            pltpu.VMEM((HERE, WIDTH), f32),
        ],
        compiler_params=params(60),
        cost_estimate=cost(1.1, 10),
        name="final_rows",
    )(heads, x, dy, part, grad, gain, w_out, w_qkv)


def sum_kernel(got, send, down, out):
    total = got[0].astype(f32)
    for r in range(1, ROWS):
        total += got[r].astype(f32)
    send[...] = total[:HERE].astype(bf16)
    first, second = total[HERE : HERE + 32], total[HERE + 32 :, :384]
    out[:, :640] = first[:8]
    out[:, 640:] = second[:8]
    down[:, :640] = first[8:30]
    down[:, 640:] = second[8:30]


def sum_rows(got):
    return pl.pallas_call(
        sum_kernel,
        out_shape=[
            jax.ShapeDtypeStruct((HERE, 640), bf16),
            jax.ShapeDtypeStruct((22, WIDTH), f32),
            jax.ShapeDtypeStruct((8, WIDTH), f32),
        ],
        in_specs=[VMEM],
        out_specs=[VMEM] * 3,
        compiler_params=params(16),
        cost_estimate=cost(0.001, 2),
        name="sum_rows",
    )(got)


def layout_kernel(mine, qkv, gate, up, vectors, sums):
    total = jnp.zeros((8, 256), f32)
    more = jnp.zeros((8, 128), f32)
    for s in range(SEQ):
        here = mine[s * 8 : (s + 1) * 8, :].astype(f32)
        gate[:, s * FF_LOCAL : (s + 1) * FF_LOCAL] = here[:, :FF_LOCAL]
        up[:, s * FF_LOCAL : (s + 1) * FF_LOCAL] = here[:, FF_LOCAL : 2 * FF_LOCAL]
        for i in range(3):
            lo = i * WIDTH + s * HEAD_DIM
            qkv[:, lo : lo + HEAD_DIM] = here[:, 384 + i * HEAD_DIM : 384 + (i + 1) * HEAD_DIM]
        total += here[:, 384:]
        more += here[:, 256:384]
    vectors[...] = more.T[96:98, :]
    sums[...] = total[0:1, 192:216]


def last_layout(mine):
    return pl.pallas_call(
        layout_kernel,
        out_shape=[
            jax.ShapeDtypeStruct((8, 3 * WIDTH), f32),
            jax.ShapeDtypeStruct((8, FF), f32),
            jax.ShapeDtypeStruct((8, FF), f32),
            jax.ShapeDtypeStruct((2, 8), f32),
            jax.ShapeDtypeStruct((1, 24), f32),
        ],
        in_specs=[VMEM],
        out_specs=[VMEM] * 5,
        compiler_params=params(16),
        cost_estimate=cost(0.001, 1),
        name="last_layout",
    )(mine)


PLACES = [(0, 0), (0, -1), (0, 1), (1, 0), (0, 2), (1, 1), (1, -1), (1, 2)]
CORE = [(i, i ^ 1) for i in range(SEQ)]
PAIR = [(i, i ^ 2) for i in range(SEQ)]
UP = [(i, (i + 4) % SEQ) for i in range(SEQ)]
DOWN = [(i, (i + 12) % SEQ) for i in range(SEQ)]


def send(value, to):
    return lax.ppermute(value, "seq", to)


def gather(x, dy, exchange, after):
    half = HERE
    own = jnp.concatenate([x, dy], 0)
    below = send(own, UP)
    above = send(own, DOWN)
    pair = send(own, PAIR)
    late = exchange((below, above, pair))
    far = send(below, UP)
    across_above = send(pair, DOWN)
    across_below = send(below, PAIR)
    far, _ = lax.optimization_barrier((far, late))
    opposite = send(far, PAIR)
    arrays = [own, below, above, pair, far, across_above, across_below, opposite]
    late, arrays[4:] = after(late, arrays[4:])
    arrays += [send(a, CORE) for a in arrays]
    table = []
    for i in range(len(PLACES)):
        for core in range(2):
            for which in range(2):
                table.append((which, i + core * len(PLACES), which * half, half, 2 * i + core, 0))
    return arrays, table, late


def shards(x, dy, order, ln_gain, ln_bias, w_qkv, b_qkv, w_out, w_gate, w_up, w_down):
    x, dy = x[0], dy[0]
    s = lax.axis_index("seq")
    slot = jnp.stack(
        [
            ((s // 4 + up) % 4) * 4 + ((s // 2 % 2) ^ across) * 2 + (s % 2 ^ core)
            for across, up in PLACES
            for core in range(2)
        ]
    ).astype(jnp.int32)
    gain, bias = ln_gain[None, :], ln_bias[None, :]

    table = rotary_tables()
    packed = own_heads(slot, order, x, dy, w_qkv, w_out, b_qkv[None, :], gain, bias, table)
    part, grad = own_rows(x, dy, gain, bias, w_gate, w_up, w_down)
    w_qkv_s, w_gate_s, w_up_s = cut_weights(slot, w_qkv, w_gate, w_up)

    def exchange(first):
        ready, _ = lax.optimization_barrier((packed, first))
        return lax.all_to_all(ready, "seq", 0, 0, tiled=True)

    def attend(packed_here, arrays):
        heads = attention(order, packed_here, table, (part, w_gate_s))
        return lax.optimization_barrier((heads, arrays))

    arrays, pieces, heads = gather(x, dy, exchange, attend)
    heads_here = lax.all_to_all(heads, "seq", 0, 0, tiled=True)
    block = weight_grads(
        slot, arrays, pieces, heads, w_qkv_s, w_gate_s, w_up_s, w_down, gain, bias
    )
    block, heads_here = lax.optimization_barrier((block, heads_here))
    got = lax.all_to_all(block, "rows", 0, 0, tiled=True)
    output, input_grad = final_rows(heads_here, x, dy, part, grad, gain, w_out, w_qkv)
    got, output, input_grad = lax.optimization_barrier((got, output, input_grad))
    outgoing, o_down, o_out = sum_rows(got)
    mine = lax.all_to_all(outgoing, "seq", 0, 0, tiled=True)
    o_qkv, o_gate, o_up, vectors, sums = last_layout(mine)
    return (
        output[None],
        input_grad[None],
        o_qkv,
        o_out,
        o_gate,
        o_up,
        o_down,
        sums[0],
        vectors[0],
        vectors[1],
    )


def solution(mesh):
    rows = P("rows", "seq", None)
    both = P(("seq", "rows"), None)
    flat = P(("seq", "rows"))
    return jax.shard_map(
        shards,
        mesh=mesh,
        in_specs=(rows, rows) + (P(),) * 9,
        out_specs=(rows, rows, both, both, both, both, both, flat, flat, flat),
        check_vma=False,
    )
```

time: 154 us -> 139 us (0.903)
  local copies, waits for them, and re-layouts: 23.5 us -> 2.26 us
  blocking collectives: 0 us -> 12.2 us
  waiting for transfers between devices: 28.9 us -> 20.1 us
  Pallas kernels: 63.3 us -> 70.1 us
  starting transfers between devices: 34.9 us -> 31.4 us
    ppermute x19 -> x15, waiting for transfers between devices: 22.5 us -> 3.3 us  [send(): return lax.ppermute(value, 'seq', to)]
    all_to_all x1, waiting for transfers between devices: 0.01 us -> 16.8 us  [shards(): got = lax.all_to_all(block, 'rows', 0, 0, tiled=True)]
    unnamed x46 -> x18, local copies, waits for them, and re-layouts: 14.2 us -> 1.09 us
    all_to_all x0 -> x1, blocking collectives: none -> 12.2 us  [shards(): mine = lax.all_to_all(outgoing, 'seq', 0, 0, tiled=True)]
    dynamic_slice x6 -> x0, local copies, waits for them, and re-layouts: 8.25 us -> none  [the longest x5 7.66 us: cut(): return lax.dynamic_slice_in_dim(array, at, size, axis)]
    all_to_all x1, waiting for transfers between devices: 6.44 us -> 0.01 us  [exchange(): return lax.all_to_all(ready, 'seq', 0, 0, tiled=True)]
    ppermute x19 -> x15, starting transfers between devices: 17.7 us -> 13.9 us  [send(): return lax.ppermute(value, 'seq', to)]
    pallas_call x2 -> x3, Pallas kernels: 25.3 us -> 28.5 us  [the longest x1 17.1 us: weight_grads(): pl.pallas_call(lambda *refs: weights_kernel(pieces, len(arrays), *refs),...]
  transfers between devices with their start and end apart: 22 -> 18, of which waited for: 8 -> 5; matrix products, arithmetic and copies ran while one was open for 5% -> 0% of each run, Pallas kernels for 23% -> 50%
where the time goes in v1:
time: 139 us; the launch traced here: 138 us
  Pallas kernels  70.1 us (50%)
  starting transfers between devices  31.4 us (23%)
  waiting for transfers between devices  20.1 us (14%)
  blocking collectives  12.2 us (9%)
  local copies, waits for them, and re-layouts  2.26 us (2%)
    pallas_call x1, Pallas kernels, weight_grads(): pl.pallas_call(lambda *refs: weights_kernel(pieces, len(arrays), *refs),...  17.1 us
    all_to_all x1, waiting for transfers between devices, shards(): got = lax.all_to_all(block, 'rows', 0, 0, tiled=True)  16.8 us
    pallas_call x1, Pallas kernels, own_rows(): pl.pallas_call(own_kernel, grid=(FF // BLOCK,), out_shape=[jax.ShapeDtype...  16.2 us
    pallas_call x1, Pallas kernels, attention(): pl.pallas_call(attention_kernel, out_shape=jax.ShapeDtypeStruct((LENGTH,...  15.8 us
    ppermute x15, starting transfers between devices, send(): return lax.ppermute(value, 'seq', to)  13.9 us
    all_to_all x1, blocking collectives, shards(): mine = lax.all_to_all(outgoing, 'seq', 0, 0, tiled=True)  12.2 us
    pallas_call x1, Pallas kernels, final_rows(): pl.pallas_call(final_kernel, grid=(WIDTH // BLOCK,), out_shape=[jax.Shape...  8.03 us
    all_to_all x1, starting transfers between devices, shards(): got = lax.all_to_all(block, 'rows', 0, 0, tiled=True)  7.47 us
  transfers between devices with their start and end apart: 18, of which 5 were waited for; matrix products, arithmetic and copies ran while one was open for 0% of the time, Pallas kernels for 50%

profile of v1, /device:TPU:1, one launch (start us, length us, event | category | flops | bytes accessed | tf_op | source)
XLA Modules:
  0.0 137.9 jit_solution(13730976658712712170)
XLA Ops:
  0.6 1.1 pad_maximum_fusion.refs_1_
  1.7 2.2 %collective-permute-start = (bf16[256,1024]{1,0:T(8,128)(2,1)S(1)}, bf16[256,1024]{1,0:T(8,128)(2,1)S(1)}, u32[]{:S(2)}, u32[]{:S(2)}) collective-permute-start(bf16[256,1024]{1,0:T(8,128)(2,1)S(1)} %pad_maximum_fusion.refs_1_), channel_id=1, source_target_pairs={{0,32},{8,40},{16,48},{24,56},{32,64},{40,72},{48,80},{56,88},{64,... | collective-permute-start | bytes 1572872 | tf_op jit(solution)/shard_map/ppermute | solution.py:538
  3.9 1.2 collective-permute-start.2
  5.1 1.5 %collective-permute-start.1 = (bf16[256,1024]{1,0:T(8,128)(2,1)S(1)}, bf16[256,1024]{1,0:T(8,128)(2,1)S(1)}, u32[]{:S(2)}, u32[]{:S(2)}) collective-permute-start(bf16[256,1024]{1,0:T(8,128)(2,1)S(1)} %pad_maximum_fusion.refs_1_), channel_id=1, source_target_pairs={{0,96},{8,104},{16,112},{24,120},{32,0},{40,8},{48,16},{56,24},{64... | collective-permute-start | bytes 1572872 | tf_op jit(solution)/shard_map/ppermute | solution.py:538
  6.7 0.6 stack.67.slot.refs_0_
  7.3 7.1 %own_heads.1 = bf16[2048,256]{1,0:T(8,128)(2,1)} custom-call(s32[16]{0:T(128)} %stack.67.slot.refs_0_, s32[32]{0:T(128)} %refs_2_.1, bf16[128,1024]{1,0:T(8,128)(2,1)} %bitcast.37, bf16[128,1024]{1,0:T(8,128)(2,1)} %bitcast.41, bf16[1024,3072]{1,0:T(8,128)(2,1)} %w_qkv.3, bf16[1024,3072]{1,0:T(8,128)(2,1)} %w_qkv.3, bf16[1024,3072]{1,0:T(8,128)(2,1)} %w_qkv.3, ...), custom_call_target="tpu_custom_call" | custom-call | flops 1100000000 | bytes 9437184 | tf_op jit(solution)/shard_map/own_heads/pallas_call | solution.py:158
  14.4 2.4 %collective-permute-done.refs_2_ = bf16[256,1024]{1,0:T(8,128)(2,1)S(1)} collective-permute-done((bf16[256,1024]{1,0:T(8,128)(2,1)S(1)}, bf16[256,1024]{1,0:T(8,128)(2,1)S(1)}, u32[]{:S(2)}, u32[]{:S(2)}) %collective-permute-start) | collective-permute-done | bytes 524320 | tf_op jit(solution)/shard_map/ppermute | solution.py:538
  16.9 0.0 collective-permute-done.2.refs_4_
  16.9 0.4 collective-permute-done.1.refs_3_
  17.3 6.5 %all-to-all-start = ((bf16[16,128,256]{2,1,0:T(8,128)(2,1)}), bf16[16,128,256]{2,1,0:T(8,128)(2,1)S(1)}, u32[]{:S(2)}, u32[]{:S(2)}) async-start(bf16[16,128,256]{2,1,0:T(8,128)(2,1)} %bitcast.45), calls=%async_computation | async-start | bytes 2097152 | tf_op jit(solution)/shard_map/all_to_all | solution.py:583
  23.8 1.4 %collective-permute-start.3 = (bf16[256,1024]{1,0:T(8,128)(2,1)S(1)}, bf16[256,1024]{1,0:T(8,128)(2,1)}, u32[]{:S(2)}, u32[]{:S(2)}) collective-permute-start(bf16[256,1024]{1,0:T(8,128)(2,1)S(1)} %collective-permute-done.refs_2_), channel_id=1, source_target_pairs={{0,32},{8,40},{16,48},{24,56},{32,64},{40,72},{48,80},{56,88},{64,... | collective-permute-start | bytes 1572872 | tf_op jit(solution)/shard_map/ppermute | solution.py:538
  25.2 1.2 collective-permute-start.5
  26.4 0.9 collective-permute-start.7
  27.3 4.3 %cut_weights.1 = (bf16[1024,256]{1,0:T(8,128)(2,1)}, bf16[1024,176]{1,0:T(8,128)(2,1)}, bf16[1024,176]{1,0:T(8,128)(2,1)}) custom-call(s32[16]{0:T(128)} %stack.67.slot.refs_0_, bf16[1024,3072]{1,0:T(8,128)(2,1)} %w_qkv.3, bf16[1024,2816]{1,0:T(8,128)(2,1)} %w_gate.1, bf16[1024,2816]{1,0:T(8,128)(2,1)} %w_up.1), custom_call_target="tpu_custom_call" | custom-call | flops 1000000 | bytes 1048 | tf_op jit(solution)/shard_map/cut_weights/pallas_call | solution.py:279
  31.6 16.2 %own_rows.1 = (f32[128,1024]{1,0:T(8,128)}, f32[128,1024]{1,0:T(8,128)}) custom-call(bf16[128,1024]{1,0:T(8,128)(2,1)} %bitcast.38, bf16[128,1024]{1,0:T(8,128)(2,1)} %bitcast.42, f32[1,1024]{1,0:T(1,128)} %bitcast.52, f32[1,1024]{1,0:T(1,128)} %bitcast.56, bf16[1024,2816]{1,0:T(8,128)(2,1)} %w_gate.1, bf16[1024,2816]{1,0:T(8,128)(2,1)} %w_up.1, ...), custom_call_target="tpu_custom_call" | custom-call | flops 1000000 | bytes 1048 | tf_op jit(solution)/shard_map/own_rows/pallas_call | solution.py:104
  47.8 1.5 %collective-permute-start.4 = (bf16[256,1024]{1,0:T(8,128)(2,1)S(1)}, bf16[256,1024]{1,0:T(8,128)(2,1)}, u32[]{:S(2)}, u32[]{:S(2)}) collective-permute-start(bf16[256,1024]{1,0:T(8,128)(2,1)S(1)} %collective-permute-done.2.refs_4_), channel_id=1, source_target_pairs={{0,96},{8,104},{16,112},{24,120},{32,0},{40,8},{48,16},{56,24},{64... | collective-permute-start | bytes 1572872 | tf_op jit(solution)/shard_map/ppermute | solution.py:538
  49.3 0.3 collective-permute-start.8
  49.6 0.3 collective-permute-done.3.refs_5_
  49.9 0.9 collective-permute-start.10
  50.8 0.0 all-to-all-done
  50.8 0.0 collective-permute-done.5.refs_7_
  50.8 1.4 %collective-permute-start.6 = (bf16[256,1024]{1,0:T(8,128)(2,1)}, bf16[256,1024]{1,0:T(8,128)(2,1)}, u32[]{:S(2)}, u32[]{:S(2)}) collective-permute-start(bf16[256,1024]{1,0:T(8,128)(2,1)} %collective-permute-done.3.refs_5_), channel_id=1, source_target_pairs={{0,16},{8,24},{16,0},{24,8},{32,48},{40,56},{48,32},{56,40},{64,80... | collective-permute-start | bytes 1572872 | tf_op jit(solution)/shard_map/ppermute | solution.py:538
  52.3 15.8 %attention.1.refs_17_ = bf16[2048,256]{1,0:T(8,128)(2,1)} custom-call(f32[128,1024]{1,0:T(8,128)} %get-tuple-element.37.refs_0_.part, bf16[1024,176]{1,0:T(8,128)(2,1)} %get-tuple-element.38.refs_1_.refs_19_, s32[32]{0:T(128)} %refs_2_.1, bf16[2048,256]{1,0:T(8,128)(2,1)} %bitcast.47, f32[192,128]{1,0:T(8,128)} %constant.212.clone.table.refs_4_), custom_call_target="tpu_custom_call" | custom-call | flops 15000000512 | bytes 8388608 | tf_op jit(solution)/shard_map/attention/pallas_call | solution.py:235
  68.1 0.0 collective-permute-done.4.refs_6_
  68.1 0.3 collective-permute-start.9
  68.4 0.2 collective-permute-start.11
  68.6 0.0 collective-permute-done.7.refs_9_
  68.6 0.3 collective-permute-start.12
  68.9 0.2 collective-permute-start.13
  69.1 0.0 collective-permute-done.10.refs_12_
  69.1 0.3 collective-permute-start.14
  69.5 3.6 %all-to-all-start.1 = ((bf16[16,128,256]{2,1,0:T(8,128)(2,1)}), bf16[16,128,256]{2,1,0:T(8,128)(2,1)S(1)}, u32[]{:S(2)}, u32[]{:S(2)}) async-start(bf16[16,128,256]{2,1,0:T(8,128)(2,1)} %bitcast.46), calls=%async_computation.1 | async-start | bytes 2097152 | tf_op jit(solution)/shard_map/all_to_all | solution.py:590
  73.1 0.0 collective-permute-done.9.refs_11_
  73.1 0.0 collective-permute-done.12.refs_14_
  73.1 0.0 collective-permute-done.13.refs_15_
  73.1 0.1 collective-permute-done.14.refs_16_
  73.2 0.7 copy-done.6
  73.9 0.2 copy-done.7
  74.1 0.1 copy-done.8
  74.3 17.1 %weight_grads.1 = bf16[8,192,640]{2,1,0:T(8,128)(2,1)} custom-call(s32[16]{0:T(128)} %stack.67.slot.refs_0_, bf16[256,1024]{1,0:T(8,128)(2,1)} %copy-done.2, bf16[256,1024]{1,0:T(8,128)(2,1)} %copy-done.3, bf16[256,1024]{1,0:T(8,128)(2,1)} %copy-done.5, bf16[256,1024]{1,0:T(8,128)(2,1)} %copy-done.4, bf16[256,1024]{1,0:T(8,128)(2,1)} %collective-permute-done.3.refs_5_, ...), custom_call_target="tpu_custom_call" | custom-call | flops 8000000000 | bytes 20971520 | tf_op jit(solution)/shard_map/weight_grads/pallas_call | solution.py:394
  91.3 0.0 all-to-all-done.1
  91.3 7.5 %all-to-all-start.2 = ((bf16[8,192,640]{2,1,0:T(8,128)(2,1)}), bf16[8,192,640]{2,1,0:T(8,128)(2,1)S(1)}, u32[]{:S(2)}, u32[]{:S(2)}) async-start(bf16[8,192,640]{2,1,0:T(8,128)(2,1)} %weight_grads.1), calls=%async_computation.2 | async-start | bytes 3932160 | tf_op jit(solution)/shard_map/all_to_all | solution.py:595
  98.8 8.0 %final_rows.1 = (bf16[128,1024]{1,0:T(8,128)(2,1)}, bf16[128,1024]{1,0:T(8,128)(2,1)}) custom-call(bf16[2048,256]{1,0:T(8,128)(2,1)} %bitcast.44, bf16[128,1024]{1,0:T(8,128)(2,1)} %bitcast.39, bf16[128,1024]{1,0:T(8,128)(2,1)} %bitcast.43, f32[128,1024]{1,0:T(8,128)} %get-tuple-element.37.refs_0_.part, f32[128,1024]{1,0:T(8,128)} %get-tuple-element.50.grad, ...), custom_call_target="tpu_custom_call" | custom-call | flops 1100000000 | bytes 10485760 | tf_op jit(solution)/shard_map/final_rows/pallas_call | solution.py:449
  106.8 16.8 %all-to-all-done.2.got = bf16[8,192,640]{2,1,0:T(8,128)(2,1)S(1)} async-done(((bf16[8,192,640]{2,1,0:T(8,128)(2,1)}), bf16[8,192,640]{2,1,0:T(8,128)(2,1)S(1)}, u32[]{:S(2)}, u32[]{:S(2)}) %all-to-all-start.2) | async-done | bytes 1966112 | tf_op jit(solution)/shard_map/all_to_all | solution.py:595
  123.6 0.7 sum_rows.1
  124.3 12.2 %all_to_all.39 = bf16[16,8,640]{2,1,0:T(8,128)(2,1)S(1)} all-to-all(bf16[16,8,640]{2,1,0:T(8,128)(2,1)S(1)} %bitcast.35), channel_id=1, replica_groups=mesh['seq'=16,'rows'=8] {'seq'}, dimensions={0} | all-to-all | bytes 327680 | tf_op jit(solution)/shard_map/all_to_all | solution.py:599
  136.5 0.8 last_layout.1
  137.3 0.5 slice_bitcast_fusion
  (18 shorter events, 0.0 us)
Async XLA Ops:
  1.7 24.6 %copy-start.2 = (bf16[256,1024]{1,0:T(8,128)(2,1)}, bf16[256,1024]{1,0:T(8,128)(2,1)S(1)}, u32[]{:S(2)}) copy-start(bf16[256,1024]{1,0:T(8,128)(2,1)S(1)} %pad_maximum_fusion.refs_1_) | copy-start | bytes 1572868
  1.7 15.1 %collective-permute-start = (bf16[256,1024]{1,0:T(8,128)(2,1)S(1)}, bf16[256,1024]{1,0:T(8,128)(2,1)S(1)}, u32[]{:S(2)}, u32[]{:S(2)}) collective-permute-start(bf16[256,1024]{1,0:T(8,128)(2,1)S(1)} %pad_maximum_fusion.refs_1_), channel_id=1, source_target_pairs={{0,32},{8,40},{16,48},{24,56},{32,64},{40,72},{48,80},{56,88},{64,... | collective-permute-start | bytes 1572872 | tf_op jit(solution)/shard_map/ppermute | solution.py:538
  3.9 12.9 %collective-permute-start.2 = (bf16[256,1024]{1,0:T(8,128)(2,1)S(1)}, bf16[256,1024]{1,0:T(8,128)(2,1)S(1)}, u32[]{:S(2)}, u32[]{:S(2)}) collective-permute-start(bf16[256,1024]{1,0:T(8,128)(2,1)S(1)} %pad_maximum_fusion.refs_1_), channel_id=1, source_target_pairs={{0,16},{8,24},{16,0},{24,8},{32,48},{40,56},{48,32},{56,40},{64,80... | collective-permute-start | bytes 1572872 | tf_op jit(solution)/shard_map/ppermute | solution.py:538
  5.1 12.2 %collective-permute-start.1 = (bf16[256,1024]{1,0:T(8,128)(2,1)S(1)}, bf16[256,1024]{1,0:T(8,128)(2,1)S(1)}, u32[]{:S(2)}, u32[]{:S(2)}) collective-permute-start(bf16[256,1024]{1,0:T(8,128)(2,1)S(1)} %pad_maximum_fusion.refs_1_), channel_id=1, source_target_pairs={{0,96},{8,104},{16,112},{24,120},{32,0},{40,8},{48,16},{56,24},{64... | collective-permute-start | bytes 1572872 | tf_op jit(solution)/shard_map/ppermute | solution.py:538
  16.9 32.5 %copy-start.3 = (bf16[256,1024]{1,0:T(8,128)(2,1)}, bf16[256,1024]{1,0:T(8,128)(2,1)S(1)}, u32[]{:S(2)}) copy-start(bf16[256,1024]{1,0:T(8,128)(2,1)S(1)} %collective-permute-done.refs_2_) | copy-start | bytes 1572868
  16.9 33.1 %copy-start.4 = (bf16[256,1024]{1,0:T(8,128)(2,1)}, bf16[256,1024]{1,0:T(8,128)(2,1)S(1)}, u32[]{:S(2)}) copy-start(bf16[256,1024]{1,0:T(8,128)(2,1)S(1)} %collective-permute-done.2.refs_4_) | copy-start | bytes 1572868
  17.3 50.8 %copy-start.5 = (bf16[256,1024]{1,0:T(8,128)(2,1)}, bf16[256,1024]{1,0:T(8,128)(2,1)S(1)}, u32[]{:S(2)}) copy-start(bf16[256,1024]{1,0:T(8,128)(2,1)S(1)} %collective-permute-done.1.refs_3_) | copy-start | bytes 1572868
  17.3 33.5 %all-to-all-start = ((bf16[16,128,256]{2,1,0:T(8,128)(2,1)}), bf16[16,128,256]{2,1,0:T(8,128)(2,1)S(1)}, u32[]{:S(2)}, u32[]{:S(2)}) async-start(bf16[16,128,256]{2,1,0:T(8,128)(2,1)} %bitcast.45), calls=%async_computation | async-start | bytes 2097152 | tf_op jit(solution)/shard_map/all_to_all | solution.py:583
  23.8 26.1 %collective-permute-start.3 = (bf16[256,1024]{1,0:T(8,128)(2,1)S(1)}, bf16[256,1024]{1,0:T(8,128)(2,1)}, u32[]{:S(2)}, u32[]{:S(2)}) collective-permute-start(bf16[256,1024]{1,0:T(8,128)(2,1)S(1)} %collective-permute-done.refs_2_), channel_id=1, source_target_pairs={{0,32},{8,40},{16,48},{24,56},{32,64},{40,72},{48,80},{56,88},{64,... | collective-permute-start | bytes 1572872 | tf_op jit(solution)/shard_map/ppermute | solution.py:538
  25.2 25.6 %collective-permute-start.5 = (bf16[256,1024]{1,0:T(8,128)(2,1)S(1)}, bf16[256,1024]{1,0:T(8,128)(2,1)}, u32[]{:S(2)}, u32[]{:S(2)}) collective-permute-start(bf16[256,1024]{1,0:T(8,128)(2,1)S(1)} %collective-permute-done.refs_2_), channel_id=1, source_target_pairs={{0,16},{8,24},{16,0},{24,8},{32,48},{40,56},{48,32},{56,40},{64,80... | collective-permute-start | bytes 1572872 | tf_op jit(solution)/shard_map/ppermute | solution.py:538
  26.4 42.2 %collective-permute-start.7 = (bf16[256,1024]{1,0:T(8,128)(2,1)S(1)}, bf16[256,1024]{1,0:T(8,128)(2,1)}, u32[]{:S(2)}, u32[]{:S(2)}) collective-permute-start(bf16[256,1024]{1,0:T(8,128)(2,1)S(1)} %pad_maximum_fusion.refs_1_), channel_id=1, source_target_pairs={{0,8},{8,0},{16,24},{24,16},{32,40},{40,32},{48,56},{56,48},{64,72... | collective-permute-start | bytes 1572872 | tf_op jit(solution)/shard_map/ppermute | solution.py:538
  47.8 20.3 %collective-permute-start.4 = (bf16[256,1024]{1,0:T(8,128)(2,1)S(1)}, bf16[256,1024]{1,0:T(8,128)(2,1)}, u32[]{:S(2)}, u32[]{:S(2)}) collective-permute-start(bf16[256,1024]{1,0:T(8,128)(2,1)S(1)} %collective-permute-done.2.refs_4_), channel_id=1, source_target_pairs={{0,96},{8,104},{16,112},{24,120},{32,0},{40,8},{48,16},{56,24},{64... | collective-permute-start | bytes 1572872 | tf_op jit(solution)/shard_map/ppermute | solution.py:538
  49.3 19.6 %collective-permute-start.8 = (bf16[256,1024]{1,0:T(8,128)(2,1)S(1)}, bf16[256,1024]{1,0:T(8,128)(2,1)}, u32[]{:S(2)}, u32[]{:S(2)}) collective-permute-start(bf16[256,1024]{1,0:T(8,128)(2,1)S(1)} %collective-permute-done.refs_2_), channel_id=1, source_target_pairs={{0,8},{8,0},{16,24},{24,16},{32,40},{40,32},{48,56},{56,48},{64,72... | collective-permute-start | bytes 1572872 | tf_op jit(solution)/shard_map/ppermute | solution.py:538
  49.9 19.2 %collective-permute-start.10 = (bf16[256,1024]{1,0:T(8,128)(2,1)S(1)}, bf16[256,1024]{1,0:T(8,128)(2,1)}, u32[]{:S(2)}, u32[]{:S(2)}) collective-permute-start(bf16[256,1024]{1,0:T(8,128)(2,1)S(1)} %collective-permute-done.2.refs_4_), channel_id=1, source_target_pairs={{0,8},{8,0},{16,24},{24,16},{32,40},{40,32},{48,56},{56,48},{64,72... | collective-permute-start | bytes 1572872 | tf_op jit(solution)/shard_map/ppermute | solution.py:538
  50.8 1.5 %copy-start.1 = (bf16[16,128,256]{2,1,0:T(8,128)(2,1)}, bf16[16,128,256]{2,1,0:T(8,128)(2,1)S(1)}, u32[]{:S(2)}) copy-start(bf16[16,128,256]{2,1,0:T(8,128)(2,1)S(1)} %all-to-all-done) | copy-start | bytes 3145732
  50.8 17.6 %collective-permute-start.6 = (bf16[256,1024]{1,0:T(8,128)(2,1)}, bf16[256,1024]{1,0:T(8,128)(2,1)}, u32[]{:S(2)}, u32[]{:S(2)}) collective-permute-start(bf16[256,1024]{1,0:T(8,128)(2,1)} %collective-permute-done.3.refs_5_), channel_id=1, source_target_pairs={{0,16},{8,24},{16,0},{24,8},{32,48},{40,56},{48,32},{56,40},{64,80... | collective-permute-start | bytes 1572872 | tf_op jit(solution)/shard_map/ppermute | solution.py:538
  68.1 5.0 %collective-permute-start.9 = (bf16[256,1024]{1,0:T(8,128)(2,1)S(1)}, bf16[256,1024]{1,0:T(8,128)(2,1)}, u32[]{:S(2)}, u32[]{:S(2)}) collective-permute-start(bf16[256,1024]{1,0:T(8,128)(2,1)S(1)} %collective-permute-done.1.refs_3_), channel_id=1, source_target_pairs={{0,8},{8,0},{16,24},{24,16},{32,40},{40,32},{48,56},{56,48},{64,72... | collective-permute-start | bytes 1572872 | tf_op jit(solution)/shard_map/ppermute | solution.py:538
  68.4 4.6 %collective-permute-start.11 = (bf16[256,1024]{1,0:T(8,128)(2,1)}, bf16[256,1024]{1,0:T(8,128)(2,1)}, u32[]{:S(2)}, u32[]{:S(2)}) collective-permute-start(bf16[256,1024]{1,0:T(8,128)(2,1)} %collective-permute-done.3.refs_5_), channel_id=1, source_target_pairs={{0,8},{8,0},{16,24},{24,16},{32,40},{40,32},{48,56},{56,48},{64,72... | collective-permute-start | bytes 1572872 | tf_op jit(solution)/shard_map/ppermute | solution.py:538
  68.6 4.5 %collective-permute-start.12 = (bf16[256,1024]{1,0:T(8,128)(2,1)}, bf16[256,1024]{1,0:T(8,128)(2,1)S(1)}, u32[]{:S(2)}, u32[]{:S(2)}) collective-permute-start(bf16[256,1024]{1,0:T(8,128)(2,1)} %collective-permute-done.4.refs_6_), channel_id=1, source_target_pairs={{0,8},{8,0},{16,24},{24,16},{32,40},{40,32},{48,56},{56,48},{64,72... | collective-permute-start | bytes 1572872 | tf_op jit(solution)/shard_map/ppermute | solution.py:538
  68.9 4.2 %collective-permute-start.13 = (bf16[256,1024]{1,0:T(8,128)(2,1)}, bf16[256,1024]{1,0:T(8,128)(2,1)S(1)}, u32[]{:S(2)}, u32[]{:S(2)}) collective-permute-start(bf16[256,1024]{1,0:T(8,128)(2,1)} %collective-permute-done.5.refs_7_), channel_id=1, source_target_pairs={{0,8},{8,0},{16,24},{24,16},{32,40},{40,32},{48,56},{56,48},{64,72... | collective-permute-start | bytes 1572872 | tf_op jit(solution)/shard_map/ppermute | solution.py:538
  69.1 4.1 %collective-permute-start.14 = (bf16[256,1024]{1,0:T(8,128)(2,1)}, bf16[256,1024]{1,0:T(8,128)(2,1)S(1)}, u32[]{:S(2)}, u32[]{:S(2)}) collective-permute-start(bf16[256,1024]{1,0:T(8,128)(2,1)} %collective-permute-done.6.refs_8_), channel_id=1, source_target_pairs={{0,8},{8,0},{16,24},{24,16},{32,40},{40,32},{48,56},{56,48},{64,72... | collective-permute-start | bytes 1572872 | tf_op jit(solution)/shard_map/ppermute | solution.py:538
  69.5 21.9 %all-to-all-start.1 = ((bf16[16,128,256]{2,1,0:T(8,128)(2,1)}), bf16[16,128,256]{2,1,0:T(8,128)(2,1)S(1)}, u32[]{:S(2)}, u32[]{:S(2)}) async-start(bf16[16,128,256]{2,1,0:T(8,128)(2,1)} %bitcast.46), calls=%async_computation.1 | async-start | bytes 2097152 | tf_op jit(solution)/shard_map/all_to_all | solution.py:590
  73.1 0.8 copy-start.6
  73.1 1.0 copy-start.7
  73.2 1.1 copy-start.8
  91.3 7.5 %copy-start = (bf16[16,128,256]{2,1,0:T(8,128)(2,1)}, bf16[16,128,256]{2,1,0:T(8,128)(2,1)S(1)}, u32[]{:S(2)}) copy-start(bf16[16,128,256]{2,1,0:T(8,128)(2,1)S(1)} %all-to-all-done.1) | copy-start | bytes 3145732
  91.3 32.3 %all-to-all-start.2 = ((bf16[8,192,640]{2,1,0:T(8,128)(2,1)}), bf16[8,192,640]{2,1,0:T(8,128)(2,1)S(1)}, u32[]{:S(2)}, u32[]{:S(2)}) async-start(bf16[8,192,640]{2,1,0:T(8,128)(2,1)} %weight_grads.1), calls=%async_computation.2 | async-start | bytes 3932160 | tf_op jit(solution)/shard_map/all_to_all | solution.py:595

commit v2 on v1

v2 whole, which is shorter than its diff:
```python
import jax
import jax.numpy as jnp
import numpy as np
from jax import lax
from jax.experimental import pallas as pl
from jax.experimental.pallas import tpu as pltpu
from jax.sharding import PartitionSpec as P

HEADS = 16
HEAD_DIM = 64
ROT = 16
GROUP = 64
LENGTH = 2048
WIDTH = 1024
FF = 2816
FF_LOCAL = 176
BLOCK = 256
SEQ = 16
ROWS = 8
HERE = 128
epsilon = 1e-05
f32 = jnp.float32
bf16 = jnp.bfloat16
SMEM = pl.BlockSpec(memory_space=pltpu.SMEM)
VMEM = pl.BlockSpec(memory_space=pltpu.VMEM)
ANY = pl.BlockSpec(memory_space=pl.ANY)


def dot_nn(a, b):
    return lax.dot_general(a, b, (((1,), (0,)), ((), ())), preferred_element_type=f32)


def dot_nt(a, b):
    return lax.dot_general(a, b, (((1,), (1,)), ((), ())), preferred_element_type=f32)


def dot_tn(a, b):
    return lax.dot_general(a, b, (((0,), (0,)), ((), ())), preferred_element_type=f32)


def dot_tt(a, b):
    return lax.dot_general(a, b, (((0,), (1,)), ((), ())), preferred_element_type=f32)


def params(mib):
    return pltpu.CompilerParams(vmem_limit_bytes=mib * 1024 * 1024)


def cost(gflop, mib, exps=0):
    return pl.CostEstimate(
        flops=int(gflop * 1e9), bytes_accessed=int(mib * 2**20), transcendentals=int(exps)
    )


def normalise(rows):
    rows = rows.astype(f32)
    mean = jnp.mean(rows, 1, keepdims=True)
    centred = rows - mean
    inv_std = lax.rsqrt(jnp.mean(centred * centred, 1, keepdims=True) + epsilon)
    return centred * inv_std, inv_std


def gated(gate, up, grad_act):
    sig = 1.0 / (1.0 + jnp.exp(-gate))
    silu = gate * sig
    grad_g = grad_act * up * (sig * (1.0 + gate - silu))
    grad_u = grad_act * silu
    return (silu * up).astype(bf16), grad_g.astype(bf16), grad_u.astype(bf16)


def rotary_tables():
    half = ROT // 2
    lane = np.arange(2 * HEAD_DIM) % HEAD_DIM
    frequency = np.where(lane < ROT, 10000.0 ** (-(lane % half) * (2.0 / ROT)), 0.0)
    groups = np.arange(LENGTH // GROUP)[:, None] * GROUP * frequency
    inside = np.arange(GROUP)[:, None] * frequency
    parts = (np.cos(groups), np.sin(groups), np.cos(inside), np.sin(inside))
    return jnp.asarray(np.concatenate(parts), f32)


def group_rotation(table, group):
    count = LENGTH // GROUP
    cos_g, sin_g = table[pl.ds(group, 1), :], table[pl.ds(group + count, 1), :]
    cos_i = table[2 * count : 2 * count + GROUP, :]
    sin_i = table[2 * count + GROUP :, :]
    return cos_g * cos_i - sin_g * sin_i, sin_g * cos_i + cos_g * sin_i


def own_kernel(x, dy, gain, bias, wg_in, wu_in, wd_in, out, grad, wg, wu, wd, sems):
    groups = ((0, 512), (512, 1280), (1280, 2048), (2048, 2816))
    copies = []
    for i, (lo, hi) in enumerate(groups):
        part = slice(lo, hi)
        pairs = ((wg_in.at[:, part], wg.at[:, part]), (wu_in.at[:, part], wu.at[:, part]))
        pairs += ((wd_in.at[part, :], wd.at[part, :]),)
        copies.append([pltpu.make_async_copy(*pair, sems.at[j, i]) for j, pair in enumerate(pairs)])
        for copy in copies[i]:
            copy.start()
    unit, _ = normalise(x[...])
    hid = (unit * gain[...] + bias[...]).astype(bf16)
    for i, (lo, hi) in enumerate(groups):
        for copy in copies[i]:
            copy.wait()
        part = slice(lo, hi)
        gate, up = dot_nn(hid, wg[:, part]), dot_nn(hid, wu[:, part])
        act, grad_g, grad_u = gated(gate, up, dot_nt(dy[...], wd[part, :]))
        more = dot_nt(grad_g, wg[:, part]) + dot_nt(grad_u, wu[:, part])
        out[...] = (x[...].astype(f32) if i == 0 else out[...]) + dot_nn(act, wd[part, :])
        grad[...] = more if i == 0 else grad[...] + more


def own_rows(x, dy, gain, bias, w_gate, w_up, w_down):
    return pl.pallas_call(
        own_kernel,
        out_shape=[jax.ShapeDtypeStruct((HERE, WIDTH), f32)] * 2,
        in_specs=[VMEM] * 4 + [ANY] * 3,
        out_specs=[VMEM] * 2,
        scratch_shapes=[
            pltpu.VMEM((WIDTH, FF), bf16),
            pltpu.VMEM((WIDTH, FF), bf16),
            pltpu.VMEM((FF, WIDTH), bf16),
            pltpu.SemaphoreType.DMA((3, 4)),
        ],
        compiler_params=params(60),
        cost_estimate=cost(4.5, 18),
        name="own_rows",
    )(x, dy, gain, bias, w_gate, w_up, w_down)


def heads_kernel(
    slot, order, x, dy, w_q, w_k, w_v, w_o, b_q, b_k, b_v, gain, bias,
    table, out, hid, cosine, sine,
):
    lanes = 2 * HEAD_DIM
    lane = lax.broadcasted_iota(jnp.int32, (1, lanes), 1)
    low = lane % HEAD_DIM < ROT // 2
    scale = jnp.where(lane < HEAD_DIM, HEAD_DIM**-0.5, 1.0)

    @pl.when(pl.program_id(0) == 0)
    def _():
        unit, _ = normalise(x[...])
        hid[...] = (unit * gain[...] + bias[...]).astype(bf16)
        for g in range(HERE // GROUP):
            rows = slice(g * GROUP, (g + 1) * GROUP)
            group = order[slot[0] * (HERE // GROUP) + g]
            cosine[rows, :], sine[rows, :] = group_rotation(table, group)

    q = dot_nn(hid[...], w_q[...]) + b_q[...]
    k = dot_nn(hid[...], w_k[...]) + b_k[...]
    v = dot_nn(hid[...], w_v[...]) + b_v[...]
    grad_att = dot_nt(dy[...], w_o[...])
    for h in range(BLOCK // HEAD_DIM):
        part = slice(h * HEAD_DIM, (h + 1) * HEAD_DIM)
        raw = jnp.concatenate([q[:, part], k[:, part]], 1)
        before, after = pltpu.roll(raw, ROT // 2, 1), pltpu.roll(raw, lanes - ROT // 2, 1)
        turned = (raw * cosine[...] + jnp.where(low, -after, before) * sine[...]) * scale
        rows = slice(h * HERE, (h + 1) * HERE)
        out[rows, :lanes] = turned.astype(bf16)
        out[rows, lanes:] = jnp.concatenate([v[:, part], grad_att[:, part]], 1).astype(bf16)


def own_heads(slot, order, x, dy, w_qkv, w_out, b_qkv, gain, bias, table):
    fixed = lambda shape: pl.BlockSpec(shape, lambda j: (0,) * len(shape))
    own, vector = fixed((HERE, WIDTH)), fixed((1, WIDTH))
    steps = WIDTH // BLOCK

    def part(rows, i):
        return pl.BlockSpec((rows, BLOCK), lambda j: (0, i * steps + j))

    return pl.pallas_call(
        heads_kernel,
        grid=(steps,),
        out_shape=jax.ShapeDtypeStruct((LENGTH, 4 * HEAD_DIM), bf16),
        in_specs=[SMEM] * 2
        + [own, own, part(WIDTH, 0), part(WIDTH, 1), part(WIDTH, 2)]
        + [pl.BlockSpec((BLOCK, WIDTH), lambda j: (j, 0)), part(1, 0), part(1, 1), part(1, 2)]
        + [vector, vector, fixed(table.shape)],
        out_specs=pl.BlockSpec((4 * HERE, 4 * HEAD_DIM), lambda j: (j, 0)),
        scratch_shapes=[
            pltpu.VMEM((HERE, WIDTH), bf16),
            pltpu.VMEM((HERE, 2 * HEAD_DIM), f32),
            pltpu.VMEM((HERE, 2 * HEAD_DIM), f32),
        ],
        compiler_params=params(60),
        cost_estimate=cost(1.1, 9),
        name="own_heads",
    )(slot, order, x, dy, w_qkv, w_qkv, w_qkv, w_out, b_qkv, b_qkv, b_qkv, gain, bias, table)


def attention_kernel(*refs):
    order, packed, table, out_ref, rows_in, cols_in, cols, turn = refs[-8:]
    groups = LENGTH // GROUP
    for g in range(groups):
        at = pl.multiple_of(order[g] * GROUP, GROUP)
        rows_in[pl.ds(at, GROUP), :] = packed[g * GROUP : (g + 1) * GROUP, :]
    cols_in[...] = rows_in[...].T
    k = rows_in[:, HEAD_DIM : 2 * HEAD_DIM]
    v = rows_in[:, 2 * HEAD_DIM : 3 * HEAD_DIM]
    q_t, k_t, v_t, do_t = (cols_in.at[i * HEAD_DIM : (i + 1) * HEAD_DIM, :] for i in range(4))
    dq_t, dk_t, dv_t, att_t = (cols.at[i * HEAD_DIM : (i + 1) * HEAD_DIM, :] for i in range(4))
    row = lax.broadcasted_iota(jnp.int32, (BLOCK, BLOCK), 0)
    col = lax.broadcasted_iota(jnp.int32, (BLOCK, BLOCK), 1)
    visible = row <= col
    def products(i):
        here, n = slice(i * BLOCK, (i + 1) * BLOCK), (i + 1) * BLOCK
        return dot_nn(k[:n], q_t[:, here]), dot_nn(v[:n], do_t[:, here])

    def softmax(i, scores):
        lo = i * BLOCK
        last = jnp.where(visible, scores[lo:], -1e30)
        scores = last if i == 0 else jnp.concatenate([scores[:lo], last], 0)
        top = jnp.max(scores, 0, keepdims=True)
        weights = jnp.exp(scores - top)
        inverse = 1.0 / jnp.sum(weights, 0, keepdims=True)
        return weights, weights.astype(bf16), inverse

    order_of = list(reversed(range(LENGTH // BLOCK)))
    ahead = products(order_of[0])
    for j, i in enumerate(order_of):
        lo, n = i * BLOCK, (i + 1) * BLOCK
        here, seen = slice(lo, n), slice(0, n)
        scores, grad_p = ahead
        if j + 1 < len(order_of):
            ahead = products(order_of[j + 1])
        weights, weights_b, inverse = softmax(i, scores)
        att = dot_nn(v_t[:, seen], weights_b) * inverse
        do_f = do_t[:, here].astype(f32)
        delta = jnp.sum(weights * grad_p, 0, keepdims=True) * inverse
        grad_s = (weights * (grad_p - delta)).astype(bf16)
        dv = dot_nt((do_f * inverse).astype(bf16), weights_b)
        att_t[:, here] = att
        dq_t[:, here] = dot_nn(k_t[:, seen], grad_s) * (inverse * HEAD_DIM**-0.5)
        dk = dot_nt((q_t[:, here].astype(f32) * inverse).astype(bf16), grad_s)
        if n == LENGTH:
            dk_t[...], dv_t[...] = dk, dv
        else:
            dk_t[:, seen] += dk
            dv_t[:, seen] += dv
    half = ROT // 2
    cosine, sine = table[:half, :], table[half:, :]
    for part in (dq_t, dk_t):
        first, second = part[:half, :], part[half:ROT, :]
        part[:half, :] = first * cosine + second * sine
        part[half:ROT, :] = second * cosine - first * sine
    turn[...] = cols[...].T.astype(bf16)
    for g in range(groups):
        at = pl.multiple_of(order[g] * GROUP, GROUP)
        out_ref[g * GROUP : (g + 1) * GROUP, :] = turn[pl.ds(at, GROUP), :]


def position_table():
    half = ROT // 2
    angles = 10000.0 ** (-np.arange(half)[:, None] * (2.0 / ROT)) * np.arange(LENGTH)
    return jnp.asarray(np.concatenate([np.cos(angles), np.sin(angles)]), f32)


def attention(order, packed, first=()):
    size = 4 * HEAD_DIM
    return pl.pallas_call(
        attention_kernel,
        out_shape=jax.ShapeDtypeStruct((LENGTH, size), bf16),
        in_specs=[ANY] * len(first) + [SMEM] + [VMEM] * 2,
        out_specs=VMEM,
        scratch_shapes=[
            pltpu.VMEM((LENGTH, size), bf16),
            pltpu.VMEM((size, LENGTH), bf16),
            pltpu.VMEM((size, LENGTH), f32),
            pltpu.VMEM((LENGTH, size), bf16),
        ],
        compiler_params=params(60),
        cost_estimate=cost(15, 8, LENGTH * LENGTH // 2),
        name="attention",
    )(*first, order, packed, position_table())


def cut_kernel(slot, w_qkv, w_gate, w_up, out_qkv, out_gu, wide_qkv, wide_gu, sems):
    here = slot[0]
    first = here * FF_LOCAL
    tile = jnp.minimum(first // 128, (FF - 384) // 128) * 128
    copies = []
    for i in range(3):
        lanes = pl.ds(pl.multiple_of(here // 2 * 128 + i * WIDTH, 128), 128)
        to = wide_qkv.at[:, i * 128 : (i + 1) * 128]
        copies.append(pltpu.make_async_copy(w_qkv.at[:, lanes], to, sems.at[i]))
    for i, source in enumerate((w_gate, w_up)):
        lanes = pl.ds(pl.multiple_of(tile, 128), 384)
        copies.append(pltpu.make_async_copy(source.at[:, lanes], wide_gu.at[i], sems.at[3 + i]))
    for copy in copies:
        copy.start()
    row = lax.broadcasted_iota(jnp.int32, (384, 256), 0)
    lane = lax.broadcasted_iota(jnp.int32, (384, 256), 1)
    source = lane // HEAD_DIM * 128 + here % 2 * HEAD_DIM + lane % HEAD_DIM
    pick_qkv = (row == source).astype(bf16)[:, : 3 * HEAD_DIM]
    pick_gu = (row == lane + (first - tile)).astype(bf16)[:, :FF_LOCAL]
    for copy in copies:
        copy.wait()
    out_qkv[...] = dot_tt(pick_qkv, wide_qkv[...]).astype(bf16)
    out_gu[:FF_LOCAL, :] = dot_tt(pick_gu, wide_gu[0]).astype(bf16)
    out_gu[FF_LOCAL:, :] = dot_tt(pick_gu, wide_gu[1]).astype(bf16)


def cut_weights(slot, w_qkv, w_gate, w_up):
    return pl.pallas_call(
        cut_kernel,
        out_shape=[
            jax.ShapeDtypeStruct((3 * HEAD_DIM, WIDTH), bf16),
            jax.ShapeDtypeStruct((2 * FF_LOCAL, WIDTH), bf16),
        ],
        in_specs=[SMEM] + [ANY] * 3,
        out_specs=[VMEM] * 2,
        scratch_shapes=[
            pltpu.VMEM((WIDTH, 384), bf16),
            pltpu.VMEM((2, WIDTH, 384), bf16),
            pltpu.SemaphoreType.DMA((5,)),
        ],
        compiler_params=params(60),
        cost_estimate=cost(0.001, 0.001),
        name="cut_weights",
    )(slot, w_qkv, w_gate, w_up)


def column(row):
    return jnp.broadcast_to(row, (8, row.shape[1])).T[:, :1]


def piece_copies(pieces, inputs, x_all, dy, sems):
    return [
        pltpu.make_async_copy(
            inputs[ref].at[pl.ds(which * HERE, HERE), :],
            (x_all, dy)[which].at[pl.ds(to * HERE, HERE), :],
            sems.at[i],
        )
        for i, (which, ref, to) in enumerate(pieces)
    ]


def down_copy(slot, source, to, sem):
    rows = pl.ds(pl.multiple_of(slot[0] * FF_LOCAL, 16), FF_LOCAL)
    return pltpu.make_async_copy(source.at[rows, :], to, sem)


def gate_blocks(count, x_all, dy, unit, w_gu, w_d, gain, bias, keep):
    total = 0.0
    for i in range(count):
        rows = slice(i * BLOCK, (i + 1) * BLOCK)
        unit_f, _ = normalise(x_all[rows, :])
        hid = (unit_f * gain[...] + bias[...]).astype(bf16)
        unit[rows, :] = unit_f.astype(bf16)
        gu = dot_nt(w_gu[...], hid)
        act, grad_g, grad_u = gated(gu[:FF_LOCAL], gu[FF_LOCAL:], dot_nt(w_d[...], dy[rows, :]))
        grads = jnp.concatenate([grad_g, grad_u], 0)
        keep(i, act, grads)
        total += jnp.sum(grads.astype(f32), 1, keepdims=True)
    return total


def first_kernel(pieces, n_refs, slot, *refs):
    inputs, refs = refs[:n_refs], refs[n_refs:]
    w_gu, w_d_in, gain, bias, unit, acts, grads, sums, x_all, dy, w_d, sems, sem = refs
    copies = piece_copies(pieces, inputs, x_all, dy, sems)
    copies.append(down_copy(slot, w_d_in, w_d, sem))
    for copy in copies:
        copy.start()
    for copy in copies:
        copy.wait()

    def keep(i, act, grad):
        acts[:, i * BLOCK : (i + 1) * BLOCK] = act
        grads[:, i * BLOCK : (i + 1) * BLOCK] = grad

    total = gate_blocks(x_all.shape[0] // BLOCK, x_all, dy, unit, w_gu, w_d, gain, bias, keep)
    sums[...] = jnp.broadcast_to(total, sums.shape)


def first_half(slot, arrays, pieces, w_gu, w_d, gain, bias):
    half = LENGTH // 2
    return pl.pallas_call(
        lambda *refs: first_kernel(pieces, len(arrays), *refs),
        out_shape=[
            jax.ShapeDtypeStruct((half, WIDTH), bf16),
            jax.ShapeDtypeStruct((FF_LOCAL, half), bf16),
            jax.ShapeDtypeStruct((2 * FF_LOCAL, half), bf16),
            jax.ShapeDtypeStruct((2 * FF_LOCAL, 128), f32),
        ],
        in_specs=[SMEM] + [ANY] * len(arrays) + [VMEM] + [ANY] + [VMEM] * 2,
        out_specs=[VMEM] * 4,
        scratch_shapes=[
            pltpu.VMEM((half, WIDTH), bf16),
            pltpu.VMEM((half, WIDTH), bf16),
            pltpu.VMEM((FF_LOCAL, WIDTH), bf16),
            pltpu.SemaphoreType.DMA((len(pieces),)),
            pltpu.SemaphoreType.DMA,
        ],
        compiler_params=params(60),
        cost_estimate=cost(0.001, 0.001),
        name="first_half",
    )(slot, *arrays, w_gu, w_d, gain, bias)


def weights_kernel(pieces, n_refs, slot, *refs):
    inputs, refs = refs[:n_refs], refs[n_refs:]
    heads_in, w_qkv, w_gu, w_d_in, gain, bias = refs[:6]
    unit_in, acts_in, grads_in, sums, block_out = refs[6:11]
    x_all, dy, unit, heads, left, right, stage, w_d, block = refs[11:20]
    piece_sems, head_sems, out_sems, first_sems, weight_sem = refs[20:]
    hidden, both = FF_LOCAL, 2 * FF_LOCAL
    here = slot[0]
    half = LENGTH // 2
    late = (dy.at[half:, :], unit.at[half:, :])
    copies = piece_copies(pieces, inputs, x_all, dy, piece_sems)
    now = [copy for copy, piece in zip(copies, pieces) if piece[2] >= SEQ // 2]
    now.append(down_copy(slot, w_d_in, w_d, weight_sem))
    later = [copy for copy, piece in zip(copies, pieces) if piece[0] and piece[2] < SEQ // 2]
    later.append(pltpu.make_async_copy(unit_in, unit.at[:half, :], first_sems.at[0]))
    later.append(pltpu.make_async_copy(acts_in, right.at[:hidden, :half], first_sems.at[1]))
    later.append(pltpu.make_async_copy(grads_in, left.at[:both, :half], first_sems.at[2]))
    for i in range(SEQ):
        rows = pl.ds(pl.multiple_of(slot[i] * HERE, HERE), HERE)
        to = heads.at[i * HERE : (i + 1) * HERE, :]
        later.append(pltpu.make_async_copy(heads_in.at[rows, :], to, head_sems.at[i]))
    for copy in now + later:
        copy.start()
    for copy in now:
        copy.wait()

    def keep(i, act, grad):
        at = slice(half + i * BLOCK, half + (i + 1) * BLOCK)
        right[:hidden, at] = act
        left[:both, at] = grad

    total = gate_blocks(half // BLOCK, x_all.at[half:, :], *late, w_gu, w_d, gain, bias, keep)
    total += sums[:, :1]
    for copy in later:
        copy.wait()
    heads_t = heads[...].T
    left[both:, :] = heads_t[: 3 * HEAD_DIM]
    right[hidden:, :] = heads_t[3 * HEAD_DIM :]
    total_h = jnp.sum(heads_t[: 3 * HEAD_DIM].astype(f32), 1, keepdims=True)
    inner = dot_nn(left[...], unit[...])
    total = jnp.concatenate([total, total_h], 0)
    wide = jnp.concatenate([w_gu[...], w_qkv[...]], 0).astype(f32)
    terms = inner * gain[...] + bias[...] * total
    gain_part = jnp.sum(inner * wide, 0, keepdims=True)
    bias_part = jnp.sum(wide * total, 0, keepdims=True)
    at_row = lax.broadcasted_iota(jnp.int32, (192, WIDTH), 0)
    column_at = at_row // HEAD_DIM * WIDTH + here * HEAD_DIM + at_row % HEAD_DIM
    mine = column_at // 24 * 8 == lax.broadcasted_iota(jnp.int32, (192, WIDTH), 1)
    at_lane = lax.broadcasted_iota(jnp.int32, (32, 192), 1)
    column_at = at_lane // HEAD_DIM * WIDTH + here * HEAD_DIM + at_lane % HEAD_DIM
    pick = (column_at % 24 + 2 == lax.broadcasted_iota(jnp.int32, (32, 192), 0)).astype(bf16)
    extra = dot_nn(pick, jnp.where(mine, total_h, 0.0).astype(bf16))
    row32 = lax.broadcasted_iota(jnp.int32, (32, WIDTH), 0)
    extra += jnp.where(row32 == 0, gain_part, jnp.where(row32 == 1, bias_part, 0.0))
    stage[...] = jnp.concatenate([terms[:both], extra, terms[both:]], 0).T
    products = dot_nn(right[...], dy[...])
    down_all, out_all = products[:hidden], products[hidden:]
    outs = []

    def two(s, lanes):
        first, second = (s * ROWS + r) * 8, ((s + 1) * ROWS + r) * 8
        return jnp.concatenate([stage[first : first + 8, lanes], stage[second : second + 8, lanes]], 0)

    for r in range(ROWS):
        for s in range(0, SEQ, 2):
            for i in range(4):
                lanes = slice(i * 128, (i + 1) * 128)
                block[r, i * HERE + s * 8 : i * HERE + s * 8 + 16, :] = two(s, lanes).astype(bf16)
        for s in range(0, SEQ // 2, 2):
            lanes = slice(512, 576)
            block[r, 512 + s * 8 : 528 + s * 8, :] = jnp.concatenate(
                [two(s, lanes), two(s + 8, lanes)], 1
            ).astype(bf16)
        last = jnp.concatenate(
            [out_all[r * 8 : r * 8 + 8], down_all[r * 22 : (r + 1) * 22], jnp.zeros((2, WIDTH), f32)],
            0,
        ).astype(bf16)
        for i in range(8):
            block[r, 576 + i * 32 : 608 + i * 32, :] = last[:, i * 128 : (i + 1) * 128]
        outs.append(pltpu.make_async_copy(block.at[r], block_out.at[r], out_sems.at[r]))
        outs[r].start()
    for copy in outs:
        copy.wait()


def weight_grads(slot, arrays, pieces, heads, w_qkv, w_gu, w_d, gain, bias, first):
    big = (LENGTH, WIDTH)
    return pl.pallas_call(
        lambda *refs: weights_kernel(pieces, len(arrays), *refs),
        out_shape=jax.ShapeDtypeStruct((ROWS, 832, 128), bf16),
        in_specs=[SMEM] + [ANY] * (len(arrays) + 1) + [VMEM] * 2 + [ANY] + [VMEM] * 2 + [ANY] * 3 + [VMEM],
        out_specs=ANY,
        scratch_shapes=[pltpu.VMEM(big, bf16)] * 3
        + [
            pltpu.VMEM((LENGTH, 4 * HEAD_DIM), bf16),
            pltpu.VMEM((2 * FF_LOCAL + 3 * HEAD_DIM, LENGTH), bf16),
            pltpu.VMEM((FF_LOCAL + HEAD_DIM, LENGTH), bf16),
            pltpu.VMEM((WIDTH, 576), f32),
            pltpu.VMEM((FF_LOCAL, WIDTH), bf16),
            pltpu.VMEM((ROWS, 832, 128), bf16),
            pltpu.SemaphoreType.DMA((len(pieces),)),
            pltpu.SemaphoreType.DMA((SEQ,)),
            pltpu.SemaphoreType.DMA((ROWS,)),
            pltpu.SemaphoreType.DMA((3,)),
            pltpu.SemaphoreType.DMA,
        ],
        compiler_params=params(60),
        cost_estimate=cost(8, 20),
        name="weight_grads",
    )(slot, *arrays, heads, w_qkv, w_gu, w_d, gain, bias, *first)


def final_kernel(heads, x, dy, part, grad, gain, w_out, w_qkv, out, input_grad, att, rows, total):
    step = pl.program_id(0)

    @pl.when(step == 0)
    def _():
        for h in range(HEADS):
            here = heads[h * HERE : (h + 1) * HERE, :]
            at = h * HEAD_DIM
            for i in range(3):
                lo = i * WIDTH + at
                rows[:, lo : lo + HEAD_DIM] = here[:, i * HEAD_DIM : (i + 1) * HEAD_DIM]
            att[:, at : at + HEAD_DIM] = here[:, 3 * HEAD_DIM :]

    columns = pl.ds(pl.multiple_of(step * BLOCK, BLOCK), BLOCK)
    out[:, columns] = (part[:, columns] + dot_nn(att[...], w_out[...])).astype(bf16)
    total[:, columns] = grad[:, columns] + dot_nt(rows[...], w_qkv[...])

    @pl.when(step == pl.num_programs(0) - 1)
    def _():
        unit, inv_std = normalise(x[...])
        grad_unit = total[...] * gain[...]
        grad_norm = inv_std * (
            grad_unit
            - jnp.mean(grad_unit, 1, keepdims=True)
            - unit * jnp.mean(grad_unit * unit, 1, keepdims=True)
        )
        input_grad[...] = (dy[...].astype(f32) + grad_norm).astype(bf16)


def final_rows(heads, x, dy, part, grad, gain, w_out, w_qkv):
    fixed = lambda shape: pl.BlockSpec(shape, lambda j: (0,) * len(shape))
    own = fixed((HERE, WIDTH))
    return pl.pallas_call(
        final_kernel,
        grid=(WIDTH // BLOCK,),
        out_shape=[jax.ShapeDtypeStruct((HERE, WIDTH), bf16)] * 2,
        in_specs=[fixed((LENGTH, 256)), own, own, own, own, fixed((1, WIDTH))]
        + [pl.BlockSpec((WIDTH, BLOCK), lambda j: (0, j))]
        + [pl.BlockSpec((BLOCK, 3 * WIDTH), lambda j: (j, 0))],
        out_specs=[own, own],
        scratch_shapes=[
            pltpu.VMEM((HERE, WIDTH), bf16),
            pltpu.VMEM((HERE, 3 * WIDTH), bf16),
            pltpu.VMEM((HERE, WIDTH), f32),
        ],
        compiler_params=params(60),
        cost_estimate=cost(1.1, 10),
        name="final_rows",
    )(heads, x, dy, part, grad, gain, w_out, w_qkv)


def sum_kernel(got, send, down, out):
    total = got[0].astype(f32)
    for r in range(1, ROWS):
        total += got[r].astype(f32)
    for i in range(4):
        send[:, i * 128 : (i + 1) * 128] = total[i * HERE : (i + 1) * HERE].astype(bf16)
    left = jnp.concatenate([total[512:576, :64], total[512:576, 64:]], 0)
    send[:, 512:] = jnp.concatenate([left, jnp.zeros((HERE, 64), f32)], 1).astype(bf16)
    for i in range(8):
        lanes = slice(i * 128, (i + 1) * 128)
        out[:, lanes] = total[576 + i * 32 : 584 + i * 32]
        down[:, lanes] = total[584 + i * 32 : 606 + i * 32]


def sum_rows(got):
    return pl.pallas_call(
        sum_kernel,
        out_shape=[
            jax.ShapeDtypeStruct((HERE, 640), bf16),
            jax.ShapeDtypeStruct((22, WIDTH), f32),
            jax.ShapeDtypeStruct((8, WIDTH), f32),
        ],
        in_specs=[VMEM],
        out_specs=[VMEM] * 3,
        compiler_params=params(16),
        cost_estimate=cost(0.001, 2),
        name="sum_rows",
    )(got)


def layout_kernel(mine, qkv, gate, up, vectors, sums):
    more = jnp.zeros((8, 128), f32)
    for s in range(SEQ):
        here = mine[s * 8 : (s + 1) * 8, :].astype(f32)
        gate[:, s * FF_LOCAL : (s + 1) * FF_LOCAL] = here[:, :FF_LOCAL]
        up[:, s * FF_LOCAL : (s + 1) * FF_LOCAL] = here[:, FF_LOCAL : 2 * FF_LOCAL]
        for i in range(3):
            lo = i * WIDTH + s * HEAD_DIM
            qkv[:, lo : lo + HEAD_DIM] = here[:, 384 + i * HEAD_DIM : 384 + (i + 1) * HEAD_DIM]
        more += here[:, 256:384]
    vectors[...] = more.T[96:98, :]
    sums[...] = more[0:1, 98:122]


def last_layout(mine):
    return pl.pallas_call(
        layout_kernel,
        out_shape=[
            jax.ShapeDtypeStruct((8, 3 * WIDTH), f32),
            jax.ShapeDtypeStruct((8, FF), f32),
            jax.ShapeDtypeStruct((8, FF), f32),
            jax.ShapeDtypeStruct((2, 8), f32),
            jax.ShapeDtypeStruct((1, 24), f32),
        ],
        in_specs=[VMEM],
        out_specs=[VMEM] * 5,
        compiler_params=params(16),
        cost_estimate=cost(0.001, 1),
        name="last_layout",
    )(mine)


PLACES = [(0, 0), (0, -1), (0, 1), (1, 0), (0, 2), (1, 1), (1, -1), (1, 2)]
CORE = [(i, i ^ 1) for i in range(SEQ)]
PAIR = [(i, i ^ 2) for i in range(SEQ)]
UP = [(i, (i + 4) % SEQ) for i in range(SEQ)]
DOWN = [(i, (i + 12) % SEQ) for i in range(SEQ)]
DOWN_PAIR = [(i, (i + 12) % SEQ ^ 2) for i in range(SEQ)]


def send(value, to):
    return lax.ppermute(value, "seq", to)


def gather(x, dy, exchange, after):
    own = jnp.concatenate([x, dy], 0)
    below = send(own, UP)
    above = send(own, DOWN)
    pair = send(own, PAIR)
    late = exchange((below, above, pair))
    far = send(below, UP)
    across_below = send(below, PAIR)
    across_above = send(pair, DOWN)
    opposite = send(above, DOWN_PAIR)
    arrays = [own, below, above, pair, far, across_above, across_below, opposite]
    first = [both for a in arrays[:4] for both in (a, send(a, CORE))]
    late, rest = after(late, first, arrays[4:])
    return first, [both for a in rest for both in (a, send(a, CORE))], late


def pieces_of(count):
    return [(which, i, i) for i in range(count) for which in range(2)]


def shards(x, dy, order, ln_gain, ln_bias, w_qkv, b_qkv, w_out, w_gate, w_up, w_down):
    x, dy = x[0], dy[0]
    s = lax.axis_index("seq")
    slot = jnp.stack(
        [
            ((s // 4 + up) % 4) * 4 + ((s // 2 % 2) ^ across) * 2 + (s % 2 ^ core)
            for across, up in PLACES
            for core in range(2)
        ]
    ).astype(jnp.int32)
    gain, bias = ln_gain[None, :], ln_bias[None, :]

    table = rotary_tables()
    packed = own_heads(slot, order, x, dy, w_qkv, w_out, b_qkv[None, :], gain, bias, table)
    w_qkv_s, w_gu_s = cut_weights(slot, w_qkv, w_gate, w_up)

    def exchange(first):
        ready, _ = lax.optimization_barrier((packed, (first, w_gu_s)))
        return lax.all_to_all(ready, "seq", 0, 0, tiled=True)

    def attend(packed_here, early, arrays):
        first = first_half(
            slot, early, pieces_of(len(early)), w_gu_s, w_down, gain, bias
        )
        heads = attention(order, packed_here, first)
        (heads, first), arrays = lax.optimization_barrier(((heads, first), arrays))
        return (heads, first), arrays

    early, arrays, (heads, first) = gather(x, dy, exchange, attend)
    heads_here = lax.all_to_all(heads, "seq", 0, 0, tiled=True)
    arrays = early + arrays
    block = weight_grads(
        slot, arrays, pieces_of(SEQ), heads, w_qkv_s, w_gu_s, w_down, gain, bias, first
    )
    block, heads_here = lax.optimization_barrier((block, heads_here))
    got = lax.all_to_all(block, "rows", 0, 0, tiled=True)
    x_late, _ = lax.optimization_barrier((x, heads_here))
    part, grad = own_rows(x_late, dy, gain, bias, w_gate, w_up, w_down)
    output, input_grad = final_rows(heads_here, x, dy, part, grad, gain, w_out, w_qkv)
    got, output, input_grad = lax.optimization_barrier((got, output, input_grad))
    outgoing, o_down, o_out = sum_rows(got)
    mine = lax.all_to_all(outgoing, "seq", 0, 0, tiled=True)
    o_qkv, o_gate, o_up, vectors, sums = last_layout(mine)
    return (
        output[None],
        input_grad[None],
        o_qkv,
        o_out,
        o_gate,
        o_up,
        o_down,
        sums[0],
        vectors[0],
        vectors[1],
    )


def solution(mesh):
    rows = P("rows", "seq", None)
    both = P(("seq", "rows"), None)
    flat = P(("seq", "rows"))
    return jax.shard_map(
        shards,
        mesh=mesh,
        in_specs=(rows, rows) + (P(),) * 9,
        out_specs=(rows, rows, both, both, both, both, both, flat, flat, flat),
        check_vma=False,
    )
```

time: 139 us -> 126 us (0.906)
  waiting for transfers between devices: 20.1 us -> 13.4 us
  Pallas kernels: 70.1 us -> 64.6 us
  blocking collectives: 12.2 us -> 10.8 us
    all_to_all x1, waiting for transfers between devices: 16.8 us -> 1.8 us  [shards(): got = lax.all_to_all(block, 'rows', 0, 0, tiled=True)]
    ppermute x15, waiting for transfers between devices: 3.3 us -> 9.49 us  [send(): return lax.ppermute(value, 'seq', to)]
    pallas_call x1, Pallas kernels: 15.8 us -> 10.9 us  [attention(): pl.pallas_call(attention_kernel, out_shape=jax.ShapeDtypeStruct((LENGTH,...]
    pallas_call x1, Pallas kernels: 17.1 us -> 13.2 us  [weight_grads(): pl.pallas_call(lambda *refs: weights_kernel(pieces, len(arrays), *refs),...]
    pallas_call x2 -> x3, Pallas kernels: 20.5 us -> 23.6 us  [the longest x1 12 us: own_rows(): pl.pallas_call(own_kernel, out_shape=[jax.ShapeDtypeStruct((HERE, WIDTH),...]
    all_to_all x1, waiting for transfers between devices: 0.01 us -> 1.47 us  [shards(): heads_here = lax.all_to_all(heads, 'seq', 0, 0, tiled=True)]
    all_to_all x1, starting transfers between devices: 6.47 us -> 5.07 us  [exchange(): return lax.all_to_all(ready, 'seq', 0, 0, tiled=True)]
    all_to_all x1, blocking collectives: 12.2 us -> 10.8 us  [shards(): mine = lax.all_to_all(outgoing, 'seq', 0, 0, tiled=True)]
  transfers between devices with their start and end apart: 18 -> 18, of which waited for: 5 -> 4; matrix products, arithmetic and copies ran while one was open for 0% -> 1% of each run, Pallas kernels for 50% -> 50%
where the time goes in v2:
time: 126 us; the launch traced here: 125 us
  Pallas kernels  64.6 us (51%)
  starting transfers between devices  30.9 us (25%)
  waiting for transfers between devices  13.4 us (11%)
  blocking collectives  10.8 us (9%)
  local copies, waits for them, and re-layouts  3.31 us (3%)
    ppermute x15, starting transfers between devices, send(): return lax.ppermute(value, 'seq', to)  14.1 us
    pallas_call x1, Pallas kernels, weight_grads(): pl.pallas_call(lambda *refs: weights_kernel(pieces, len(arrays), *refs),...  13.2 us
    pallas_call x1, Pallas kernels, own_rows(): pl.pallas_call(own_kernel, out_shape=[jax.ShapeDtypeStruct((HERE, WIDTH),...  12 us
    pallas_call x1, Pallas kernels, attention(): pl.pallas_call(attention_kernel, out_shape=jax.ShapeDtypeStruct((LENGTH,...  10.9 us
    all_to_all x1, blocking collectives, shards(): mine = lax.all_to_all(outgoing, 'seq', 0, 0, tiled=True)  10.8 us
    ppermute x15, waiting for transfers between devices, send(): return lax.ppermute(value, 'seq', to)  9.49 us
    pallas_call x1, Pallas kernels, final_rows(): pl.pallas_call(final_kernel, grid=(WIDTH // BLOCK,), out_shape=[jax.Shape...  8.02 us
    pallas_call x1, Pallas kernels, first_half(): pl.pallas_call(lambda *refs: first_kernel(pieces, len(arrays), *refs), ou...  7.32 us
  transfers between devices with their start and end apart: 18, of which 4 were waited for; matrix products, arithmetic and copies ran while one was open for 1% of the time, Pallas kernels for 50%

profile of v2, /device:TPU:1, one launch (start us, length us, event | category | flops | bytes accessed | tf_op | source)
XLA Modules:
  0.0 124.9 jit_solution(17866775307823943413)
XLA Ops:
  0.6 1.1 pad_maximum_fusion.refs_1_
  1.7 2.2 %collective-permute-start.1 = (bf16[256,1024]{1,0:T(8,128)(2,1)S(1)}, bf16[256,1024]{1,0:T(8,128)(2,1)S(1)}, u32[]{:S(2)}, u32[]{:S(2)}) collective-permute-start(bf16[256,1024]{1,0:T(8,128)(2,1)S(1)} %pad_maximum_fusion.refs_1_), channel_id=1, source_target_pairs={{0,32},{8,40},{16,48},{24,56},{32,64},{40,72},{48,80},{56,88},{64,... | collective-permute-start | bytes 1572872 | tf_op jit(solution)/shard_map/ppermute | solution.py:634
  3.9 1.5 %collective-permute-start.3 = (bf16[256,1024]{1,0:T(8,128)(2,1)S(1)}, bf16[256,1024]{1,0:T(8,128)(2,1)S(1)}, u32[]{:S(2)}, u32[]{:S(2)}) collective-permute-start(bf16[256,1024]{1,0:T(8,128)(2,1)S(1)} %pad_maximum_fusion.refs_1_), channel_id=1, source_target_pairs={{0,96},{8,104},{16,112},{24,120},{32,0},{40,8},{48,16},{56,24},{64... | collective-permute-start | bytes 1572872 | tf_op jit(solution)/shard_map/ppermute | solution.py:634
  5.4 1.2 collective-permute-start.5
  6.6 0.7 stack.67.slot.refs_0_
  7.3 4.2 %cut_weights.1 = (bf16[192,1024]{1,0:T(8,128)(2,1)}, bf16[352,1024]{1,0:T(8,128)(2,1)}) custom-call(s32[16]{0:T(128)} %stack.67.slot.refs_0_, bf16[1024,3072]{1,0:T(8,128)(2,1)} %w_qkv.3, bf16[1024,2816]{1,0:T(8,128)(2,1)} %wg_in.1, bf16[1024,2816]{1,0:T(8,128)(2,1)} %wu_in.1), custom_call_target="tpu_custom_call" | custom-call | flops 1000000 | bytes 1048 | tf_op jit(solution)/shard_map/cut_weights/pallas_call | solution.py:303
  11.6 7.1 %own_heads.1 = bf16[2048,256]{1,0:T(8,128)(2,1)} custom-call(s32[16]{0:T(128)} %stack.67.slot.refs_0_, s32[32]{0:T(128)} %refs_4_.1, bf16[128,1024]{1,0:T(8,128)(2,1)} %bitcast.41, bf16[128,1024]{1,0:T(8,128)(2,1)} %bitcast.37, bf16[1024,3072]{1,0:T(8,128)(2,1)} %w_qkv.3, bf16[1024,3072]{1,0:T(8,128)(2,1)} %w_qkv.3, bf16[1024,3072]{1,0:T(8,128)(2,1)} %w_qkv.3, ...), custom_call_target="tpu_custom_call" | custom-call | flops 1100000000 | bytes 9437184 | tf_op jit(solution)/shard_map/own_heads/pallas_call | solution.py:170
  18.7 0.0 collective-permute-done.1.refs_3_
  18.8 0.0 collective-permute-done.5.refs_7_
  18.8 5.1 %all-to-all-start = ((bf16[16,128,256]{2,1,0:T(8,128)(2,1)}), bf16[16,128,256]{2,1,0:T(8,128)(2,1)S(1)}, u32[]{:S(2)}, u32[]{:S(2)}) async-start(bf16[16,128,256]{2,1,0:T(8,128)(2,1)} %bitcast.44), calls=%async_computation | async-start | bytes 2097152 | tf_op jit(solution)/shard_map/all_to_all | solution.py:675
  23.8 0.2 collective-permute-start
  24.0 0.4 collective-permute-start.2
  24.4 0.1 collective-permute-start.4
  24.5 0.4 collective-permute-start.6
  24.9 1.4 %collective-permute-start.7 = (bf16[256,1024]{1,0:T(8,128)(2,1)S(1)}, bf16[256,1024]{1,0:T(8,128)(2,1)}, u32[]{:S(2)}, u32[]{:S(2)}) collective-permute-start(bf16[256,1024]{1,0:T(8,128)(2,1)S(1)} %collective-permute-done.1.refs_3_), channel_id=1, source_target_pairs={{0,32},{8,40},{16,48},{24,56},{32,64},{40,72},{48,80},{56,88},{64,... | collective-permute-start | bytes 1572872 | tf_op jit(solution)/shard_map/ppermute | solution.py:634
  26.3 0.0 collective-permute-done.refs_2_
  26.3 1.2 collective-permute-start.9
  27.5 0.0 collective-permute-done.2.refs_4_
  27.5 3.3 %collective-permute-start.10 = (bf16[256,1024]{1,0:T(8,128)(2,1)S(1)}, bf16[256,1024]{1,0:T(8,128)(2,1)}, u32[]{:S(2)}, u32[]{:S(2)}) collective-permute-start(bf16[256,1024]{1,0:T(8,128)(2,1)S(1)} %collective-permute-done.3.refs_5_), channel_id=1, source_target_pairs={{0,112},{8,120},{16,96},{24,104},{32,16},{40,24},{48,0},{56,8},{64... | collective-permute-start | bytes 1572872 | tf_op jit(solution)/shard_map/ppermute | solution.py:634
  30.8 0.0 collective-permute-done.4.refs_6_
  30.8 0.8 collective-permute-start.8
  31.7 0.0 collective-permute-done.6.refs_8_
  31.7 7.3 %first_half.1 = (bf16[1024,1024]{1,0:T(8,128)(2,1)}, bf16[176,1024]{1,0:T(8,128)(2,1)}, bf16[352,1024]{1,0:T(8,128)(2,1)}, f32[352,128]{1,0:T(8,128)}) custom-call(s32[16]{0:T(128)} %stack.67.slot.refs_0_, bf16[256,1024]{1,0:T(8,128)(2,1)} %copy-done.1, bf16[256,1024]{1,0:T(8,128)(2,1)} %copy-done.6, bf16[256,1024]{1,0:T(8,128)(2,1)} %copy-done.3, ...), custom_call_target="tpu_custom_call" | custom-call | flops 1000000 | bytes 1048 | tf_op jit(solution)/shard_map/first_half/pallas_call | solution.py:377
  39.0 0.6 all-to-all-done
  39.7 1.0 copy-done.2
  40.6 10.9 %attention.1.refs_17_ = bf16[2048,256]{1,0:T(8,128)(2,1)} custom-call(bf16[1024,1024]{1,0:T(8,128)(2,1)} %get-tuple-element.56.refs_0_.refs_23_, bf16[176,1024]{1,0:T(8,128)(2,1)} %get-tuple-element.57.refs_1_.refs_24_, bf16[352,1024]{1,0:T(8,128)(2,1)} %get-tuple-element.58.refs_2_.refs_25_, f32[352,128]{1,0:T(8,128)} %get-tuple-element.59.refs_3_.refs_26_, ...), custom_call_target="tpu_custom_call" | custom-call | flops 15000000512 | bytes 8388608 | tf_op jit(solution)/shard_map/attention/pallas_call | solution.py:259
  51.6 0.0 collective-permute-done.7.refs_9_
  51.6 0.0 collective-permute-done.9.refs_13_
  51.6 9.4 %collective-permute-done.10.refs_15_ = bf16[256,1024]{1,0:T(8,128)(2,1)} collective-permute-done((bf16[256,1024]{1,0:T(8,128)(2,1)S(1)}, bf16[256,1024]{1,0:T(8,128)(2,1)}, u32[]{:S(2)}, u32[]{:S(2)}) %collective-permute-start.10) | collective-permute-done | bytes 524320 | tf_op jit(solution)/shard_map/ppermute | solution.py:634
  61.0 0.9 collective-permute-start.11
  61.9 0.0 collective-permute-start.12
  61.9 0.5 collective-permute-start.13
  62.4 0.0 collective-permute-start.14
  62.4 4.5 %all-to-all-start.1 = ((bf16[16,128,256]{2,1,0:T(8,128)(2,1)}), bf16[16,128,256]{2,1,0:T(8,128)(2,1)S(1)}, u32[]{:S(2)}, u32[]{:S(2)}) async-start(bf16[16,128,256]{2,1,0:T(8,128)(2,1)} %bitcast.46), calls=%async_computation.1 | async-start | bytes 2097152 | tf_op jit(solution)/shard_map/all_to_all | solution.py:686
  66.9 0.0 collective-permute-done.11.refs_10_
  67.0 0.8 copy-done.10
  67.7 0.2 copy-done.11
  67.9 0.1 copy-done.12
  68.1 13.2 %weight_grads.1 = bf16[8,832,128]{2,1,0:T(8,128)(2,1)} custom-call(s32[16]{0:T(128)} %stack.67.slot.refs_0_, bf16[256,1024]{1,0:T(8,128)(2,1)} %copy-done.1, bf16[256,1024]{1,0:T(8,128)(2,1)} %copy-done.6, bf16[256,1024]{1,0:T(8,128)(2,1)} %copy-done.3, bf16[256,1024]{1,0:T(8,128)(2,1)} %copy-done.7, bf16[256,1024]{1,0:T(8,128)(2,1)} %copy-done.4, ...), custom_call_target="tpu_custom_call" | custom-call | flops 8000000000 | bytes 20971520 | tf_op jit(solution)/shard_map/weight_grads/pallas_call | solution.py:487
  81.2 1.5 %all-to-all-done.1 = bf16[16,128,256]{2,1,0:T(8,128)(2,1)S(1)} async-done(((bf16[16,128,256]{2,1,0:T(8,128)(2,1)}), bf16[16,128,256]{2,1,0:T(8,128)(2,1)S(1)}, u32[]{:S(2)}, u32[]{:S(2)}) %all-to-all-start.1) | async-done | bytes 1048608 | tf_op jit(solution)/shard_map/all_to_all | solution.py:686
  82.7 7.2 %all-to-all-start.2 = ((bf16[8,832,128]{2,1,0:T(8,128)(2,1)}), bf16[8,832,128]{2,1,0:T(8,128)(2,1)S(1)}, u32[]{:S(2)}, u32[]{:S(2)}) async-start(bf16[8,832,128]{2,1,0:T(8,128)(2,1)} %weight_grads.1), calls=%async_computation.2 | async-start | bytes 3407872 | tf_op jit(solution)/shard_map/all_to_all | solution.py:692
  89.9 12.0 %own_rows.1 = (f32[128,1024]{1,0:T(8,128)}, f32[128,1024]{1,0:T(8,128)}) custom-call(bf16[128,1024]{1,0:T(8,128)(2,1)} %bitcast.42, bf16[128,1024]{1,0:T(8,128)(2,1)} %bitcast.38, f32[1,1024]{1,0:T(1,128)} %bitcast.54, f32[1,1024]{1,0:T(1,128)} %bitcast.59, bf16[1024,2816]{1,0:T(8,128)(2,1)} %wg_in.1, bf16[1024,2816]{1,0:T(8,128)(2,1)} %wu_in.1, ...), custom_call_target="tpu_custom_call" | custom-call | flops 4499999744 | bytes 18874368 | tf_op jit(solution)/shard_map/own_rows/pallas_call | solution.py:113
  102.0 8.0 %final_rows.1 = (bf16[128,1024]{1,0:T(8,128)(2,1)}, bf16[128,1024]{1,0:T(8,128)(2,1)}) custom-call(bf16[2048,256]{1,0:T(8,128)(2,1)} %bitcast.45, bf16[128,1024]{1,0:T(8,128)(2,1)} %bitcast.43, bf16[128,1024]{1,0:T(8,128)(2,1)} %bitcast.39, f32[128,1024]{1,0:T(8,128)} %get-tuple-element.63.part, f32[128,1024]{1,0:T(8,128)} %get-tuple-element.64.grad, ...), custom_call_target="tpu_custom_call" | custom-call | flops 1100000000 | bytes 10485760 | tf_op jit(solution)/shard_map/final_rows/pallas_call | solution.py:544
  110.0 1.8 %all-to-all-done.2.got = bf16[8,832,128]{2,1,0:T(8,128)(2,1)S(1)} async-done(((bf16[8,832,128]{2,1,0:T(8,128)(2,1)}), bf16[8,832,128]{2,1,0:T(8,128)(2,1)S(1)}, u32[]{:S(2)}, u32[]{:S(2)}) %all-to-all-start.2) | async-done | bytes 1703968 | tf_op jit(solution)/shard_map/all_to_all | solution.py:692
  111.8 1.0 sum_rows.1
  112.8 10.8 %all_to_all.39 = bf16[16,8,640]{2,1,0:T(8,128)(2,1)S(1)} all-to-all(bf16[16,8,640]{2,1,0:T(8,128)(2,1)S(1)} %bitcast.35), channel_id=1, replica_groups=mesh['seq'=16,'rows'=8] {'seq'}, dimensions={0} | all-to-all | bytes 327680 | tf_op jit(solution)/shard_map/all_to_all | solution.py:698
  123.6 0.8 last_layout.1
  124.4 0.5 slice_bitcast_fusion
  (27 shorter events, 0.1 us)
Async XLA Ops:
  1.7 22.1 %copy-start.1 = (bf16[256,1024]{1,0:T(8,128)(2,1)}, bf16[256,1024]{1,0:T(8,128)(2,1)S(1)}, u32[]{:S(2)}) copy-start(bf16[256,1024]{1,0:T(8,128)(2,1)S(1)} %pad_maximum_fusion.refs_1_) | copy-start | bytes 1572868
  1.7 17.0 %collective-permute-start.1 = (bf16[256,1024]{1,0:T(8,128)(2,1)S(1)}, bf16[256,1024]{1,0:T(8,128)(2,1)S(1)}, u32[]{:S(2)}, u32[]{:S(2)}) collective-permute-start(bf16[256,1024]{1,0:T(8,128)(2,1)S(1)} %pad_maximum_fusion.refs_1_), channel_id=1, source_target_pairs={{0,32},{8,40},{16,48},{24,56},{32,64},{40,72},{48,80},{56,88},{64,... | collective-permute-start | bytes 1572872 | tf_op jit(solution)/shard_map/ppermute | solution.py:634
  3.9 14.8 %collective-permute-start.3 = (bf16[256,1024]{1,0:T(8,128)(2,1)S(1)}, bf16[256,1024]{1,0:T(8,128)(2,1)S(1)}, u32[]{:S(2)}, u32[]{:S(2)}) collective-permute-start(bf16[256,1024]{1,0:T(8,128)(2,1)S(1)} %pad_maximum_fusion.refs_1_), channel_id=1, source_target_pairs={{0,96},{8,104},{16,112},{24,120},{32,0},{40,8},{48,16},{56,24},{64... | collective-permute-start | bytes 1572872 | tf_op jit(solution)/shard_map/ppermute | solution.py:634
  5.4 13.3 %collective-permute-start.5 = (bf16[256,1024]{1,0:T(8,128)(2,1)S(1)}, bf16[256,1024]{1,0:T(8,128)(2,1)S(1)}, u32[]{:S(2)}, u32[]{:S(2)}) collective-permute-start(bf16[256,1024]{1,0:T(8,128)(2,1)S(1)} %pad_maximum_fusion.refs_1_), channel_id=1, source_target_pairs={{0,16},{8,24},{16,0},{24,8},{32,48},{40,56},{48,32},{56,40},{64,80... | collective-permute-start | bytes 1572872 | tf_op jit(solution)/shard_map/ppermute | solution.py:634
  18.7 12.9 %copy-start.3 = (bf16[256,1024]{1,0:T(8,128)(2,1)}, bf16[256,1024]{1,0:T(8,128)(2,1)S(1)}, u32[]{:S(2)}) copy-start(bf16[256,1024]{1,0:T(8,128)(2,1)S(1)} %collective-permute-done.1.refs_3_) | copy-start | bytes 1572868
  18.7 12.9 %copy-start.4 = (bf16[256,1024]{1,0:T(8,128)(2,1)}, bf16[256,1024]{1,0:T(8,128)(2,1)S(1)}, u32[]{:S(2)}) copy-start(bf16[256,1024]{1,0:T(8,128)(2,1)S(1)} %collective-permute-done.3.refs_5_) | copy-start | bytes 1572868
  18.8 12.9 %copy-start.5 = (bf16[256,1024]{1,0:T(8,128)(2,1)}, bf16[256,1024]{1,0:T(8,128)(2,1)S(1)}, u32[]{:S(2)}) copy-start(bf16[256,1024]{1,0:T(8,128)(2,1)S(1)} %collective-permute-done.5.refs_7_) | copy-start | bytes 1572868
  18.8 20.9 %all-to-all-start = ((bf16[16,128,256]{2,1,0:T(8,128)(2,1)}), bf16[16,128,256]{2,1,0:T(8,128)(2,1)S(1)}, u32[]{:S(2)}, u32[]{:S(2)}) async-start(bf16[16,128,256]{2,1,0:T(8,128)(2,1)} %bitcast.44), calls=%async_computation | async-start | bytes 2097152 | tf_op jit(solution)/shard_map/all_to_all | solution.py:675
  23.8 2.5 %collective-permute-start = (bf16[256,1024]{1,0:T(8,128)(2,1)S(1)}, bf16[256,1024]{1,0:T(8,128)(2,1)S(1)}, u32[]{:S(2)}, u32[]{:S(2)}) collective-permute-start(bf16[256,1024]{1,0:T(8,128)(2,1)S(1)} %pad_maximum_fusion.refs_1_), channel_id=1, source_target_pairs={{0,8},{8,0},{16,24},{24,16},{32,40},{40,32},{48,56},{56,48},{64,72... | collective-permute-start | bytes 1572872 | tf_op jit(solution)/shard_map/ppermute | solution.py:634
  24.0 3.5 %collective-permute-start.2 = (bf16[256,1024]{1,0:T(8,128)(2,1)S(1)}, bf16[256,1024]{1,0:T(8,128)(2,1)S(1)}, u32[]{:S(2)}, u32[]{:S(2)}) collective-permute-start(bf16[256,1024]{1,0:T(8,128)(2,1)S(1)} %collective-permute-done.1.refs_3_), channel_id=1, source_target_pairs={{0,8},{8,0},{16,24},{24,16},{32,40},{40,32},{48,56},{56,48},{64,72... | collective-permute-start | bytes 1572872 | tf_op jit(solution)/shard_map/ppermute | solution.py:634
  24.4 6.4 %collective-permute-start.4 = (bf16[256,1024]{1,0:T(8,128)(2,1)S(1)}, bf16[256,1024]{1,0:T(8,128)(2,1)S(1)}, u32[]{:S(2)}, u32[]{:S(2)}) collective-permute-start(bf16[256,1024]{1,0:T(8,128)(2,1)S(1)} %collective-permute-done.3.refs_5_), channel_id=1, source_target_pairs={{0,8},{8,0},{16,24},{24,16},{32,40},{40,32},{48,56},{56,48},{64,72... | collective-permute-start | bytes 1572872 | tf_op jit(solution)/shard_map/ppermute | solution.py:634
  24.5 7.1 %collective-permute-start.6 = (bf16[256,1024]{1,0:T(8,128)(2,1)S(1)}, bf16[256,1024]{1,0:T(8,128)(2,1)}, u32[]{:S(2)}, u32[]{:S(2)}) collective-permute-start(bf16[256,1024]{1,0:T(8,128)(2,1)S(1)} %collective-permute-done.5.refs_7_), channel_id=1, source_target_pairs={{0,8},{8,0},{16,24},{24,16},{32,40},{40,32},{48,56},{56,48},{64,72... | collective-permute-start | bytes 1572872 | tf_op jit(solution)/shard_map/ppermute | solution.py:634
  24.9 26.6 %collective-permute-start.7 = (bf16[256,1024]{1,0:T(8,128)(2,1)S(1)}, bf16[256,1024]{1,0:T(8,128)(2,1)}, u32[]{:S(2)}, u32[]{:S(2)}) collective-permute-start(bf16[256,1024]{1,0:T(8,128)(2,1)S(1)} %collective-permute-done.1.refs_3_), channel_id=1, source_target_pairs={{0,32},{8,40},{16,48},{24,56},{32,64},{40,72},{48,80},{56,88},{64,... | collective-permute-start | bytes 1572872 | tf_op jit(solution)/shard_map/ppermute | solution.py:634
  26.3 5.4 %copy-start.6 = (bf16[256,1024]{1,0:T(8,128)(2,1)}, bf16[256,1024]{1,0:T(8,128)(2,1)S(1)}, u32[]{:S(2)}) copy-start(bf16[256,1024]{1,0:T(8,128)(2,1)S(1)} %collective-permute-done.refs_2_) | copy-start | bytes 1572868
  26.3 25.2 %collective-permute-start.9 = (bf16[256,1024]{1,0:T(8,128)(2,1)S(1)}, bf16[256,1024]{1,0:T(8,128)(2,1)S(1)}, u32[]{:S(2)}, u32[]{:S(2)}) collective-permute-start(bf16[256,1024]{1,0:T(8,128)(2,1)S(1)} %collective-permute-done.1.refs_3_), channel_id=1, source_target_pairs={{0,16},{8,24},{16,0},{24,8},{32,48},{40,56},{48,32},{56,40},{64,80... | collective-permute-start | bytes 1572872 | tf_op jit(solution)/shard_map/ppermute | solution.py:634
  27.5 3.3 %copy-start.7 = (bf16[256,1024]{1,0:T(8,128)(2,1)}, bf16[256,1024]{1,0:T(8,128)(2,1)S(1)}, u32[]{:S(2)}) copy-start(bf16[256,1024]{1,0:T(8,128)(2,1)S(1)} %collective-permute-done.2.refs_4_) | copy-start | bytes 1572868
  27.5 33.5 %collective-permute-start.10 = (bf16[256,1024]{1,0:T(8,128)(2,1)S(1)}, bf16[256,1024]{1,0:T(8,128)(2,1)}, u32[]{:S(2)}, u32[]{:S(2)}) collective-permute-start(bf16[256,1024]{1,0:T(8,128)(2,1)S(1)} %collective-permute-done.3.refs_5_), channel_id=1, source_target_pairs={{0,112},{8,120},{16,96},{24,104},{32,16},{40,24},{48,0},{56,8},{64... | collective-permute-start | bytes 1572872 | tf_op jit(solution)/shard_map/ppermute | solution.py:634
  30.8 0.8 copy-start.8
  30.8 30.2 %collective-permute-start.8 = (bf16[256,1024]{1,0:T(8,128)(2,1)S(1)}, bf16[256,1024]{1,0:T(8,128)(2,1)}, u32[]{:S(2)}, u32[]{:S(2)}) collective-permute-start(bf16[256,1024]{1,0:T(8,128)(2,1)S(1)} %collective-permute-done.5.refs_7_), channel_id=1, source_target_pairs={{0,96},{8,104},{16,112},{24,120},{32,0},{40,8},{48,16},{56,24},{64... | collective-permute-start | bytes 1572872 | tf_op jit(solution)/shard_map/ppermute | solution.py:634
  39.7 1.0 copy-start.2
  51.6 15.4 %copy-start.9 = (bf16[256,1024]{1,0:T(8,128)(2,1)}, bf16[256,1024]{1,0:T(8,128)(2,1)S(1)}, u32[]{:S(2)}) copy-start(bf16[256,1024]{1,0:T(8,128)(2,1)S(1)} %collective-permute-done.9.refs_13_) | copy-start | bytes 1572868
  61.0 5.9 %collective-permute-start.11 = (bf16[256,1024]{1,0:T(8,128)(2,1)}, bf16[256,1024]{1,0:T(8,128)(2,1)S(1)}, u32[]{:S(2)}, u32[]{:S(2)}) collective-permute-start(bf16[256,1024]{1,0:T(8,128)(2,1)} %collective-permute-done.7.refs_9_), channel_id=1, source_target_pairs={{0,8},{8,0},{16,24},{24,16},{32,40},{40,32},{48,56},{56,48},{64,72... | collective-permute-start | bytes 1572872 | tf_op jit(solution)/shard_map/ppermute | solution.py:634
  61.9 5.0 %collective-permute-start.12 = (bf16[256,1024]{1,0:T(8,128)(2,1)}, bf16[256,1024]{1,0:T(8,128)(2,1)S(1)}, u32[]{:S(2)}, u32[]{:S(2)}) collective-permute-start(bf16[256,1024]{1,0:T(8,128)(2,1)} %collective-permute-done.8.refs_11_), channel_id=1, source_target_pairs={{0,8},{8,0},{16,24},{24,16},{32,40},{40,32},{48,56},{56,48},{64,72... | collective-permute-start | bytes 1572872 | tf_op jit(solution)/shard_map/ppermute | solution.py:634
  61.9 5.0 %collective-permute-start.13 = (bf16[256,1024]{1,0:T(8,128)(2,1)S(1)}, bf16[256,1024]{1,0:T(8,128)(2,1)S(1)}, u32[]{:S(2)}, u32[]{:S(2)}) collective-permute-start(bf16[256,1024]{1,0:T(8,128)(2,1)S(1)} %collective-permute-done.9.refs_13_), channel_id=1, source_target_pairs={{0,8},{8,0},{16,24},{24,16},{32,40},{40,32},{48,56},{56,48},{64,72... | collective-permute-start | bytes 1572872 | tf_op jit(solution)/shard_map/ppermute | solution.py:634
  62.4 4.5 %collective-permute-start.14 = (bf16[256,1024]{1,0:T(8,128)(2,1)}, bf16[256,1024]{1,0:T(8,128)(2,1)}, u32[]{:S(2)}, u32[]{:S(2)}) collective-permute-start(bf16[256,1024]{1,0:T(8,128)(2,1)} %collective-permute-done.10.refs_15_), channel_id=1, source_target_pairs={{0,8},{8,0},{16,24},{24,16},{32,40},{40,32},{48,56},{56,48},{64,72... | collective-permute-start | bytes 1572872 | tf_op jit(solution)/shard_map/ppermute | solution.py:634
  62.4 20.3 %all-to-all-start.1 = ((bf16[16,128,256]{2,1,0:T(8,128)(2,1)}), bf16[16,128,256]{2,1,0:T(8,128)(2,1)S(1)}, u32[]{:S(2)}, u32[]{:S(2)}) async-start(bf16[16,128,256]{2,1,0:T(8,128)(2,1)} %bitcast.46), calls=%async_computation.1 | async-start | bytes 2097152 | tf_op jit(solution)/shard_map/all_to_all | solution.py:686
  66.9 0.8 copy-start.10
  66.9 1.0 copy-start.11
  66.9 1.1 copy-start.12
  82.7 19.3 %copy-start = (bf16[16,128,256]{2,1,0:T(8,128)(2,1)}, bf16[16,128,256]{2,1,0:T(8,128)(2,1)S(1)}, u32[]{:S(2)}) copy-start(bf16[16,128,256]{2,1,0:T(8,128)(2,1)S(1)} %all-to-all-done.1) | copy-start | bytes 3145732
  82.7 29.1 %all-to-all-start.2 = ((bf16[8,832,128]{2,1,0:T(8,128)(2,1)}), bf16[8,832,128]{2,1,0:T(8,128)(2,1)S(1)}, u32[]{:S(2)}, u32[]{:S(2)}) async-start(bf16[8,832,128]{2,1,0:T(8,128)(2,1)} %weight_grads.1), calls=%async_computation.2 | async-start | bytes 3407872 | tf_op jit(solution)/shard_map/all_to_all | solution.py:692

commit v3 on v2

--- a/solution.py
+++ b/solution.py
@@ -128,7 +128,7 @@
 
 
 def heads_kernel(
-    slot, order, x, dy, w_q, w_k, w_v, w_o, b_q, b_k, b_v, gain, bias,
+    order, x, dy, w_q, w_k, w_v, w_o, b_q, b_k, b_v, gain, bias,
     table, out, hid, cosine, sine,
 ):
     lanes = 2 * HEAD_DIM
@@ -142,7 +142,7 @@
         hid[...] = (unit * gain[...] + bias[...]).astype(bf16)
         for g in range(HERE // GROUP):
             rows = slice(g * GROUP, (g + 1) * GROUP)
-            group = order[slot[0] * (HERE // GROUP) + g]
+            group = order[lax.axis_index("seq") * (HERE // GROUP) + g]
             cosine[rows, :], sine[rows, :] = group_rotation(table, group)
 
     q = dot_nn(hid[...], w_q[...]) + b_q[...]
@@ -159,7 +159,7 @@
         out[rows, lanes:] = jnp.concatenate([v[:, part], grad_att[:, part]], 1).astype(bf16)
 
 
-def own_heads(slot, order, x, dy, w_qkv, w_out, b_qkv, gain, bias, table):
+def own_heads(order, x, dy, w_qkv, w_out, b_qkv, gain, bias, table):
     fixed = lambda shape: pl.BlockSpec(shape, lambda j: (0,) * len(shape))
     own, vector = fixed((HERE, WIDTH)), fixed((1, WIDTH))
     steps = WIDTH // BLOCK
@@ -171,7 +171,7 @@
         heads_kernel,
         grid=(steps,),
         out_shape=jax.ShapeDtypeStruct((LENGTH, 4 * HEAD_DIM), bf16),
-        in_specs=[SMEM] * 2
+        in_specs=[SMEM]
         + [own, own, part(WIDTH, 0), part(WIDTH, 1), part(WIDTH, 2)]
         + [pl.BlockSpec((BLOCK, WIDTH), lambda j: (j, 0)), part(1, 0), part(1, 1), part(1, 2)]
         + [vector, vector, fixed(table.shape)],
@@ -184,7 +184,7 @@
         compiler_params=params(60),
         cost_estimate=cost(1.1, 9),
         name="own_heads",
-    )(slot, order, x, dy, w_qkv, w_qkv, w_qkv, w_out, b_qkv, b_qkv, b_qkv, gain, bias, table)
+    )(order, x, dy, w_qkv, w_qkv, w_qkv, w_out, b_qkv, b_qkv, b_qkv, gain, bias, table)
 
 
 def attention_kernel(*refs):
@@ -273,8 +273,8 @@
     )(*first, order, packed, position_table())
 
 
-def cut_kernel(slot, w_qkv, w_gate, w_up, out_qkv, out_gu, wide_qkv, wide_gu, sems):
-    here = slot[0]
+def cut_kernel(w_qkv, w_gate, w_up, out_qkv, out_gu, wide_qkv, wide_gu, sems):
+    here = lax.axis_index("seq")
     first = here * FF_LOCAL
     tile = jnp.minimum(first // 128, (FF - 384) // 128) * 128
     copies = []
@@ -299,14 +299,14 @@
     out_gu[FF_LOCAL:, :] = dot_tt(pick_gu, wide_gu[1]).astype(bf16)
 
 
-def cut_weights(slot, w_qkv, w_gate, w_up):
+def cut_weights(w_qkv, w_gate, w_up):
     return pl.pallas_call(
         cut_kernel,
         out_shape=[
             jax.ShapeDtypeStruct((3 * HEAD_DIM, WIDTH), bf16),
             jax.ShapeDtypeStruct((2 * FF_LOCAL, WIDTH), bf16),
         ],
-        in_specs=[SMEM] + [ANY] * 3,
+        in_specs=[ANY] * 3,
         out_specs=[VMEM] * 2,
         scratch_shapes=[
             pltpu.VMEM((WIDTH, 384), bf16),
@@ -316,26 +316,34 @@
         compiler_params=params(60),
         cost_estimate=cost(0.001, 0.001),
         name="cut_weights",
-    )(slot, w_qkv, w_gate, w_up)
+    )(w_qkv, w_gate, w_up)
 
 
 def column(row):
     return jnp.broadcast_to(row, (8, row.shape[1])).T[:, :1]
+
+
+def slot_of(i):
+    here = lax.axis_index("seq")
+    across, up = PLACES[i // 2]
+    y = lax.rem(lax.div(here, 4) + (4 + up), 4)
+    x = lax.rem(lax.div(here, 2) + across, 2)
+    return y * 4 + x * 2 + lax.rem(here + i % 2, 2)
 
 
 def piece_copies(pieces, inputs, x_all, dy, sems):
     return [
         pltpu.make_async_copy(
-            inputs[ref].at[pl.ds(which * HERE, HERE), :],
-            (x_all, dy)[which].at[pl.ds(to * HERE, HERE), :],
+            inputs[ref].at[pl.ds(at, rows), :],
+            (x_all, dy)[which].at[pl.ds(to, rows), :],
             sems.at[i],
         )
-        for i, (which, ref, to) in enumerate(pieces)
+        for i, (which, ref, at, rows, to) in enumerate(pieces)
     ]
 
 
-def down_copy(slot, source, to, sem):
-    rows = pl.ds(pl.multiple_of(slot[0] * FF_LOCAL, 16), FF_LOCAL)
+def down_copy(source, to, sem):
+    rows = pl.ds(pl.multiple_of(lax.axis_index("seq") * FF_LOCAL, 16), FF_LOCAL)
     return pltpu.make_async_copy(source.at[rows, :], to, sem)
 
 
@@ -354,11 +362,11 @@
     return total
 
 
-def first_kernel(pieces, n_refs, slot, *refs):
+def first_kernel(pieces, n_refs, *refs):
     inputs, refs = refs[:n_refs], refs[n_refs:]
     w_gu, w_d_in, gain, bias, unit, acts, grads, sums, x_all, dy, w_d, sems, sem = refs
     copies = piece_copies(pieces, inputs, x_all, dy, sems)
-    copies.append(down_copy(slot, w_d_in, w_d, sem))
+    copies.append(down_copy(w_d_in, w_d, sem))
     for copy in copies:
         copy.start()
     for copy in copies:
@@ -372,7 +380,7 @@
     sums[...] = jnp.broadcast_to(total, sums.shape)
 
 
-def first_half(slot, arrays, pieces, w_gu, w_d, gain, bias):
+def first_half(arrays, pieces, w_gu, w_d, gain, bias):
     half = LENGTH // 2
     return pl.pallas_call(
         lambda *refs: first_kernel(pieces, len(arrays), *refs),
@@ -382,7 +390,7 @@
             jax.ShapeDtypeStruct((2 * FF_LOCAL, half), bf16),
             jax.ShapeDtypeStruct((2 * FF_LOCAL, 128), f32),
         ],
-        in_specs=[SMEM] + [ANY] * len(arrays) + [VMEM] + [ANY] + [VMEM] * 2,
+        in_specs=[ANY] * len(arrays) + [VMEM] + [ANY] + [VMEM] * 2,
         out_specs=[VMEM] * 4,
         scratch_shapes=[
             pltpu.VMEM((half, WIDTH), bf16),
@@ -394,28 +402,28 @@
         compiler_params=params(60),
         cost_estimate=cost(0.001, 0.001),
         name="first_half",
-    )(slot, *arrays, w_gu, w_d, gain, bias)
-
-
-def weights_kernel(pieces, n_refs, slot, *refs):
+    )(*arrays, w_gu, w_d, gain, bias)
+
+
+def weights_kernel(pieces, n_refs, *refs):
     inputs, refs = refs[:n_refs], refs[n_refs:]
     heads_in, w_qkv, w_gu, w_d_in, gain, bias = refs[:6]
     unit_in, acts_in, grads_in, sums, block_out = refs[6:11]
     x_all, dy, unit, heads, left, right, stage, w_d, block = refs[11:20]
     piece_sems, head_sems, out_sems, first_sems, weight_sem = refs[20:]
     hidden, both = FF_LOCAL, 2 * FF_LOCAL
-    here = slot[0]
+    here = lax.axis_index("seq")
     half = LENGTH // 2
     late = (dy.at[half:, :], unit.at[half:, :])
     copies = piece_copies(pieces, inputs, x_all, dy, piece_sems)
-    now = [copy for copy, piece in zip(copies, pieces) if piece[2] >= SEQ // 2]
-    now.append(down_copy(slot, w_d_in, w_d, weight_sem))
-    later = [copy for copy, piece in zip(copies, pieces) if piece[0] and piece[2] < SEQ // 2]
+    now = [copy for copy, piece in zip(copies, pieces) if piece[4] >= half]
+    now.append(down_copy(w_d_in, w_d, weight_sem))
+    later = [copy for copy, piece in zip(copies, pieces) if piece[0] and piece[4] < half]
     later.append(pltpu.make_async_copy(unit_in, unit.at[:half, :], first_sems.at[0]))
     later.append(pltpu.make_async_copy(acts_in, right.at[:hidden, :half], first_sems.at[1]))
     later.append(pltpu.make_async_copy(grads_in, left.at[:both, :half], first_sems.at[2]))
     for i in range(SEQ):
-        rows = pl.ds(pl.multiple_of(slot[i] * HERE, HERE), HERE)
+        rows = pl.ds(pl.multiple_of(slot_of(i) * HERE, HERE), HERE)
         to = heads.at[i * HERE : (i + 1) * HERE, :]
         later.append(pltpu.make_async_copy(heads_in.at[rows, :], to, head_sems.at[i]))
     for copy in now + later:
@@ -482,12 +490,12 @@
         copy.wait()
 
 
-def weight_grads(slot, arrays, pieces, heads, w_qkv, w_gu, w_d, gain, bias, first):
+def weight_grads(arrays, pieces, heads, w_qkv, w_gu, w_d, gain, bias, first):
     big = (LENGTH, WIDTH)
     return pl.pallas_call(
         lambda *refs: weights_kernel(pieces, len(arrays), *refs),
         out_shape=jax.ShapeDtypeStruct((ROWS, 832, 128), bf16),
-        in_specs=[SMEM] + [ANY] * (len(arrays) + 1) + [VMEM] * 2 + [ANY] + [VMEM] * 2 + [ANY] * 3 + [VMEM],
+        in_specs=[ANY] * (len(arrays) + 1) + [VMEM] * 2 + [ANY] + [VMEM] * 2 + [ANY] * 3 + [VMEM],
         out_specs=ANY,
         scratch_shapes=[pltpu.VMEM(big, bf16)] * 3
         + [
@@ -506,7 +514,7 @@
         compiler_params=params(60),
         cost_estimate=cost(8, 20),
         name="weight_grads",
-    )(slot, *arrays, heads, w_qkv, w_gu, w_d, gain, bias, *first)
+    )(*arrays, heads, w_qkv, w_gu, w_d, gain, bias, *first)
 
 
 def final_kernel(heads, x, dy, part, grad, gain, w_out, w_qkv, out, input_grad, att, rows, total):
@@ -590,7 +598,7 @@
     )(got)
 
 
-def layout_kernel(mine, qkv, gate, up, vectors, sums):
+def layout_kernel(mine, qkv, gate, up, gain, bias, sums):
     more = jnp.zeros((8, 128), f32)
     for s in range(SEQ):
         here = mine[s * 8 : (s + 1) * 8, :].astype(f32)
@@ -600,7 +608,9 @@
             lo = i * WIDTH + s * HEAD_DIM
             qkv[:, lo : lo + HEAD_DIM] = here[:, 384 + i * HEAD_DIM : 384 + (i + 1) * HEAD_DIM]
         more += here[:, 256:384]
-    vectors[...] = more.T[96:98, :]
+    turned = more.T
+    gain[...] = turned[96:97, :]
+    bias[...] = turned[97:98, :]
     sums[...] = more[0:1, 98:122]
 
 
@@ -611,18 +621,19 @@
             jax.ShapeDtypeStruct((8, 3 * WIDTH), f32),
             jax.ShapeDtypeStruct((8, FF), f32),
             jax.ShapeDtypeStruct((8, FF), f32),
-            jax.ShapeDtypeStruct((2, 8), f32),
+            jax.ShapeDtypeStruct((1, 8), f32),
+            jax.ShapeDtypeStruct((1, 8), f32),
             jax.ShapeDtypeStruct((1, 24), f32),
         ],
         in_specs=[VMEM],
-        out_specs=[VMEM] * 5,
+        out_specs=[VMEM] * 6,
         compiler_params=params(16),
         cost_estimate=cost(0.001, 1),
         name="last_layout",
     )(mine)
 
 
-PLACES = [(0, 0), (0, -1), (0, 1), (1, 0), (0, 2), (1, 1), (1, -1), (1, 2)]
+PLACES = [(0, 0), (0, -1), (0, 1), (1, 0), (0, 2), (1, 2), (1, 1), (1, -1)]
 CORE = [(i, i ^ 1) for i in range(SEQ)]
 PAIR = [(i, i ^ 2) for i in range(SEQ)]
 UP = [(i, (i + 4) % SEQ) for i in range(SEQ)]
@@ -641,34 +652,43 @@
     pair = send(own, PAIR)
     late = exchange((below, above, pair))
     far = send(below, UP)
-    across_below = send(below, PAIR)
-    across_above = send(pair, DOWN)
     opposite = send(above, DOWN_PAIR)
-    arrays = [own, below, above, pair, far, across_above, across_below, opposite]
-    first = [both for a in arrays[:4] for both in (a, send(a, CORE))]
-    late, rest = after(late, first, arrays[4:])
+    most = pair[:MOST]
+    rest = [far, opposite, send(most, DOWN), send(most, UP)]
+    rest.append(send(jnp.concatenate([above[MOST:], below[MOST:]], 0), PAIR))
+    first = [both for a in (own, below, above, pair) for both in (a, send(a, CORE))]
+    late, rest = after(late, first, rest)
     return first, [both for a in rest for both in (a, send(a, CORE))], late
 
 
-def pieces_of(count):
-    return [(which, i, i) for i in range(count) for which in range(2)]
+MOST = 176
+
+
+def pieces_of(places):
+    return [
+        (which, i, which * HERE, HERE, i * HERE) for i in range(places) for which in range(2)
+    ]
+
+
+def pieces_late():
+    pieces = pieces_of(12)
+    for place in range(2):
+        for core in range(2):
+            to = (12 + 2 * place + core) * HERE
+            first, left = 12 + 2 * place + core, 2 * HERE - MOST
+            pieces.append((0, first, 0, HERE, to))
+            pieces.append((1, first, HERE, MOST - HERE, to))
+            pieces.append((1, 16 + core, place * left, left, to + MOST - HERE))
+    return pieces
 
 
 def shards(x, dy, order, ln_gain, ln_bias, w_qkv, b_qkv, w_out, w_gate, w_up, w_down):
     x, dy = x[0], dy[0]
-    s = lax.axis_index("seq")
-    slot = jnp.stack(
-        [
-            ((s // 4 + up) % 4) * 4 + ((s // 2 % 2) ^ across) * 2 + (s % 2 ^ core)
-            for across, up in PLACES
-            for core in range(2)
-        ]
-    ).astype(jnp.int32)
     gain, bias = ln_gain[None, :], ln_bias[None, :]
 
     table = rotary_tables()
-    packed = own_heads(slot, order, x, dy, w_qkv, w_out, b_qkv[None, :], gain, bias, table)
-    w_qkv_s, w_gu_s = cut_weights(slot, w_qkv, w_gate, w_up)
+    packed = own_heads(order, x, dy, w_qkv, w_out, b_qkv[None, :], gain, bias, table)
+    w_qkv_s, w_gu_s = cut_weights(w_qkv, w_gate, w_up)
 
     def exchange(first):
         ready, _ = lax.optimization_barrier((packed, (first, w_gu_s)))
@@ -676,7 +696,7 @@
 
     def attend(packed_here, early, arrays):
         first = first_half(
-            slot, early, pieces_of(len(early)), w_gu_s, w_down, gain, bias
+            early, pieces_of(len(early)), w_gu_s, w_down, gain, bias
         )
         heads = attention(order, packed_here, first)
         (heads, first), arrays = lax.optimization_barrier(((heads, first), arrays))
@@ -686,7 +706,7 @@
     heads_here = lax.all_to_all(heads, "seq", 0, 0, tiled=True)
     arrays = early + arrays
     block = weight_grads(
-        slot, arrays, pieces_of(SEQ), heads, w_qkv_s, w_gu_s, w_down, gain, bias, first
+        arrays, pieces_late(), heads, w_qkv_s, w_gu_s, w_down, gain, bias, first
     )
     block, heads_here = lax.optimization_barrier((block, heads_here))
     got = lax.all_to_all(block, "rows", 0, 0, tiled=True)
@@ -696,7 +716,7 @@
     got, output, input_grad = lax.optimization_barrier((got, output, input_grad))
     outgoing, o_down, o_out = sum_rows(got)
     mine = lax.all_to_all(outgoing, "seq", 0, 0, tiled=True)
-    o_qkv, o_gate, o_up, vectors, sums = last_layout(mine)
+    o_qkv, o_gate, o_up, o_gain, o_bias, sums = last_layout(mine)
     return (
         output[None],
         input_grad[None],
@@ -706,8 +726,8 @@
         o_up,
         o_down,
         sums[0],
-        vectors[0],
-        vectors[1],
+        o_gain[0],
+        o_bias[0],
     )
 
 

time: 126 us -> 122 us (0.968)
  waiting for transfers between devices: 13.4 us -> 8.95 us
    ppermute x15 -> x17, waiting for transfers between devices: 9.49 us -> 5.86 us  [send(): return lax.ppermute(value, 'seq', to)]
    unnamed x26 -> x30, local copies, waits for them, and re-layouts: 2.12 us -> 3.84 us
    ppermute x15 -> x17, starting transfers between devices: 14.1 us -> 13.8 us  [send(): return lax.ppermute(value, 'seq', to)]
  transfers between devices with their start and end apart: 18 -> 20, of which waited for: 4 -> 4; matrix products, arithmetic and copies ran while one was open for 1% -> 1% of each run, Pallas kernels for 50% -> 51%
where the time goes in v3:
time: 122 us; the launch traced here: 121 us
  Pallas kernels  63.8 us (52%)
  starting transfers between devices  30.8 us (25%)
  blocking collectives  11 us (9%)
  waiting for transfers between devices  8.95 us (7%)
  local copies, waits for them, and re-layouts  3.89 us (3%)
  other arithmetic  1.83 us (2%)
    ppermute x17, starting transfers between devices, send(): return lax.ppermute(value, 'seq', to)  13.8 us
    pallas_call x1, Pallas kernels, weight_grads(): pl.pallas_call(lambda *refs: weights_kernel(pieces, len(arrays), *refs),...  13.2 us
    pallas_call x1, Pallas kernels, own_rows(): pl.pallas_call(own_kernel, out_shape=[jax.ShapeDtypeStruct((HERE, WIDTH),...  12.1 us
    all_to_all x1, blocking collectives, shards(): mine = lax.all_to_all(outgoing, 'seq', 0, 0, tiled=True)  11 us
    pallas_call x1, Pallas kernels, attention(): pl.pallas_call(attention_kernel, out_shape=jax.ShapeDtypeStruct((LENGTH,...  10.9 us
    pallas_call x1, Pallas kernels, final_rows(): pl.pallas_call(final_kernel, grid=(WIDTH // BLOCK,), out_shape=[jax.Shape...  8.02 us
    pallas_call x1, Pallas kernels, first_half(): pl.pallas_call(lambda *refs: first_kernel(pieces, len(arrays), *refs), ou...  7.31 us
    all_to_all x1, starting transfers between devices, shards(): got = lax.all_to_all(block, 'rows', 0, 0, tiled=True)  7.2 us
  transfers between devices with their start and end apart: 20, of which 4 were waited for; matrix products, arithmetic and copies ran while one was open for 1% of the time, Pallas kernels for 51%

profile of v3, /device:TPU:1, one launch (start us, length us, event | category | flops | bytes accessed | tf_op | source)
XLA Modules:
  0.0 121.1 jit_solution(6563477280627317430)
XLA Ops:
  0.6 1.1 pad_maximum_fusion.refs_0_
  1.7 2.2 %collective-permute-start.1 = (bf16[256,1024]{1,0:T(8,128)(2,1)S(1)}, bf16[256,1024]{1,0:T(8,128)(2,1)S(1)}, u32[]{:S(2)}, u32[]{:S(2)}) collective-permute-start(bf16[256,1024]{1,0:T(8,128)(2,1)S(1)} %pad_maximum_fusion.refs_0_), channel_id=1, source_target_pairs={{0,32},{8,40},{16,48},{24,56},{32,64},{40,72},{48,80},{56,88},{64,... | collective-permute-start | bytes 1572872 | tf_op jit(solution)/shard_map/ppermute | solution.py:645
  3.9 1.5 %collective-permute-start.3 = (bf16[256,1024]{1,0:T(8,128)(2,1)S(1)}, bf16[256,1024]{1,0:T(8,128)(2,1)S(1)}, u32[]{:S(2)}, u32[]{:S(2)}) collective-permute-start(bf16[256,1024]{1,0:T(8,128)(2,1)S(1)} %pad_maximum_fusion.refs_0_), channel_id=1, source_target_pairs={{0,96},{8,104},{16,112},{24,120},{32,0},{40,8},{48,16},{56,24},{64... | collective-permute-start | bytes 1572872 | tf_op jit(solution)/shard_map/ppermute | solution.py:645
  5.4 1.2 %collective-permute-start.5 = (bf16[256,1024]{1,0:T(8,128)(2,1)S(1)}, bf16[256,1024]{1,0:T(8,128)(2,1)S(1)}, u32[]{:S(2)}, u32[]{:S(2)}) collective-permute-start(bf16[256,1024]{1,0:T(8,128)(2,1)S(1)} %pad_maximum_fusion.refs_0_), channel_id=1, source_target_pairs={{0,16},{8,24},{16,0},{24,8},{32,48},{40,56},{48,32},{56,40},{64,80... | collective-permute-start | bytes 1572872 | tf_op jit(solution)/shard_map/ppermute | solution.py:645
  6.6 3.6 %cut_weights.1 = (bf16[192,1024]{1,0:T(8,128)(2,1)}, bf16[352,1024]{1,0:T(8,128)(2,1)}) custom-call(bf16[1024,3072]{1,0:T(8,128)(2,1)} %w_qkv.3, bf16[1024,2816]{1,0:T(8,128)(2,1)} %wg_in.1, bf16[1024,2816]{1,0:T(8,128)(2,1)} %wu_in.1), custom_call_target="tpu_custom_call" | custom-call | flops 1000000 | bytes 1048 | tf_op jit(solution)/shard_map/cut_weights/pallas_call | solution.py:303
  10.2 7.0 %own_heads.1 = bf16[2048,256]{1,0:T(8,128)(2,1)} custom-call(s32[32]{0:T(128)} %refs_4_.1, bf16[128,1024]{1,0:T(8,128)(2,1)} %bitcast.23, bf16[128,1024]{1,0:T(8,128)(2,1)} %bitcast.19, bf16[1024,3072]{1,0:T(8,128)(2,1)} %w_qkv.3, bf16[1024,3072]{1,0:T(8,128)(2,1)} %w_qkv.3, bf16[1024,3072]{1,0:T(8,128)(2,1)} %w_qkv.3, bf16[1024,1024]{1,0:T(8,128)(2,1)} %w_out.1, ...), custom_call_target="tpu_custom_call" | custom-call | flops 1100000000 | bytes 9437184 | tf_op jit(solution)/shard_map/own_heads/pallas_call | solution.py:170
  17.2 0.0 collective-permute-done.3.refs_4_
  17.2 0.6 collective-permute-done.5.refs_6_
  17.8 6.0 %all-to-all-start = ((bf16[16,128,256]{2,1,0:T(8,128)(2,1)}), bf16[16,128,256]{2,1,0:T(8,128)(2,1)S(1)}, u32[]{:S(2)}, u32[]{:S(2)}) async-start(bf16[16,128,256]{2,1,0:T(8,128)(2,1)} %bitcast.26), calls=%async_computation | async-start | bytes 2097152 | tf_op jit(solution)/shard_map/all_to_all | solution.py:695
  23.8 0.2 collective-permute-start
  24.0 0.4 collective-permute-start.2
  24.4 0.1 collective-permute-start.4
  24.5 0.4 collective-permute-start.6
  25.0 1.5 %collective-permute-start.10 = (bf16[176,1024]{1,0:T(8,128)(2,1)S(1)}, bf16[176,1024]{1,0:T(8,128)(2,1)}, u32[]{:S(2)}, u32[]{:S(2)}) collective-permute-start(bf16[176,1024]{1,0:T(8,128)(2,1)S(1)} %slice.12), channel_id=1, source_target_pairs={{0,32},{8,40},{16,48},{24,56},{32,64},{40,72},{48,80},{56,88},{64,... | collective-permute-start | bytes 1081352 | tf_op jit(solution)/shard_map/ppermute | solution.py:645
  26.5 0.8 pad_maximum_fusion.1
  27.2 1.3 %collective-permute-start.9 = (bf16[176,1024]{1,0:T(8,128)(2,1)S(1)}, bf16[176,1024]{1,0:T(8,128)(2,1)}, u32[]{:S(2)}, u32[]{:S(2)}) collective-permute-start(bf16[176,1024]{1,0:T(8,128)(2,1)S(1)} %slice.12), channel_id=1, source_target_pairs={{0,96},{8,104},{16,112},{24,120},{32,0},{40,8},{48,16},{56,24},{64... | collective-permute-start | bytes 1081352 | tf_op jit(solution)/shard_map/ppermute | solution.py:645
  28.6 1.4 %collective-permute-start.11 = (bf16[160,1024]{1,0:T(8,128)(2,1)}, bf16[160,1024]{1,0:T(8,128)(2,1)}, u32[]{:S(2)}, u32[]{:S(2)}) collective-permute-start(bf16[160,1024]{1,0:T(8,128)(2,1)} %pad_maximum_fusion.1), channel_id=1, source_target_pairs={{0,16},{8,24},{16,0},{24,8},{32,48},{40,56},{48,32},{56,40},{64,80... | collective-permute-start | bytes 983048 | tf_op jit(solution)/shard_map/ppermute | solution.py:645
  29.9 0.0 collective-permute-done.4.refs_5_
  29.9 0.0 collective-permute-start.7
  29.9 0.0 collective-permute-done.6.refs_7_
  30.0 0.8 copy-done.8
  30.7 0.8 copy-done.9
  31.5 1.7 %collective-permute-start.8 = (bf16[256,1024]{1,0:T(8,128)(2,1)S(1)}, bf16[256,1024]{1,0:T(8,128)(2,1)}, u32[]{:S(2)}, u32[]{:S(2)}) collective-permute-start(bf16[256,1024]{1,0:T(8,128)(2,1)S(1)} %collective-permute-done.3.refs_4_), channel_id=1, source_target_pairs={{0,112},{8,120},{16,96},{24,104},{32,16},{40,24},{48,0},{56,8},{64... | collective-permute-start | bytes 1572872 | tf_op jit(solution)/shard_map/ppermute | solution.py:645
  33.3 7.3 %first_half.1 = (bf16[1024,1024]{1,0:T(8,128)(2,1)}, bf16[176,1024]{1,0:T(8,128)(2,1)}, bf16[352,1024]{1,0:T(8,128)(2,1)}, f32[352,128]{1,0:T(8,128)}) custom-call(bf16[256,1024]{1,0:T(8,128)(2,1)} %copy-done.1, bf16[256,1024]{1,0:T(8,128)(2,1)} %copy-done.6, bf16[256,1024]{1,0:T(8,128)(2,1)} %copy-done.4, bf16[256,1024]{1,0:T(8,128)(2,1)} %copy-done.7, ...), custom_call_target="tpu_custom_call" | custom-call | flops 1000000 | bytes 1048 | tf_op jit(solution)/shard_map/first_half/pallas_call | solution.py:385
  40.6 0.0 all-to-all-done
  40.6 1.0 copy-done.3
  41.6 10.9 %attention.1.refs_18_ = bf16[2048,256]{1,0:T(8,128)(2,1)} custom-call(bf16[1024,1024]{1,0:T(8,128)(2,1)} %get-tuple-element.59.refs_0_.refs_24_, bf16[176,1024]{1,0:T(8,128)(2,1)} %get-tuple-element.60.refs_1_.refs_25_, bf16[352,1024]{1,0:T(8,128)(2,1)} %get-tuple-element.61.refs_2_.refs_26_, f32[352,128]{1,0:T(8,128)} %get-tuple-element.62.refs_3_.refs_27_, ...), custom_call_target="tpu_custom_call" | custom-call | flops 15000000512 | bytes 8388608 | tf_op jit(solution)/shard_map/attention/pallas_call | solution.py:259
  52.5 5.2 %collective-permute-done.7.refs_8_ = bf16[256,1024]{1,0:T(8,128)(2,1)} collective-permute-done((bf16[256,1024]{1,0:T(8,128)(2,1)S(1)}, bf16[256,1024]{1,0:T(8,128)(2,1)}, u32[]{:S(2)}, u32[]{:S(2)}) %collective-permute-start.7) | collective-permute-done | bytes 524320 | tf_op jit(solution)/shard_map/ppermute | solution.py:645
  57.7 0.9 collective-permute-start.12
  58.6 0.0 collective-permute-start.13
  58.6 0.5 collective-permute-start.14
  59.1 0.0 collective-permute-start.15
  59.1 0.5 collective-permute-start.16
  59.6 3.8 %all-to-all-start.1 = ((bf16[16,128,256]{2,1,0:T(8,128)(2,1)}), bf16[16,128,256]{2,1,0:T(8,128)(2,1)S(1)}, u32[]{:S(2)}, u32[]{:S(2)}) async-start(bf16[16,128,256]{2,1,0:T(8,128)(2,1)} %bitcast.28), calls=%async_computation.1 | async-start | bytes 2097152 | tf_op jit(solution)/shard_map/all_to_all | solution.py:706
  63.5 0.6 copy-done.14
  64.2 0.1 copy-done.12
  64.3 0.1 copy-done.13
  64.4 0.2 copy-done.10
  64.6 0.2 copy-done.11
  64.8 13.2 %weight_grads.1 = bf16[8,832,128]{2,1,0:T(8,128)(2,1)} custom-call(bf16[256,1024]{1,0:T(8,128)(2,1)} %copy-done.1, bf16[256,1024]{1,0:T(8,128)(2,1)} %copy-done.6, bf16[256,1024]{1,0:T(8,128)(2,1)} %copy-done.4, bf16[256,1024]{1,0:T(8,128)(2,1)} %copy-done.7, bf16[256,1024]{1,0:T(8,128)(2,1)} %copy-done.5, bf16[256,1024]{1,0:T(8,128)(2,1)} %copy-done.8, ...), custom_call_target="tpu_custom_call" | custom-call | flops 8000000000 | bytes 20971520 | tf_op jit(solution)/shard_map/weight_grads/pallas_call | solution.py:495
  78.0 1.3 %all-to-all-done.1 = bf16[16,128,256]{2,1,0:T(8,128)(2,1)S(1)} async-done(((bf16[16,128,256]{2,1,0:T(8,128)(2,1)}), bf16[16,128,256]{2,1,0:T(8,128)(2,1)S(1)}, u32[]{:S(2)}, u32[]{:S(2)}) %all-to-all-start.1) | async-done | bytes 1048608 | tf_op jit(solution)/shard_map/all_to_all | solution.py:706
  79.3 7.2 %all-to-all-start.2 = ((bf16[8,832,128]{2,1,0:T(8,128)(2,1)}), bf16[8,832,128]{2,1,0:T(8,128)(2,1)S(1)}, u32[]{:S(2)}, u32[]{:S(2)}) async-start(bf16[8,832,128]{2,1,0:T(8,128)(2,1)} %weight_grads.1), calls=%async_computation.2 | async-start | bytes 3407872 | tf_op jit(solution)/shard_map/all_to_all | solution.py:712
  86.5 12.1 %own_rows.1 = (f32[128,1024]{1,0:T(8,128)}, f32[128,1024]{1,0:T(8,128)}) custom-call(bf16[128,1024]{1,0:T(8,128)(2,1)} %bitcast.24, bf16[128,1024]{1,0:T(8,128)(2,1)} %bitcast.20, f32[1,1024]{1,0:T(1,128)} %bitcast.36, f32[1,1024]{1,0:T(1,128)} %bitcast.41, bf16[1024,2816]{1,0:T(8,128)(2,1)} %wg_in.1, bf16[1024,2816]{1,0:T(8,128)(2,1)} %wu_in.1, ...), custom_call_target="tpu_custom_call" | custom-call | flops 4499999744 | bytes 18874368 | tf_op jit(solution)/shard_map/own_rows/pallas_call | solution.py:113
  98.5 8.0 %final_rows.1 = (bf16[128,1024]{1,0:T(8,128)(2,1)}, bf16[128,1024]{1,0:T(8,128)(2,1)}) custom-call(bf16[2048,256]{1,0:T(8,128)(2,1)} %bitcast.27, bf16[128,1024]{1,0:T(8,128)(2,1)} %bitcast.25, bf16[128,1024]{1,0:T(8,128)(2,1)} %bitcast.21, f32[128,1024]{1,0:T(8,128)} %get-tuple-element.66.part, f32[128,1024]{1,0:T(8,128)} %get-tuple-element.67.grad, ...), custom_call_target="tpu_custom_call" | custom-call | flops 1100000000 | bytes 10485760 | tf_op jit(solution)/shard_map/final_rows/pallas_call | solution.py:552
  106.5 1.8 %all-to-all-done.2.got = bf16[8,832,128]{2,1,0:T(8,128)(2,1)S(1)} async-done(((bf16[8,832,128]{2,1,0:T(8,128)(2,1)}), bf16[8,832,128]{2,1,0:T(8,128)(2,1)S(1)}, u32[]{:S(2)}, u32[]{:S(2)}) %all-to-all-start.2) | async-done | bytes 1703968 | tf_op jit(solution)/shard_map/all_to_all | solution.py:712
  108.3 1.0 sum_rows.1
  109.3 11.0 %all_to_all.39 = bf16[16,8,640]{2,1,0:T(8,128)(2,1)S(1)} all-to-all(bf16[16,8,640]{2,1,0:T(8,128)(2,1)S(1)} %bitcast.17), channel_id=1, replica_groups=mesh['seq'=16,'rows'=8] {'seq'}, dimensions={0} | all-to-all | bytes 327680 | tf_op jit(solution)/shard_map/all_to_all | solution.py:718
  120.3 0.8 last_layout.1
  (37 shorter events, 0.1 us)
Async XLA Ops:
  1.7 22.1 %copy-start.1 = (bf16[256,1024]{1,0:T(8,128)(2,1)}, bf16[256,1024]{1,0:T(8,128)(2,1)S(1)}, u32[]{:S(2)}) copy-start(bf16[256,1024]{1,0:T(8,128)(2,1)S(1)} %pad_maximum_fusion.refs_0_) | copy-start | bytes 1572868
  1.7 15.5 %collective-permute-start.1 = (bf16[256,1024]{1,0:T(8,128)(2,1)S(1)}, bf16[256,1024]{1,0:T(8,128)(2,1)S(1)}, u32[]{:S(2)}, u32[]{:S(2)}) collective-permute-start(bf16[256,1024]{1,0:T(8,128)(2,1)S(1)} %pad_maximum_fusion.refs_0_), channel_id=1, source_target_pairs={{0,32},{8,40},{16,48},{24,56},{32,64},{40,72},{48,80},{56,88},{64,... | collective-permute-start | bytes 1572872 | tf_op jit(solution)/shard_map/ppermute | solution.py:645
  3.9 13.3 %collective-permute-start.3 = (bf16[256,1024]{1,0:T(8,128)(2,1)S(1)}, bf16[256,1024]{1,0:T(8,128)(2,1)S(1)}, u32[]{:S(2)}, u32[]{:S(2)}) collective-permute-start(bf16[256,1024]{1,0:T(8,128)(2,1)S(1)} %pad_maximum_fusion.refs_0_), channel_id=1, source_target_pairs={{0,96},{8,104},{16,112},{24,120},{32,0},{40,8},{48,16},{56,24},{64... | collective-permute-start | bytes 1572872 | tf_op jit(solution)/shard_map/ppermute | solution.py:645
  5.4 12.4 %collective-permute-start.5 = (bf16[256,1024]{1,0:T(8,128)(2,1)S(1)}, bf16[256,1024]{1,0:T(8,128)(2,1)S(1)}, u32[]{:S(2)}, u32[]{:S(2)}) collective-permute-start(bf16[256,1024]{1,0:T(8,128)(2,1)S(1)} %pad_maximum_fusion.refs_0_), channel_id=1, source_target_pairs={{0,16},{8,24},{16,0},{24,8},{32,48},{40,56},{48,32},{56,40},{64,80... | collective-permute-start | bytes 1572872 | tf_op jit(solution)/shard_map/ppermute | solution.py:645
  17.2 16.0 %copy-start.4 = (bf16[256,1024]{1,0:T(8,128)(2,1)}, bf16[256,1024]{1,0:T(8,128)(2,1)S(1)}, u32[]{:S(2)}) copy-start(bf16[256,1024]{1,0:T(8,128)(2,1)S(1)} %collective-permute-done.1.refs_2_) | copy-start | bytes 1572868
  17.2 16.0 %copy-start.5 = (bf16[256,1024]{1,0:T(8,128)(2,1)}, bf16[256,1024]{1,0:T(8,128)(2,1)S(1)}, u32[]{:S(2)}) copy-start(bf16[256,1024]{1,0:T(8,128)(2,1)S(1)} %collective-permute-done.3.refs_4_) | copy-start | bytes 1572868
  17.8 15.4 %copy-start.2 = (bf16[256,1024]{1,0:T(8,128)(2,1)}, bf16[256,1024]{1,0:T(8,128)(2,1)S(1)}, u32[]{:S(2)}) copy-start(bf16[256,1024]{1,0:T(8,128)(2,1)S(1)} %collective-permute-done.5.refs_6_) | copy-start | bytes 1572868
  17.8 22.7 %all-to-all-start = ((bf16[16,128,256]{2,1,0:T(8,128)(2,1)}), bf16[16,128,256]{2,1,0:T(8,128)(2,1)S(1)}, u32[]{:S(2)}, u32[]{:S(2)}) async-start(bf16[16,128,256]{2,1,0:T(8,128)(2,1)} %bitcast.26), calls=%async_computation | async-start | bytes 2097152 | tf_op jit(solution)/shard_map/all_to_all | solution.py:695
  23.8 3.4 %collective-permute-start = (bf16[256,1024]{1,0:T(8,128)(2,1)S(1)}, bf16[256,1024]{1,0:T(8,128)(2,1)S(1)}, u32[]{:S(2)}, u32[]{:S(2)}) collective-permute-start(bf16[256,1024]{1,0:T(8,128)(2,1)S(1)} %pad_maximum_fusion.refs_0_), channel_id=1, source_target_pairs={{0,8},{8,0},{16,24},{24,16},{32,40},{40,32},{48,56},{56,48},{64,72... | collective-permute-start | bytes 1572872 | tf_op jit(solution)/shard_map/ppermute | solution.py:645
  24.0 4.5 %collective-permute-start.2 = (bf16[256,1024]{1,0:T(8,128)(2,1)S(1)}, bf16[256,1024]{1,0:T(8,128)(2,1)S(1)}, u32[]{:S(2)}, u32[]{:S(2)}) collective-permute-start(bf16[256,1024]{1,0:T(8,128)(2,1)S(1)} %collective-permute-done.1.refs_2_), channel_id=1, source_target_pairs={{0,8},{8,0},{16,24},{24,16},{32,40},{40,32},{48,56},{56,48},{64,72... | collective-permute-start | bytes 1572872 | tf_op jit(solution)/shard_map/ppermute | solution.py:645
  24.4 5.5 %collective-permute-start.4 = (bf16[256,1024]{1,0:T(8,128)(2,1)S(1)}, bf16[256,1024]{1,0:T(8,128)(2,1)S(1)}, u32[]{:S(2)}, u32[]{:S(2)}) collective-permute-start(bf16[256,1024]{1,0:T(8,128)(2,1)S(1)} %collective-permute-done.3.refs_4_), channel_id=1, source_target_pairs={{0,8},{8,0},{16,24},{24,16},{32,40},{40,32},{48,56},{56,48},{64,72... | collective-permute-start | bytes 1572872 | tf_op jit(solution)/shard_map/ppermute | solution.py:645
  24.5 5.4 %collective-permute-start.6 = (bf16[256,1024]{1,0:T(8,128)(2,1)S(1)}, bf16[256,1024]{1,0:T(8,128)(2,1)S(1)}, u32[]{:S(2)}, u32[]{:S(2)}) collective-permute-start(bf16[256,1024]{1,0:T(8,128)(2,1)S(1)} %collective-permute-done.5.refs_6_), channel_id=1, source_target_pairs={{0,8},{8,0},{16,24},{24,16},{32,40},{40,32},{48,56},{56,48},{64,72... | collective-permute-start | bytes 1572872 | tf_op jit(solution)/shard_map/ppermute | solution.py:645
  25.0 27.5 %collective-permute-start.10 = (bf16[176,1024]{1,0:T(8,128)(2,1)S(1)}, bf16[176,1024]{1,0:T(8,128)(2,1)}, u32[]{:S(2)}, u32[]{:S(2)}) collective-permute-start(bf16[176,1024]{1,0:T(8,128)(2,1)S(1)} %slice.12), channel_id=1, source_target_pairs={{0,32},{8,40},{16,48},{24,56},{32,64},{40,72},{48,80},{56,88},{64,... | collective-permute-start | bytes 1081352 | tf_op jit(solution)/shard_map/ppermute | solution.py:645
  27.2 6.0 %copy-start.6 = (bf16[256,1024]{1,0:T(8,128)(2,1)}, bf16[256,1024]{1,0:T(8,128)(2,1)S(1)}, u32[]{:S(2)}) copy-start(bf16[256,1024]{1,0:T(8,128)(2,1)S(1)} %collective-permute-done.refs_1_) | copy-start | bytes 1572868
  27.2 25.2 %collective-permute-start.9 = (bf16[176,1024]{1,0:T(8,128)(2,1)S(1)}, bf16[176,1024]{1,0:T(8,128)(2,1)}, u32[]{:S(2)}, u32[]{:S(2)}) collective-permute-start(bf16[176,1024]{1,0:T(8,128)(2,1)S(1)} %slice.12), channel_id=1, source_target_pairs={{0,96},{8,104},{16,112},{24,120},{32,0},{40,8},{48,16},{56,24},{64... | collective-permute-start | bytes 1081352 | tf_op jit(solution)/shard_map/ppermute | solution.py:645
  28.6 1.4 %copy-start.7 = (bf16[256,1024]{1,0:T(8,128)(2,1)}, bf16[256,1024]{1,0:T(8,128)(2,1)S(1)}, u32[]{:S(2)}) copy-start(bf16[256,1024]{1,0:T(8,128)(2,1)S(1)} %collective-permute-done.2.refs_3_) | copy-start | bytes 1572868
  28.6 23.9 %collective-permute-start.11 = (bf16[160,1024]{1,0:T(8,128)(2,1)}, bf16[160,1024]{1,0:T(8,128)(2,1)}, u32[]{:S(2)}, u32[]{:S(2)}) collective-permute-start(bf16[160,1024]{1,0:T(8,128)(2,1)} %pad_maximum_fusion.1), channel_id=1, source_target_pairs={{0,16},{8,24},{16,0},{24,8},{32,48},{40,56},{48,32},{56,40},{64,80... | collective-permute-start | bytes 983048 | tf_op jit(solution)/shard_map/ppermute | solution.py:645
  29.9 0.8 copy-start.8
  29.9 27.8 %collective-permute-start.7 = (bf16[256,1024]{1,0:T(8,128)(2,1)S(1)}, bf16[256,1024]{1,0:T(8,128)(2,1)}, u32[]{:S(2)}, u32[]{:S(2)}) collective-permute-start(bf16[256,1024]{1,0:T(8,128)(2,1)S(1)} %collective-permute-done.1.refs_2_), channel_id=1, source_target_pairs={{0,32},{8,40},{16,48},{24,56},{32,64},{40,72},{48,80},{56,88},{64,... | collective-permute-start | bytes 1572872 | tf_op jit(solution)/shard_map/ppermute | solution.py:645
  30.7 0.8 copy-start.9
  31.5 26.2 %collective-permute-start.8 = (bf16[256,1024]{1,0:T(8,128)(2,1)S(1)}, bf16[256,1024]{1,0:T(8,128)(2,1)}, u32[]{:S(2)}, u32[]{:S(2)}) collective-permute-start(bf16[256,1024]{1,0:T(8,128)(2,1)S(1)} %collective-permute-done.3.refs_4_), channel_id=1, source_target_pairs={{0,112},{8,120},{16,96},{24,104},{32,16},{40,24},{48,0},{56,8},{64... | collective-permute-start | bytes 1572872 | tf_op jit(solution)/shard_map/ppermute | solution.py:645
  40.6 1.0 copy-start.3
  57.7 5.8 %collective-permute-start.12 = (bf16[256,1024]{1,0:T(8,128)(2,1)}, bf16[256,1024]{1,0:T(8,128)(2,1)S(1)}, u32[]{:S(2)}, u32[]{:S(2)}) collective-permute-start(bf16[256,1024]{1,0:T(8,128)(2,1)} %collective-permute-done.7.refs_8_), channel_id=1, source_target_pairs={{0,8},{8,0},{16,24},{24,16},{32,40},{40,32},{48,56},{56,48},{64,72... | collective-permute-start | bytes 1572872 | tf_op jit(solution)/shard_map/ppermute | solution.py:645
  58.6 4.9 %collective-permute-start.13 = (bf16[256,1024]{1,0:T(8,128)(2,1)}, bf16[256,1024]{1,0:T(8,128)(2,1)S(1)}, u32[]{:S(2)}, u32[]{:S(2)}) collective-permute-start(bf16[256,1024]{1,0:T(8,128)(2,1)} %collective-permute-done.8.refs_10_), channel_id=1, source_target_pairs={{0,8},{8,0},{16,24},{24,16},{32,40},{40,32},{48,56},{56,48},{64,72... | collective-permute-start | bytes 1572872 | tf_op jit(solution)/shard_map/ppermute | solution.py:645
  58.6 4.9 %collective-permute-start.14 = (bf16[176,1024]{1,0:T(8,128)(2,1)}, bf16[176,1024]{1,0:T(8,128)(2,1)S(1)}, u32[]{:S(2)}, u32[]{:S(2)}) collective-permute-start(bf16[176,1024]{1,0:T(8,128)(2,1)} %collective-permute-done.9.refs_12_), channel_id=1, source_target_pairs={{0,8},{8,0},{16,24},{24,16},{32,40},{40,32},{48,56},{56,48},{64,72... | collective-permute-start | bytes 1081352 | tf_op jit(solution)/shard_map/ppermute | solution.py:645
  59.1 4.4 %collective-permute-start.15 = (bf16[176,1024]{1,0:T(8,128)(2,1)}, bf16[176,1024]{1,0:T(8,128)(2,1)S(1)}, u32[]{:S(2)}, u32[]{:S(2)}) collective-permute-start(bf16[176,1024]{1,0:T(8,128)(2,1)} %collective-permute-done.10.refs_14_), channel_id=1, source_target_pairs={{0,8},{8,0},{16,24},{24,16},{32,40},{40,32},{48,56},{56,48},{64,72... | collective-permute-start | bytes 1081352 | tf_op jit(solution)/shard_map/ppermute | solution.py:645
  59.1 4.3 %collective-permute-start.16 = (bf16[160,1024]{1,0:T(8,128)(2,1)}, bf16[160,1024]{1,0:T(8,128)(2,1)S(1)}, u32[]{:S(2)}, u32[]{:S(2)}) collective-permute-start(bf16[160,1024]{1,0:T(8,128)(2,1)} %collective-permute-done.11.refs_16_), channel_id=1, source_target_pairs={{0,8},{8,0},{16,24},{24,16},{32,40},{40,32},{48,56},{56,48},{64,72... | collective-permute-start | bytes 983048 | tf_op jit(solution)/shard_map/ppermute | solution.py:645
  59.6 19.6 %all-to-all-start.1 = ((bf16[16,128,256]{2,1,0:T(8,128)(2,1)}), bf16[16,128,256]{2,1,0:T(8,128)(2,1)S(1)}, u32[]{:S(2)}, u32[]{:S(2)}) async-start(bf16[16,128,256]{2,1,0:T(8,128)(2,1)} %bitcast.28), calls=%async_computation.1 | async-start | bytes 2097152 | tf_op jit(solution)/shard_map/all_to_all | solution.py:706
  63.4 0.7 copy-start.14
  63.4 0.8 copy-start.12
  63.5 0.9 copy-start.13
  63.5 1.1 copy-start.10
  63.5 1.3 %copy-start.11 = (bf16[256,1024]{1,0:T(8,128)(2,1)}, bf16[256,1024]{1,0:T(8,128)(2,1)S(1)}, u32[]{:S(2)}) copy-start(bf16[256,1024]{1,0:T(8,128)(2,1)S(1)} %collective-permute-done.13.refs_11_) | copy-start | bytes 1572868
  79.2 19.3 %copy-start = (bf16[16,128,256]{2,1,0:T(8,128)(2,1)}, bf16[16,128,256]{2,1,0:T(8,128)(2,1)S(1)}, u32[]{:S(2)}) copy-start(bf16[16,128,256]{2,1,0:T(8,128)(2,1)S(1)} %all-to-all-done.1) | copy-start | bytes 3145732
  79.3 29.1 %all-to-all-start.2 = ((bf16[8,832,128]{2,1,0:T(8,128)(2,1)}), bf16[8,832,128]{2,1,0:T(8,128)(2,1)S(1)}, u32[]{:S(2)}, u32[]{:S(2)}) async-start(bf16[8,832,128]{2,1,0:T(8,128)(2,1)} %weight_grads.1), calls=%async_computation.2 | async-start | bytes 3407872 | tf_op jit(solution)/shard_map/all_to_all | solution.py:712

commit v4 on v3

--- a/solution.py
+++ b/solution.py
@@ -650,7 +650,7 @@
     below = send(own, UP)
     above = send(own, DOWN)
     pair = send(own, PAIR)
-    late = exchange((below, above, pair))
+    late = exchange(below)
     far = send(below, UP)
     opposite = send(above, DOWN_PAIR)
     most = pair[:MOST]
@@ -691,7 +691,7 @@
     w_qkv_s, w_gu_s = cut_weights(w_qkv, w_gate, w_up)
 
     def exchange(first):
-        ready, _ = lax.optimization_barrier((packed, (first, w_gu_s)))
+        ready, _ = lax.optimization_barrier((packed, first))
         return lax.all_to_all(ready, "seq", 0, 0, tiled=True)
 
     def attend(packed_here, early, arrays):
@@ -699,8 +699,7 @@
             early, pieces_of(len(early)), w_gu_s, w_down, gain, bias
         )
         heads = attention(order, packed_here, first)
-        (heads, first), arrays = lax.optimization_barrier(((heads, first), arrays))
-        return (heads, first), arrays
+        return (heads, first), [lax.optimization_barrier((heads, a))[1] for a in arrays]
 
     early, arrays, (heads, first) = gather(x, dy, exchange, attend)
     heads_here = lax.all_to_all(heads, "seq", 0, 0, tiled=True)

time: 122 us -> 120 us (0.984)
  local copies, waits for them, and re-layouts: 3.89 us -> 2.29 us
    unnamed x30 -> x24, local copies, waits for them, and re-layouts: 3.84 us -> 2.24 us
  transfers between devices with their start and end apart: 20 -> 20, of which waited for: 4 -> 5; matrix products, arithmetic and copies ran while one was open for 1% -> 1% of each run, Pallas kernels for 51% -> 52%
where the time goes in v4:
time: 120 us
  Pallas kernels  63.8 us (53%)
  starting transfers between devices  31.5 us (26%)
  blocking collectives  10.9 us (9%)
  waiting for transfers between devices  8.26 us (7%)
  local copies, waits for them, and re-layouts  2.29 us (2%)
  other arithmetic  1.83 us (2%)
    ppermute x17, starting transfers between devices, send(): return lax.ppermute(value, 'seq', to)  14.7 us
    pallas_call x1, Pallas kernels, weight_grads(): pl.pallas_call(lambda *refs: weights_kernel(pieces, len(arrays), *refs),...  13.2 us
    pallas_call x1, Pallas kernels, own_rows(): pl.pallas_call(own_kernel, out_shape=[jax.ShapeDtypeStruct((HERE, WIDTH),...  12.1 us
    all_to_all x1, blocking collectives, shards(): mine = lax.all_to_all(outgoing, 'seq', 0, 0, tiled=True)  10.9 us
    pallas_call x1, Pallas kernels, attention(): pl.pallas_call(attention_kernel, out_shape=jax.ShapeDtypeStruct((LENGTH,...  10.9 us
    pallas_call x1, Pallas kernels, final_rows(): pl.pallas_call(final_kernel, grid=(WIDTH // BLOCK,), out_shape=[jax.Shape...  8.02 us
    pallas_call x1, Pallas kernels, first_half(): pl.pallas_call(lambda *refs: first_kernel(pieces, len(arrays), *refs), ou...  7.3 us
    all_to_all x1, starting transfers between devices, shards(): got = lax.all_to_all(block, 'rows', 0, 0, tiled=True)  7.2 us
  transfers between devices with their start and end apart: 20, of which 5 were waited for; matrix products, arithmetic and copies ran while one was open for 1% of the time, Pallas kernels for 52%

profile of v4, /device:TPU:1, one launch (start us, length us, event | category | flops | bytes accessed | tf_op | source)
XLA Modules:
  0.0 119.5 jit_solution(15488494930658220136)
XLA Ops:
  0.6 1.1 pad_maximum_fusion.refs_0_
  1.7 2.2 %collective-permute-start.1 = (bf16[256,1024]{1,0:T(8,128)(2,1)S(1)}, bf16[256,1024]{1,0:T(8,128)(2,1)S(1)}, u32[]{:S(2)}, u32[]{:S(2)}) collective-permute-start(bf16[256,1024]{1,0:T(8,128)(2,1)S(1)} %pad_maximum_fusion.refs_0_), channel_id=1, source_target_pairs={{0,32},{8,40},{16,48},{24,56},{32,64},{40,72},{48,80},{56,88},{64,... | collective-permute-start | bytes 1572872 | tf_op jit(solution)/shard_map/ppermute | solution.py:645
  3.9 1.5 %collective-permute-start.3 = (bf16[256,1024]{1,0:T(8,128)(2,1)S(1)}, bf16[256,1024]{1,0:T(8,128)(2,1)S(1)}, u32[]{:S(2)}, u32[]{:S(2)}) collective-permute-start(bf16[256,1024]{1,0:T(8,128)(2,1)S(1)} %pad_maximum_fusion.refs_0_), channel_id=1, source_target_pairs={{0,96},{8,104},{16,112},{24,120},{32,0},{40,8},{48,16},{56,24},{64... | collective-permute-start | bytes 1572872 | tf_op jit(solution)/shard_map/ppermute | solution.py:645
  5.4 1.2 %collective-permute-start.5 = (bf16[256,1024]{1,0:T(8,128)(2,1)S(1)}, bf16[256,1024]{1,0:T(8,128)(2,1)S(1)}, u32[]{:S(2)}, u32[]{:S(2)}) collective-permute-start(bf16[256,1024]{1,0:T(8,128)(2,1)S(1)} %pad_maximum_fusion.refs_0_), channel_id=1, source_target_pairs={{0,16},{8,24},{16,0},{24,8},{32,48},{40,56},{48,32},{56,40},{64,80... | collective-permute-start | bytes 1572872 | tf_op jit(solution)/shard_map/ppermute | solution.py:645
  6.6 6.9 %own_heads.1 = bf16[2048,256]{1,0:T(8,128)(2,1)} custom-call(s32[32]{0:T(128)} %refs_4_.1, bf16[128,1024]{1,0:T(8,128)(2,1)} %bitcast.23, bf16[128,1024]{1,0:T(8,128)(2,1)} %bitcast.19, bf16[1024,3072]{1,0:T(8,128)(2,1)} %w_qkv.3, bf16[1024,3072]{1,0:T(8,128)(2,1)} %w_qkv.3, bf16[1024,3072]{1,0:T(8,128)(2,1)} %w_qkv.3, bf16[1024,1024]{1,0:T(8,128)(2,1)} %w_out.1, ...), custom_call_target="tpu_custom_call" | custom-call | flops 1100000000 | bytes 9437184 | tf_op jit(solution)/shard_map/own_heads/pallas_call | solution.py:170
  13.6 3.3 %collective-permute-done.1.refs_2_ = bf16[256,1024]{1,0:T(8,128)(2,1)S(1)} collective-permute-done((bf16[256,1024]{1,0:T(8,128)(2,1)S(1)}, bf16[256,1024]{1,0:T(8,128)(2,1)S(1)}, u32[]{:S(2)}, u32[]{:S(2)}) %collective-permute-start.1) | collective-permute-done | bytes 524320 | tf_op jit(solution)/shard_map/ppermute | solution.py:645
  16.9 5.5 %all-to-all-start = ((bf16[16,128,256]{2,1,0:T(8,128)(2,1)}), bf16[16,128,256]{2,1,0:T(8,128)(2,1)S(1)}, u32[]{:S(2)}, u32[]{:S(2)}) async-start(bf16[16,128,256]{2,1,0:T(8,128)(2,1)} %bitcast.26), calls=%async_computation | async-start | bytes 2097152 | tf_op jit(solution)/shard_map/all_to_all | solution.py:695
  22.4 0.2 collective-permute-start
  22.6 0.4 collective-permute-start.2
  23.0 0.0 collective-permute-done.3.refs_4_
  23.0 0.1 collective-permute-start.4
  23.1 0.0 collective-permute-done.5.refs_6_
  23.1 0.4 collective-permute-start.6
  23.5 3.6 %cut_weights.1 = (bf16[192,1024]{1,0:T(8,128)(2,1)}, bf16[352,1024]{1,0:T(8,128)(2,1)}) custom-call(bf16[1024,3072]{1,0:T(8,128)(2,1)} %w_qkv.3, bf16[1024,2816]{1,0:T(8,128)(2,1)} %wg_in.1, bf16[1024,2816]{1,0:T(8,128)(2,1)} %wu_in.1), custom_call_target="tpu_custom_call" | custom-call | flops 1000000 | bytes 1048 | tf_op jit(solution)/shard_map/cut_weights/pallas_call | solution.py:303
  27.1 2.7 %collective-permute-start.11 = (bf16[176,1024]{1,0:T(8,128)(2,1)S(1)}, bf16[176,1024]{1,0:T(8,128)(2,1)}, u32[]{:S(2)}, u32[]{:S(2)}) collective-permute-start(bf16[176,1024]{1,0:T(8,128)(2,1)S(1)} %slice.12), channel_id=1, source_target_pairs={{0,96},{8,104},{16,112},{24,120},{32,0},{40,8},{48,16},{56,24},{64... | collective-permute-start | bytes 1081352 | tf_op jit(solution)/shard_map/ppermute | solution.py:645
  29.9 0.8 pad_maximum_fusion.1
  30.6 0.0 collective-permute-done.refs_1_
  30.6 0.0 collective-permute-start.13
  30.7 1.3 %collective-permute-start.15 = (bf16[160,1024]{1,0:T(8,128)(2,1)}, bf16[160,1024]{1,0:T(8,128)(2,1)}, u32[]{:S(2)}, u32[]{:S(2)}) collective-permute-start(bf16[160,1024]{1,0:T(8,128)(2,1)} %pad_maximum_fusion.1), channel_id=1, source_target_pairs={{0,16},{8,24},{16,0},{24,8},{32,48},{40,56},{48,32},{56,40},{64,80... | collective-permute-start | bytes 983048 | tf_op jit(solution)/shard_map/ppermute | solution.py:645
  31.9 0.0 collective-permute-done.4.refs_5_
  31.9 2.6 %collective-permute-start.9 = (bf16[256,1024]{1,0:T(8,128)(2,1)S(1)}, bf16[256,1024]{1,0:T(8,128)(2,1)}, u32[]{:S(2)}, u32[]{:S(2)}) collective-permute-start(bf16[256,1024]{1,0:T(8,128)(2,1)S(1)} %collective-permute-done.3.refs_4_), channel_id=1, source_target_pairs={{0,112},{8,120},{16,96},{24,104},{32,16},{40,24},{48,0},{56,8},{64... | collective-permute-start | bytes 1572872 | tf_op jit(solution)/shard_map/ppermute | solution.py:645
  34.5 0.0 collective-permute-done.6.refs_7_
  34.5 0.0 collective-permute-start.7
  34.5 7.3 %first_half.1 = (bf16[1024,1024]{1,0:T(8,128)(2,1)}, bf16[176,1024]{1,0:T(8,128)(2,1)}, bf16[352,1024]{1,0:T(8,128)(2,1)}, f32[352,128]{1,0:T(8,128)}) custom-call(bf16[256,1024]{1,0:T(8,128)(2,1)} %copy-done.1, bf16[256,1024]{1,0:T(8,128)(2,1)} %copy-done.6, bf16[256,1024]{1,0:T(8,128)(2,1)} %copy-done.4, bf16[256,1024]{1,0:T(8,128)(2,1)} %collective-permute-done.2.refs_3_, ...), custom_call_target="tpu_custom_call" | custom-call | flops 1000000 | bytes 1048 | tf_op jit(solution)/shard_map/first_half/pallas_call | solution.py:385
  41.9 1.0 copy-done.3
  42.8 10.9 %attention.1.refs_18_ = bf16[2048,256]{1,0:T(8,128)(2,1)} custom-call(bf16[1024,1024]{1,0:T(8,128)(2,1)} %get-tuple-element.42.refs_0_.refs_24_, bf16[176,1024]{1,0:T(8,128)(2,1)} %get-tuple-element.43.refs_1_.refs_25_, bf16[352,1024]{1,0:T(8,128)(2,1)} %get-tuple-element.44.refs_2_.refs_26_, f32[352,128]{1,0:T(8,128)} %get-tuple-element.45.refs_3_.refs_27_, ...), custom_call_target="tpu_custom_call" | custom-call | flops 15000000512 | bytes 8388608 | tf_op jit(solution)/shard_map/attention/pallas_call | solution.py:259
  53.8 1.6 %collective-permute-done.9.refs_10_ = bf16[256,1024]{1,0:T(8,128)(2,1)} collective-permute-done((bf16[256,1024]{1,0:T(8,128)(2,1)S(1)}, bf16[256,1024]{1,0:T(8,128)(2,1)}, u32[]{:S(2)}, u32[]{:S(2)}) %collective-permute-start.9) | collective-permute-done | bytes 524320 | tf_op jit(solution)/shard_map/ppermute | solution.py:645
  55.3 0.9 collective-permute-start.10
  56.2 0.2 collective-permute-done.7.refs_8_
  56.4 0.7 collective-permute-start.8
  57.1 0.0 collective-permute-start.12
  57.1 0.5 collective-permute-start.14
  57.6 0.1 collective-permute-start.16
  57.7 4.1 %all-to-all-start.1 = ((bf16[16,128,256]{2,1,0:T(8,128)(2,1)}), bf16[16,128,256]{2,1,0:T(8,128)(2,1)S(1)}, u32[]{:S(2)}, u32[]{:S(2)}) async-start(bf16[16,128,256]{2,1,0:T(8,128)(2,1)} %bitcast.28), calls=%async_computation.1 | async-start | bytes 2097152 | tf_op jit(solution)/shard_map/all_to_all | solution.py:705
  61.9 0.6 copy-done.11
  62.5 0.1 copy-done.9
  62.7 0.1 copy-done.10
  62.8 0.2 copy-done.7
  63.0 0.2 copy-done.8
  63.1 13.2 %weight_grads.1 = bf16[8,832,128]{2,1,0:T(8,128)(2,1)} custom-call(bf16[256,1024]{1,0:T(8,128)(2,1)} %copy-done.1, bf16[256,1024]{1,0:T(8,128)(2,1)} %copy-done.6, bf16[256,1024]{1,0:T(8,128)(2,1)} %copy-done.4, bf16[256,1024]{1,0:T(8,128)(2,1)} %collective-permute-done.2.refs_3_, bf16[256,1024]{1,0:T(8,128)(2,1)} %copy-done.5, ...), custom_call_target="tpu_custom_call" | custom-call | flops 8000000000 | bytes 20971520 | tf_op jit(solution)/shard_map/weight_grads/pallas_call | solution.py:495
  76.4 1.4 %all-to-all-done.1 = bf16[16,128,256]{2,1,0:T(8,128)(2,1)S(1)} async-done(((bf16[16,128,256]{2,1,0:T(8,128)(2,1)}), bf16[16,128,256]{2,1,0:T(8,128)(2,1)S(1)}, u32[]{:S(2)}, u32[]{:S(2)}) %all-to-all-start.1) | async-done | bytes 1048608 | tf_op jit(solution)/shard_map/all_to_all | solution.py:705
  77.7 7.2 %all-to-all-start.2 = ((bf16[8,832,128]{2,1,0:T(8,128)(2,1)}), bf16[8,832,128]{2,1,0:T(8,128)(2,1)S(1)}, u32[]{:S(2)}, u32[]{:S(2)}) async-start(bf16[8,832,128]{2,1,0:T(8,128)(2,1)} %weight_grads.1), calls=%async_computation.2 | async-start | bytes 3407872 | tf_op jit(solution)/shard_map/all_to_all | solution.py:711
  84.9 12.1 %own_rows.1 = (f32[128,1024]{1,0:T(8,128)}, f32[128,1024]{1,0:T(8,128)}) custom-call(bf16[128,1024]{1,0:T(8,128)(2,1)} %bitcast.24, bf16[128,1024]{1,0:T(8,128)(2,1)} %bitcast.20, f32[1,1024]{1,0:T(1,128)} %bitcast.36, f32[1,1024]{1,0:T(1,128)} %bitcast.41, bf16[1024,2816]{1,0:T(8,128)(2,1)} %wg_in.1, bf16[1024,2816]{1,0:T(8,128)(2,1)} %wu_in.1, ...), custom_call_target="tpu_custom_call" | custom-call | flops 4499999744 | bytes 18874368 | tf_op jit(solution)/shard_map/own_rows/pallas_call | solution.py:113
  97.0 8.0 %final_rows.1 = (bf16[128,1024]{1,0:T(8,128)(2,1)}, bf16[128,1024]{1,0:T(8,128)(2,1)}) custom-call(bf16[2048,256]{1,0:T(8,128)(2,1)} %bitcast.27, bf16[128,1024]{1,0:T(8,128)(2,1)} %bitcast.25, bf16[128,1024]{1,0:T(8,128)(2,1)} %bitcast.21, f32[128,1024]{1,0:T(8,128)} %get-tuple-element.56.part, f32[128,1024]{1,0:T(8,128)} %get-tuple-element.57.grad, ...), custom_call_target="tpu_custom_call" | custom-call | flops 1100000000 | bytes 10485760 | tf_op jit(solution)/shard_map/final_rows/pallas_call | solution.py:552
  105.0 1.8 %all-to-all-done.2.got = bf16[8,832,128]{2,1,0:T(8,128)(2,1)S(1)} async-done(((bf16[8,832,128]{2,1,0:T(8,128)(2,1)}), bf16[8,832,128]{2,1,0:T(8,128)(2,1)S(1)}, u32[]{:S(2)}, u32[]{:S(2)}) %all-to-all-start.2) | async-done | bytes 1703968 | tf_op jit(solution)/shard_map/all_to_all | solution.py:711
  106.8 1.0 sum_rows.1
  107.8 10.9 %all_to_all.39 = bf16[16,8,640]{2,1,0:T(8,128)(2,1)S(1)} all-to-all(bf16[16,8,640]{2,1,0:T(8,128)(2,1)S(1)} %bitcast.17), channel_id=1, replica_groups=mesh['seq'=16,'rows'=8] {'seq'}, dimensions={0} | all-to-all | bytes 327680 | tf_op jit(solution)/shard_map/all_to_all | solution.py:717
  118.7 0.8 last_layout.1
  (31 shorter events, 0.1 us)
Async XLA Ops:
  1.7 20.7 %copy-start.1 = (bf16[256,1024]{1,0:T(8,128)(2,1)}, bf16[256,1024]{1,0:T(8,128)(2,1)S(1)}, u32[]{:S(2)}) copy-start(bf16[256,1024]{1,0:T(8,128)(2,1)S(1)} %pad_maximum_fusion.refs_0_) | copy-start | bytes 1572868
  1.7 15.1 %collective-permute-start.1 = (bf16[256,1024]{1,0:T(8,128)(2,1)S(1)}, bf16[256,1024]{1,0:T(8,128)(2,1)S(1)}, u32[]{:S(2)}, u32[]{:S(2)}) collective-permute-start(bf16[256,1024]{1,0:T(8,128)(2,1)S(1)} %pad_maximum_fusion.refs_0_), channel_id=1, source_target_pairs={{0,32},{8,40},{16,48},{24,56},{32,64},{40,72},{48,80},{56,88},{64,... | collective-permute-start | bytes 1572872 | tf_op jit(solution)/shard_map/ppermute | solution.py:645
  3.9 19.1 %collective-permute-start.3 = (bf16[256,1024]{1,0:T(8,128)(2,1)S(1)}, bf16[256,1024]{1,0:T(8,128)(2,1)S(1)}, u32[]{:S(2)}, u32[]{:S(2)}) collective-permute-start(bf16[256,1024]{1,0:T(8,128)(2,1)S(1)} %pad_maximum_fusion.refs_0_), channel_id=1, source_target_pairs={{0,96},{8,104},{16,112},{24,120},{32,0},{40,8},{48,16},{56,24},{64... | collective-permute-start | bytes 1572872 | tf_op jit(solution)/shard_map/ppermute | solution.py:645
  5.4 17.6 %collective-permute-start.5 = (bf16[256,1024]{1,0:T(8,128)(2,1)S(1)}, bf16[256,1024]{1,0:T(8,128)(2,1)S(1)}, u32[]{:S(2)}, u32[]{:S(2)}) collective-permute-start(bf16[256,1024]{1,0:T(8,128)(2,1)S(1)} %pad_maximum_fusion.refs_0_), channel_id=1, source_target_pairs={{0,16},{8,24},{16,0},{24,8},{32,48},{40,56},{48,32},{56,40},{64,80... | collective-permute-start | bytes 1572872 | tf_op jit(solution)/shard_map/ppermute | solution.py:645
  16.9 17.7 %copy-start.4 = (bf16[256,1024]{1,0:T(8,128)(2,1)}, bf16[256,1024]{1,0:T(8,128)(2,1)S(1)}, u32[]{:S(2)}) copy-start(bf16[256,1024]{1,0:T(8,128)(2,1)S(1)} %collective-permute-done.1.refs_2_) | copy-start | bytes 1572868
  16.9 25.0 %all-to-all-start = ((bf16[16,128,256]{2,1,0:T(8,128)(2,1)}), bf16[16,128,256]{2,1,0:T(8,128)(2,1)S(1)}, u32[]{:S(2)}, u32[]{:S(2)}) async-start(bf16[16,128,256]{2,1,0:T(8,128)(2,1)} %bitcast.26), calls=%async_computation | async-start | bytes 2097152 | tf_op jit(solution)/shard_map/all_to_all | solution.py:695
  22.4 8.3 %collective-permute-start = (bf16[256,1024]{1,0:T(8,128)(2,1)S(1)}, bf16[256,1024]{1,0:T(8,128)(2,1)S(1)}, u32[]{:S(2)}, u32[]{:S(2)}) collective-permute-start(bf16[256,1024]{1,0:T(8,128)(2,1)S(1)} %pad_maximum_fusion.refs_0_), channel_id=1, source_target_pairs={{0,8},{8,0},{16,24},{24,16},{32,40},{40,32},{48,56},{56,48},{64,72... | collective-permute-start | bytes 1572872 | tf_op jit(solution)/shard_map/ppermute | solution.py:645
  22.6 8.1 %collective-permute-start.2 = (bf16[256,1024]{1,0:T(8,128)(2,1)S(1)}, bf16[256,1024]{1,0:T(8,128)(2,1)}, u32[]{:S(2)}, u32[]{:S(2)}) collective-permute-start(bf16[256,1024]{1,0:T(8,128)(2,1)S(1)} %collective-permute-done.1.refs_2_), channel_id=1, source_target_pairs={{0,8},{8,0},{16,24},{24,16},{32,40},{40,32},{48,56},{56,48},{64,72... | collective-permute-start | bytes 1572872 | tf_op jit(solution)/shard_map/ppermute | solution.py:645
  23.0 9.0 %copy-start.5 = (bf16[256,1024]{1,0:T(8,128)(2,1)}, bf16[256,1024]{1,0:T(8,128)(2,1)S(1)}, u32[]{:S(2)}) copy-start(bf16[256,1024]{1,0:T(8,128)(2,1)S(1)} %collective-permute-done.3.refs_4_) | copy-start | bytes 1572868
  23.0 8.9 %collective-permute-start.4 = (bf16[256,1024]{1,0:T(8,128)(2,1)S(1)}, bf16[256,1024]{1,0:T(8,128)(2,1)}, u32[]{:S(2)}, u32[]{:S(2)}) collective-permute-start(bf16[256,1024]{1,0:T(8,128)(2,1)S(1)} %collective-permute-done.3.refs_4_), channel_id=1, source_target_pairs={{0,8},{8,0},{16,24},{24,16},{32,40},{40,32},{48,56},{56,48},{64,72... | collective-permute-start | bytes 1572872 | tf_op jit(solution)/shard_map/ppermute | solution.py:645
  23.1 4.0 %copy-start.2 = (bf16[256,1024]{1,0:T(8,128)(2,1)}, bf16[256,1024]{1,0:T(8,128)(2,1)S(1)}, u32[]{:S(2)}) copy-start(bf16[256,1024]{1,0:T(8,128)(2,1)S(1)} %collective-permute-done.5.refs_6_) | copy-start | bytes 1572868
  23.1 11.4 %collective-permute-start.6 = (bf16[256,1024]{1,0:T(8,128)(2,1)S(1)}, bf16[256,1024]{1,0:T(8,128)(2,1)}, u32[]{:S(2)}, u32[]{:S(2)}) collective-permute-start(bf16[256,1024]{1,0:T(8,128)(2,1)S(1)} %collective-permute-done.5.refs_6_), channel_id=1, source_target_pairs={{0,8},{8,0},{16,24},{24,16},{32,40},{40,32},{48,56},{56,48},{64,72... | collective-permute-start | bytes 1572872 | tf_op jit(solution)/shard_map/ppermute | solution.py:645
  27.1 30.0 %collective-permute-start.11 = (bf16[176,1024]{1,0:T(8,128)(2,1)S(1)}, bf16[176,1024]{1,0:T(8,128)(2,1)}, u32[]{:S(2)}, u32[]{:S(2)}) collective-permute-start(bf16[176,1024]{1,0:T(8,128)(2,1)S(1)} %slice.12), channel_id=1, source_target_pairs={{0,96},{8,104},{16,112},{24,120},{32,0},{40,8},{48,16},{56,24},{64... | collective-permute-start | bytes 1081352 | tf_op jit(solution)/shard_map/ppermute | solution.py:645
  30.6 3.9 %copy-start.6 = (bf16[256,1024]{1,0:T(8,128)(2,1)}, bf16[256,1024]{1,0:T(8,128)(2,1)S(1)}, u32[]{:S(2)}) copy-start(bf16[256,1024]{1,0:T(8,128)(2,1)S(1)} %collective-permute-done.refs_1_) | copy-start | bytes 1572868
  30.6 26.5 %collective-permute-start.13 = (bf16[176,1024]{1,0:T(8,128)(2,1)S(1)}, bf16[176,1024]{1,0:T(8,128)(2,1)}, u32[]{:S(2)}, u32[]{:S(2)}) collective-permute-start(bf16[176,1024]{1,0:T(8,128)(2,1)S(1)} %slice.12), channel_id=1, source_target_pairs={{0,32},{8,40},{16,48},{24,56},{32,64},{40,72},{48,80},{56,88},{64,... | collective-permute-start | bytes 1081352 | tf_op jit(solution)/shard_map/ppermute | solution.py:645
  30.7 27.0 %collective-permute-start.15 = (bf16[160,1024]{1,0:T(8,128)(2,1)}, bf16[160,1024]{1,0:T(8,128)(2,1)}, u32[]{:S(2)}, u32[]{:S(2)}) collective-permute-start(bf16[160,1024]{1,0:T(8,128)(2,1)} %pad_maximum_fusion.1), channel_id=1, source_target_pairs={{0,16},{8,24},{16,0},{24,8},{32,48},{40,56},{48,32},{56,40},{64,80... | collective-permute-start | bytes 983048 | tf_op jit(solution)/shard_map/ppermute | solution.py:645
  31.9 23.4 %collective-permute-start.9 = (bf16[256,1024]{1,0:T(8,128)(2,1)S(1)}, bf16[256,1024]{1,0:T(8,128)(2,1)}, u32[]{:S(2)}, u32[]{:S(2)}) collective-permute-start(bf16[256,1024]{1,0:T(8,128)(2,1)S(1)} %collective-permute-done.3.refs_4_), channel_id=1, source_target_pairs={{0,112},{8,120},{16,96},{24,104},{32,16},{40,24},{48,0},{56,8},{64... | collective-permute-start | bytes 1572872 | tf_op jit(solution)/shard_map/ppermute | solution.py:645
  34.5 21.9 %collective-permute-start.7 = (bf16[256,1024]{1,0:T(8,128)(2,1)S(1)}, bf16[256,1024]{1,0:T(8,128)(2,1)}, u32[]{:S(2)}, u32[]{:S(2)}) collective-permute-start(bf16[256,1024]{1,0:T(8,128)(2,1)S(1)} %collective-permute-done.1.refs_2_), channel_id=1, source_target_pairs={{0,32},{8,40},{16,48},{24,56},{32,64},{40,72},{48,80},{56,88},{64,... | collective-permute-start | bytes 1572872 | tf_op jit(solution)/shard_map/ppermute | solution.py:645
  41.9 1.0 copy-start.3
  55.3 6.5 %collective-permute-start.10 = (bf16[256,1024]{1,0:T(8,128)(2,1)}, bf16[256,1024]{1,0:T(8,128)(2,1)S(1)}, u32[]{:S(2)}, u32[]{:S(2)}) collective-permute-start(bf16[256,1024]{1,0:T(8,128)(2,1)} %collective-permute-done.9.refs_10_), channel_id=1, source_target_pairs={{0,8},{8,0},{16,24},{24,16},{32,40},{40,32},{48,56},{56,48},{64,72... | collective-permute-start | bytes 1572872 | tf_op jit(solution)/shard_map/ppermute | solution.py:645
  56.4 5.5 %collective-permute-start.8 = (bf16[256,1024]{1,0:T(8,128)(2,1)}, bf16[256,1024]{1,0:T(8,128)(2,1)S(1)}, u32[]{:S(2)}, u32[]{:S(2)}) collective-permute-start(bf16[256,1024]{1,0:T(8,128)(2,1)} %collective-permute-done.7.refs_8_), channel_id=1, source_target_pairs={{0,8},{8,0},{16,24},{24,16},{32,40},{40,32},{48,56},{56,48},{64,72... | collective-permute-start | bytes 1572872 | tf_op jit(solution)/shard_map/ppermute | solution.py:645
  57.1 4.7 %collective-permute-start.12 = (bf16[176,1024]{1,0:T(8,128)(2,1)}, bf16[176,1024]{1,0:T(8,128)(2,1)S(1)}, u32[]{:S(2)}, u32[]{:S(2)}) collective-permute-start(bf16[176,1024]{1,0:T(8,128)(2,1)} %collective-permute-done.11.refs_12_), channel_id=1, source_target_pairs={{0,8},{8,0},{16,24},{24,16},{32,40},{40,32},{48,56},{56,48},{64,72... | collective-permute-start | bytes 1081352 | tf_op jit(solution)/shard_map/ppermute | solution.py:645
  57.1 4.7 %collective-permute-start.14 = (bf16[176,1024]{1,0:T(8,128)(2,1)}, bf16[176,1024]{1,0:T(8,128)(2,1)S(1)}, u32[]{:S(2)}, u32[]{:S(2)}) collective-permute-start(bf16[176,1024]{1,0:T(8,128)(2,1)} %collective-permute-done.13.refs_14_), channel_id=1, source_target_pairs={{0,8},{8,0},{16,24},{24,16},{32,40},{40,32},{48,56},{56,48},{64,72... | collective-permute-start | bytes 1081352 | tf_op jit(solution)/shard_map/ppermute | solution.py:645
  57.6 4.2 %collective-permute-start.16 = (bf16[160,1024]{1,0:T(8,128)(2,1)}, bf16[160,1024]{1,0:T(8,128)(2,1)S(1)}, u32[]{:S(2)}, u32[]{:S(2)}) collective-permute-start(bf16[160,1024]{1,0:T(8,128)(2,1)} %collective-permute-done.15.refs_16_), channel_id=1, source_target_pairs={{0,8},{8,0},{16,24},{24,16},{32,40},{40,32},{48,56},{56,48},{64,72... | collective-permute-start | bytes 983048 | tf_op jit(solution)/shard_map/ppermute | solution.py:645
  57.7 20.0 %all-to-all-start.1 = ((bf16[16,128,256]{2,1,0:T(8,128)(2,1)}), bf16[16,128,256]{2,1,0:T(8,128)(2,1)S(1)}, u32[]{:S(2)}, u32[]{:S(2)}) async-start(bf16[16,128,256]{2,1,0:T(8,128)(2,1)} %bitcast.28), calls=%async_computation.1 | async-start | bytes 2097152 | tf_op jit(solution)/shard_map/all_to_all | solution.py:705
  61.8 0.7 copy-start.11
  61.8 0.9 copy-start.9
  61.9 0.9 copy-start.10
  61.9 1.1 copy-start.7
  61.9 1.3 %copy-start.8 = (bf16[256,1024]{1,0:T(8,128)(2,1)}, bf16[256,1024]{1,0:T(8,128)(2,1)S(1)}, u32[]{:S(2)}) copy-start(bf16[256,1024]{1,0:T(8,128)(2,1)S(1)} %collective-permute-done.8.refs_9_) | copy-start | bytes 1572868
  77.7 19.3 %copy-start = (bf16[16,128,256]{2,1,0:T(8,128)(2,1)}, bf16[16,128,256]{2,1,0:T(8,128)(2,1)S(1)}, u32[]{:S(2)}) copy-start(bf16[16,128,256]{2,1,0:T(8,128)(2,1)S(1)} %all-to-all-done.1) | copy-start | bytes 3145732
  77.7 29.1 %all-to-all-start.2 = ((bf16[8,832,128]{2,1,0:T(8,128)(2,1)}), bf16[8,832,128]{2,1,0:T(8,128)(2,1)S(1)}, u32[]{:S(2)}, u32[]{:S(2)}) async-start(bf16[8,832,128]{2,1,0:T(8,128)(2,1)} %weight_grads.1), calls=%async_computation.2 | async-start | bytes 3407872 | tf_op jit(solution)/shard_map/all_to_all | solution.py:711

commit v5 on v4

--- a/solution.py
+++ b/solution.py
@@ -691,8 +691,7 @@
     w_qkv_s, w_gu_s = cut_weights(w_qkv, w_gate, w_up)
 
     def exchange(first):
-        ready, _ = lax.optimization_barrier((packed, first))
-        return lax.all_to_all(ready, "seq", 0, 0, tiled=True)
+        return lax.all_to_all(packed, "seq", 0, 0, tiled=True)
 
     def attend(packed_here, early, arrays):
         first = first_half(

time: 120 us -> 116 us (0.967)
  waiting for transfers between devices: 8.26 us -> 5.01 us
    ppermute x17, waiting for transfers between devices: 5.1 us -> 1.86 us  [send(): return lax.ppermute(value, 'seq', to)]
  transfers between devices with their start and end apart: 20 -> 20, of which waited for: 5 -> 4; matrix products, arithmetic and copies ran while one was open for 1% -> 1% of each run, Pallas kernels for 52% -> 54%
where the time goes in v5:
time: 116 us
  Pallas kernels  63.8 us (55%)
  starting transfers between devices  30.9 us (27%)
  blocking collectives  10.9 us (9%)
  waiting for transfers between devices  5.01 us (4%)
  local copies, waits for them, and re-layouts  2.29 us (2%)
  other arithmetic  1.83 us (2%)
    ppermute x17, starting transfers between devices, send(): return lax.ppermute(value, 'seq', to)  14.8 us
    pallas_call x1, Pallas kernels, weight_grads(): pl.pallas_call(lambda *refs: weights_kernel(pieces, len(arrays), *refs),...  13.2 us
    pallas_call x1, Pallas kernels, own_rows(): pl.pallas_call(own_kernel, out_shape=[jax.ShapeDtypeStruct((HERE, WIDTH),...  12.1 us
    all_to_all x1, blocking collectives, shards(): mine = lax.all_to_all(outgoing, 'seq', 0, 0, tiled=True)  10.9 us
    pallas_call x1, Pallas kernels, attention(): pl.pallas_call(attention_kernel, out_shape=jax.ShapeDtypeStruct((LENGTH,...  10.9 us
    pallas_call x1, Pallas kernels, final_rows(): pl.pallas_call(final_kernel, grid=(WIDTH // BLOCK,), out_shape=[jax.Shape...  8.02 us
    pallas_call x1, Pallas kernels, first_half(): pl.pallas_call(lambda *refs: first_kernel(pieces, len(arrays), *refs), ou...  7.3 us
    all_to_all x1, starting transfers between devices, shards(): got = lax.all_to_all(block, 'rows', 0, 0, tiled=True)  7.23 us
  transfers between devices with their start and end apart: 20, of which 4 were waited for; matrix products, arithmetic and copies ran while one was open for 1% of the time, Pallas kernels for 54%

profile of v5, /device:TPU:1, one launch (start us, length us, event | category | flops | bytes accessed | tf_op | source)
XLA Modules:
  0.0 115.7 jit_solution(17585483837067998074)
XLA Ops:
  0.6 1.1 pad_maximum_fusion.refs_0_
  1.7 2.2 %collective-permute-start.1 = (bf16[256,1024]{1,0:T(8,128)(2,1)S(1)}, bf16[256,1024]{1,0:T(8,128)(2,1)S(1)}, u32[]{:S(2)}, u32[]{:S(2)}) collective-permute-start(bf16[256,1024]{1,0:T(8,128)(2,1)S(1)} %pad_maximum_fusion.refs_0_), channel_id=1, source_target_pairs={{0,32},{8,40},{16,48},{24,56},{32,64},{40,72},{48,80},{56,88},{64,... | collective-permute-start | bytes 1572872 | tf_op jit(solution)/shard_map/ppermute | solution.py:645
  3.9 1.5 %collective-permute-start.3 = (bf16[256,1024]{1,0:T(8,128)(2,1)S(1)}, bf16[256,1024]{1,0:T(8,128)(2,1)S(1)}, u32[]{:S(2)}, u32[]{:S(2)}) collective-permute-start(bf16[256,1024]{1,0:T(8,128)(2,1)S(1)} %pad_maximum_fusion.refs_0_), channel_id=1, source_target_pairs={{0,96},{8,104},{16,112},{24,120},{32,0},{40,8},{48,16},{56,24},{64... | collective-permute-start | bytes 1572872 | tf_op jit(solution)/shard_map/ppermute | solution.py:645
  5.4 1.2 %collective-permute-start.5 = (bf16[256,1024]{1,0:T(8,128)(2,1)S(1)}, bf16[256,1024]{1,0:T(8,128)(2,1)S(1)}, u32[]{:S(2)}, u32[]{:S(2)}) collective-permute-start(bf16[256,1024]{1,0:T(8,128)(2,1)S(1)} %pad_maximum_fusion.refs_0_), channel_id=1, source_target_pairs={{0,16},{8,24},{16,0},{24,8},{32,48},{40,56},{48,32},{56,40},{64,80... | collective-permute-start | bytes 1572872 | tf_op jit(solution)/shard_map/ppermute | solution.py:645
  6.6 6.9 %own_heads.1 = bf16[2048,256]{1,0:T(8,128)(2,1)} custom-call(s32[32]{0:T(128)} %refs_4_.1, bf16[128,1024]{1,0:T(8,128)(2,1)} %bitcast.23, bf16[128,1024]{1,0:T(8,128)(2,1)} %bitcast.19, bf16[1024,3072]{1,0:T(8,128)(2,1)} %w_qkv.3, bf16[1024,3072]{1,0:T(8,128)(2,1)} %w_qkv.3, bf16[1024,3072]{1,0:T(8,128)(2,1)} %w_qkv.3, bf16[1024,1024]{1,0:T(8,128)(2,1)} %w_out.1, ...), custom_call_target="tpu_custom_call" | custom-call | flops 1100000000 | bytes 9437184 | tf_op jit(solution)/shard_map/own_heads/pallas_call | solution.py:170
  13.6 4.8 %all-to-all-start = ((bf16[16,128,256]{2,1,0:T(8,128)(2,1)}), bf16[16,128,256]{2,1,0:T(8,128)(2,1)S(1)}, u32[]{:S(2)}, u32[]{:S(2)}) async-start(bf16[16,128,256]{2,1,0:T(8,128)(2,1)} %bitcast.26), calls=%async_computation | async-start | bytes 2097152 | tf_op jit(solution)/shard_map/all_to_all | solution.py:694
  18.4 0.3 collective-permute-start
  18.7 0.0 collective-permute-done.1.refs_2_
  18.7 0.3 collective-permute-start.2
  19.0 0.2 collective-permute-start.4
  19.2 0.0 collective-permute-done.5.refs_6_
  19.2 0.5 collective-permute-start.6
  19.8 3.6 %cut_weights.1 = (bf16[192,1024]{1,0:T(8,128)(2,1)}, bf16[352,1024]{1,0:T(8,128)(2,1)}) custom-call(bf16[1024,3072]{1,0:T(8,128)(2,1)} %w_qkv.3, bf16[1024,2816]{1,0:T(8,128)(2,1)} %wg_in.1, bf16[1024,2816]{1,0:T(8,128)(2,1)} %wu_in.1), custom_call_target="tpu_custom_call" | custom-call | flops 1000000 | bytes 1048 | tf_op jit(solution)/shard_map/cut_weights/pallas_call | solution.py:303
  23.4 2.5 %collective-permute-start.11 = (bf16[176,1024]{1,0:T(8,128)(2,1)S(1)}, bf16[176,1024]{1,0:T(8,128)(2,1)}, u32[]{:S(2)}, u32[]{:S(2)}) collective-permute-start(bf16[176,1024]{1,0:T(8,128)(2,1)S(1)} %slice.12), channel_id=1, source_target_pairs={{0,96},{8,104},{16,112},{24,120},{32,0},{40,8},{48,16},{56,24},{64... | collective-permute-start | bytes 1081352 | tf_op jit(solution)/shard_map/ppermute | solution.py:645
  26.0 0.8 pad_maximum_fusion.1
  26.7 0.0 collective-permute-start.13
  26.7 0.0 collective-permute-done.2.refs_3_
  26.8 1.3 %collective-permute-start.15 = (bf16[160,1024]{1,0:T(8,128)(2,1)}, bf16[160,1024]{1,0:T(8,128)(2,1)}, u32[]{:S(2)}, u32[]{:S(2)}) collective-permute-start(bf16[160,1024]{1,0:T(8,128)(2,1)} %pad_maximum_fusion.1), channel_id=1, source_target_pairs={{0,16},{8,24},{16,0},{24,8},{32,48},{40,56},{48,32},{56,40},{64,80... | collective-permute-start | bytes 983048 | tf_op jit(solution)/shard_map/ppermute | solution.py:645
  28.0 2.6 %collective-permute-start.9 = (bf16[256,1024]{1,0:T(8,128)(2,1)S(1)}, bf16[256,1024]{1,0:T(8,128)(2,1)}, u32[]{:S(2)}, u32[]{:S(2)}) collective-permute-start(bf16[256,1024]{1,0:T(8,128)(2,1)S(1)} %collective-permute-done.3.refs_4_), channel_id=1, source_target_pairs={{0,112},{8,120},{16,96},{24,104},{32,16},{40,24},{48,0},{56,8},{64... | collective-permute-start | bytes 1572872 | tf_op jit(solution)/shard_map/ppermute | solution.py:645
  30.6 0.0 collective-permute-start.7
  30.6 7.3 %first_half.1 = (bf16[1024,1024]{1,0:T(8,128)(2,1)}, bf16[176,1024]{1,0:T(8,128)(2,1)}, bf16[352,1024]{1,0:T(8,128)(2,1)}, f32[352,128]{1,0:T(8,128)}) custom-call(bf16[256,1024]{1,0:T(8,128)(2,1)} %copy-done.1, bf16[256,1024]{1,0:T(8,128)(2,1)} %copy-done.6, bf16[256,1024]{1,0:T(8,128)(2,1)} %copy-done.4, bf16[256,1024]{1,0:T(8,128)(2,1)} %collective-permute-done.2.refs_3_, ...), custom_call_target="tpu_custom_call" | custom-call | flops 1000000 | bytes 1048 | tf_op jit(solution)/shard_map/first_half/pallas_call | solution.py:385
  37.9 0.0 all-to-all-done
  38.0 1.0 copy-done.3
  38.9 10.9 %attention.1.refs_18_ = bf16[2048,256]{1,0:T(8,128)(2,1)} custom-call(bf16[1024,1024]{1,0:T(8,128)(2,1)} %get-tuple-element.41.refs_0_.refs_24_, bf16[176,1024]{1,0:T(8,128)(2,1)} %get-tuple-element.42.refs_1_.refs_25_, bf16[352,1024]{1,0:T(8,128)(2,1)} %get-tuple-element.43.refs_2_.refs_26_, f32[352,128]{1,0:T(8,128)} %get-tuple-element.44.refs_3_.refs_27_, ...), custom_call_target="tpu_custom_call" | custom-call | flops 15000000512 | bytes 8388608 | tf_op jit(solution)/shard_map/attention/pallas_call | solution.py:259
  49.9 1.5 %collective-permute-done.9.refs_10_ = bf16[256,1024]{1,0:T(8,128)(2,1)} collective-permute-done((bf16[256,1024]{1,0:T(8,128)(2,1)S(1)}, bf16[256,1024]{1,0:T(8,128)(2,1)}, u32[]{:S(2)}, u32[]{:S(2)}) %collective-permute-start.9) | collective-permute-done | bytes 524320 | tf_op jit(solution)/shard_map/ppermute | solution.py:645
  51.4 0.9 collective-permute-start.10
  52.3 0.3 collective-permute-done.7.refs_8_
  52.5 0.7 collective-permute-start.8
  53.2 0.0 collective-permute-done.11.refs_12_
  53.2 0.0 collective-permute-start.12
  53.2 0.5 collective-permute-start.14
  53.7 0.0 collective-permute-done.15.refs_16_
  53.7 0.1 collective-permute-start.16
  53.8 4.1 %all-to-all-start.1 = ((bf16[16,128,256]{2,1,0:T(8,128)(2,1)}), bf16[16,128,256]{2,1,0:T(8,128)(2,1)S(1)}, u32[]{:S(2)}, u32[]{:S(2)}) async-start(bf16[16,128,256]{2,1,0:T(8,128)(2,1)} %bitcast.28), calls=%async_computation.1 | async-start | bytes 2097152 | tf_op jit(solution)/shard_map/all_to_all | solution.py:704
  58.0 0.6 copy-done.11
  58.6 0.1 copy-done.9
  58.8 0.1 copy-done.10
  58.9 0.2 copy-done.7
  59.1 0.2 copy-done.8
  59.2 13.2 %weight_grads.1 = bf16[8,832,128]{2,1,0:T(8,128)(2,1)} custom-call(bf16[256,1024]{1,0:T(8,128)(2,1)} %copy-done.1, bf16[256,1024]{1,0:T(8,128)(2,1)} %copy-done.6, bf16[256,1024]{1,0:T(8,128)(2,1)} %copy-done.4, bf16[256,1024]{1,0:T(8,128)(2,1)} %collective-permute-done.2.refs_3_, bf16[256,1024]{1,0:T(8,128)(2,1)} %copy-done.5, ...), custom_call_target="tpu_custom_call" | custom-call | flops 8000000000 | bytes 20971520 | tf_op jit(solution)/shard_map/weight_grads/pallas_call | solution.py:495
  72.5 1.4 %all-to-all-done.1 = bf16[16,128,256]{2,1,0:T(8,128)(2,1)S(1)} async-done(((bf16[16,128,256]{2,1,0:T(8,128)(2,1)}), bf16[16,128,256]{2,1,0:T(8,128)(2,1)S(1)}, u32[]{:S(2)}, u32[]{:S(2)}) %all-to-all-start.1) | async-done | bytes 1048608 | tf_op jit(solution)/shard_map/all_to_all | solution.py:704
  73.8 7.2 %all-to-all-start.2 = ((bf16[8,832,128]{2,1,0:T(8,128)(2,1)}), bf16[8,832,128]{2,1,0:T(8,128)(2,1)S(1)}, u32[]{:S(2)}, u32[]{:S(2)}) async-start(bf16[8,832,128]{2,1,0:T(8,128)(2,1)} %weight_grads.1), calls=%async_computation.2 | async-start | bytes 3407872 | tf_op jit(solution)/shard_map/all_to_all | solution.py:710
  81.1 12.1 %own_rows.1 = (f32[128,1024]{1,0:T(8,128)}, f32[128,1024]{1,0:T(8,128)}) custom-call(bf16[128,1024]{1,0:T(8,128)(2,1)} %bitcast.24, bf16[128,1024]{1,0:T(8,128)(2,1)} %bitcast.20, f32[1,1024]{1,0:T(1,128)} %bitcast.36, f32[1,1024]{1,0:T(1,128)} %bitcast.41, bf16[1024,2816]{1,0:T(8,128)(2,1)} %wg_in.1, bf16[1024,2816]{1,0:T(8,128)(2,1)} %wu_in.1, ...), custom_call_target="tpu_custom_call" | custom-call | flops 4499999744 | bytes 18874368 | tf_op jit(solution)/shard_map/own_rows/pallas_call | solution.py:113
  93.1 8.0 %final_rows.1 = (bf16[128,1024]{1,0:T(8,128)(2,1)}, bf16[128,1024]{1,0:T(8,128)(2,1)}) custom-call(bf16[2048,256]{1,0:T(8,128)(2,1)} %bitcast.27, bf16[128,1024]{1,0:T(8,128)(2,1)} %bitcast.25, bf16[128,1024]{1,0:T(8,128)(2,1)} %bitcast.21, f32[128,1024]{1,0:T(8,128)} %get-tuple-element.54.part, f32[128,1024]{1,0:T(8,128)} %get-tuple-element.55.grad, ...), custom_call_target="tpu_custom_call" | custom-call | flops 1100000000 | bytes 10485760 | tf_op jit(solution)/shard_map/final_rows/pallas_call | solution.py:552
  101.1 1.8 %all-to-all-done.2.got = bf16[8,832,128]{2,1,0:T(8,128)(2,1)S(1)} async-done(((bf16[8,832,128]{2,1,0:T(8,128)(2,1)}), bf16[8,832,128]{2,1,0:T(8,128)(2,1)S(1)}, u32[]{:S(2)}, u32[]{:S(2)}) %all-to-all-start.2) | async-done | bytes 1703968 | tf_op jit(solution)/shard_map/all_to_all | solution.py:710
  102.9 1.0 sum_rows.1
  103.9 10.9 %all_to_all.39 = bf16[16,8,640]{2,1,0:T(8,128)(2,1)S(1)} all-to-all(bf16[16,8,640]{2,1,0:T(8,128)(2,1)S(1)} %bitcast.17), channel_id=1, replica_groups=mesh['seq'=16,'rows'=8] {'seq'}, dimensions={0} | all-to-all | bytes 327680 | tf_op jit(solution)/shard_map/all_to_all | solution.py:716
  114.8 0.8 last_layout.1
  (31 shorter events, 0.1 us)
Async XLA Ops:
  1.7 16.7 %copy-start.1 = (bf16[256,1024]{1,0:T(8,128)(2,1)}, bf16[256,1024]{1,0:T(8,128)(2,1)S(1)}, u32[]{:S(2)}) copy-start(bf16[256,1024]{1,0:T(8,128)(2,1)S(1)} %pad_maximum_fusion.refs_0_) | copy-start | bytes 1572868
  1.7 17.0 %collective-permute-start.1 = (bf16[256,1024]{1,0:T(8,128)(2,1)S(1)}, bf16[256,1024]{1,0:T(8,128)(2,1)S(1)}, u32[]{:S(2)}, u32[]{:S(2)}) collective-permute-start(bf16[256,1024]{1,0:T(8,128)(2,1)S(1)} %pad_maximum_fusion.refs_0_), channel_id=1, source_target_pairs={{0,32},{8,40},{16,48},{24,56},{32,64},{40,72},{48,80},{56,88},{64,... | collective-permute-start | bytes 1572872 | tf_op jit(solution)/shard_map/ppermute | solution.py:645
  3.9 15.1 %collective-permute-start.3 = (bf16[256,1024]{1,0:T(8,128)(2,1)S(1)}, bf16[256,1024]{1,0:T(8,128)(2,1)S(1)}, u32[]{:S(2)}, u32[]{:S(2)}) collective-permute-start(bf16[256,1024]{1,0:T(8,128)(2,1)S(1)} %pad_maximum_fusion.refs_0_), channel_id=1, source_target_pairs={{0,96},{8,104},{16,112},{24,120},{32,0},{40,8},{48,16},{56,24},{64... | collective-permute-start | bytes 1572872 | tf_op jit(solution)/shard_map/ppermute | solution.py:645
  5.4 13.8 %collective-permute-start.5 = (bf16[256,1024]{1,0:T(8,128)(2,1)S(1)}, bf16[256,1024]{1,0:T(8,128)(2,1)S(1)}, u32[]{:S(2)}, u32[]{:S(2)}) collective-permute-start(bf16[256,1024]{1,0:T(8,128)(2,1)S(1)} %pad_maximum_fusion.refs_0_), channel_id=1, source_target_pairs={{0,16},{8,24},{16,0},{24,8},{32,48},{40,56},{48,32},{56,40},{64,80... | collective-permute-start | bytes 1572872 | tf_op jit(solution)/shard_map/ppermute | solution.py:645
  13.6 24.4 %all-to-all-start = ((bf16[16,128,256]{2,1,0:T(8,128)(2,1)}), bf16[16,128,256]{2,1,0:T(8,128)(2,1)S(1)}, u32[]{:S(2)}, u32[]{:S(2)}) async-start(bf16[16,128,256]{2,1,0:T(8,128)(2,1)} %bitcast.26), calls=%async_computation | async-start | bytes 2097152 | tf_op jit(solution)/shard_map/all_to_all | solution.py:694
  18.4 8.3 %collective-permute-start = (bf16[256,1024]{1,0:T(8,128)(2,1)S(1)}, bf16[256,1024]{1,0:T(8,128)(2,1)S(1)}, u32[]{:S(2)}, u32[]{:S(2)}) collective-permute-start(bf16[256,1024]{1,0:T(8,128)(2,1)S(1)} %pad_maximum_fusion.refs_0_), channel_id=1, source_target_pairs={{0,8},{8,0},{16,24},{24,16},{32,40},{40,32},{48,56},{56,48},{64,72... | collective-permute-start | bytes 1572872 | tf_op jit(solution)/shard_map/ppermute | solution.py:645
  18.7 11.9 %copy-start.4 = (bf16[256,1024]{1,0:T(8,128)(2,1)}, bf16[256,1024]{1,0:T(8,128)(2,1)S(1)}, u32[]{:S(2)}) copy-start(bf16[256,1024]{1,0:T(8,128)(2,1)S(1)} %collective-permute-done.1.refs_2_) | copy-start | bytes 1572868
  18.7 8.0 %collective-permute-start.2 = (bf16[256,1024]{1,0:T(8,128)(2,1)S(1)}, bf16[256,1024]{1,0:T(8,128)(2,1)}, u32[]{:S(2)}, u32[]{:S(2)}) collective-permute-start(bf16[256,1024]{1,0:T(8,128)(2,1)S(1)} %collective-permute-done.1.refs_2_), channel_id=1, source_target_pairs={{0,8},{8,0},{16,24},{24,16},{32,40},{40,32},{48,56},{56,48},{64,72... | collective-permute-start | bytes 1572872 | tf_op jit(solution)/shard_map/ppermute | solution.py:645
  19.0 9.0 %copy-start.5 = (bf16[256,1024]{1,0:T(8,128)(2,1)}, bf16[256,1024]{1,0:T(8,128)(2,1)S(1)}, u32[]{:S(2)}) copy-start(bf16[256,1024]{1,0:T(8,128)(2,1)S(1)} %collective-permute-done.3.refs_4_) | copy-start | bytes 1572868
  19.0 9.0 %collective-permute-start.4 = (bf16[256,1024]{1,0:T(8,128)(2,1)S(1)}, bf16[256,1024]{1,0:T(8,128)(2,1)}, u32[]{:S(2)}, u32[]{:S(2)}) collective-permute-start(bf16[256,1024]{1,0:T(8,128)(2,1)S(1)} %collective-permute-done.3.refs_4_), channel_id=1, source_target_pairs={{0,8},{8,0},{16,24},{24,16},{32,40},{40,32},{48,56},{56,48},{64,72... | collective-permute-start | bytes 1572872 | tf_op jit(solution)/shard_map/ppermute | solution.py:645
  19.2 4.1 %copy-start.2 = (bf16[256,1024]{1,0:T(8,128)(2,1)}, bf16[256,1024]{1,0:T(8,128)(2,1)S(1)}, u32[]{:S(2)}) copy-start(bf16[256,1024]{1,0:T(8,128)(2,1)S(1)} %collective-permute-done.5.refs_6_) | copy-start | bytes 1572868
  19.2 11.4 %collective-permute-start.6 = (bf16[256,1024]{1,0:T(8,128)(2,1)S(1)}, bf16[256,1024]{1,0:T(8,128)(2,1)}, u32[]{:S(2)}, u32[]{:S(2)}) collective-permute-start(bf16[256,1024]{1,0:T(8,128)(2,1)S(1)} %collective-permute-done.5.refs_6_), channel_id=1, source_target_pairs={{0,8},{8,0},{16,24},{24,16},{32,40},{40,32},{48,56},{56,48},{64,72... | collective-permute-start | bytes 1572872 | tf_op jit(solution)/shard_map/ppermute | solution.py:645
  23.4 29.8 %collective-permute-start.11 = (bf16[176,1024]{1,0:T(8,128)(2,1)S(1)}, bf16[176,1024]{1,0:T(8,128)(2,1)}, u32[]{:S(2)}, u32[]{:S(2)}) collective-permute-start(bf16[176,1024]{1,0:T(8,128)(2,1)S(1)} %slice.12), channel_id=1, source_target_pairs={{0,96},{8,104},{16,112},{24,120},{32,0},{40,8},{48,16},{56,24},{64... | collective-permute-start | bytes 1081352 | tf_op jit(solution)/shard_map/ppermute | solution.py:645
  26.7 3.9 %copy-start.6 = (bf16[256,1024]{1,0:T(8,128)(2,1)}, bf16[256,1024]{1,0:T(8,128)(2,1)S(1)}, u32[]{:S(2)}) copy-start(bf16[256,1024]{1,0:T(8,128)(2,1)S(1)} %collective-permute-done.refs_1_) | copy-start | bytes 1572868
  26.7 26.5 %collective-permute-start.13 = (bf16[176,1024]{1,0:T(8,128)(2,1)S(1)}, bf16[176,1024]{1,0:T(8,128)(2,1)}, u32[]{:S(2)}, u32[]{:S(2)}) collective-permute-start(bf16[176,1024]{1,0:T(8,128)(2,1)S(1)} %slice.12), channel_id=1, source_target_pairs={{0,32},{8,40},{16,48},{24,56},{32,64},{40,72},{48,80},{56,88},{64,... | collective-permute-start | bytes 1081352 | tf_op jit(solution)/shard_map/ppermute | solution.py:645
  26.8 27.0 %collective-permute-start.15 = (bf16[160,1024]{1,0:T(8,128)(2,1)}, bf16[160,1024]{1,0:T(8,128)(2,1)}, u32[]{:S(2)}, u32[]{:S(2)}) collective-permute-start(bf16[160,1024]{1,0:T(8,128)(2,1)} %pad_maximum_fusion.1), channel_id=1, source_target_pairs={{0,16},{8,24},{16,0},{24,8},{32,48},{40,56},{48,32},{56,40},{64,80... | collective-permute-start | bytes 983048 | tf_op jit(solution)/shard_map/ppermute | solution.py:645
  28.0 23.4 %collective-permute-start.9 = (bf16[256,1024]{1,0:T(8,128)(2,1)S(1)}, bf16[256,1024]{1,0:T(8,128)(2,1)}, u32[]{:S(2)}, u32[]{:S(2)}) collective-permute-start(bf16[256,1024]{1,0:T(8,128)(2,1)S(1)} %collective-permute-done.3.refs_4_), channel_id=1, source_target_pairs={{0,112},{8,120},{16,96},{24,104},{32,16},{40,24},{48,0},{56,8},{64... | collective-permute-start | bytes 1572872 | tf_op jit(solution)/shard_map/ppermute | solution.py:645
  30.6 21.9 %collective-permute-start.7 = (bf16[256,1024]{1,0:T(8,128)(2,1)S(1)}, bf16[256,1024]{1,0:T(8,128)(2,1)}, u32[]{:S(2)}, u32[]{:S(2)}) collective-permute-start(bf16[256,1024]{1,0:T(8,128)(2,1)S(1)} %collective-permute-done.1.refs_2_), channel_id=1, source_target_pairs={{0,32},{8,40},{16,48},{24,56},{32,64},{40,72},{48,80},{56,88},{64,... | collective-permute-start | bytes 1572872 | tf_op jit(solution)/shard_map/ppermute | solution.py:645
  38.0 1.0 copy-start.3
  51.4 6.6 %collective-permute-start.10 = (bf16[256,1024]{1,0:T(8,128)(2,1)}, bf16[256,1024]{1,0:T(8,128)(2,1)S(1)}, u32[]{:S(2)}, u32[]{:S(2)}) collective-permute-start(bf16[256,1024]{1,0:T(8,128)(2,1)} %collective-permute-done.9.refs_10_), channel_id=1, source_target_pairs={{0,8},{8,0},{16,24},{24,16},{32,40},{40,32},{48,56},{56,48},{64,72... | collective-permute-start | bytes 1572872 | tf_op jit(solution)/shard_map/ppermute | solution.py:645
  52.5 5.4 %collective-permute-start.8 = (bf16[256,1024]{1,0:T(8,128)(2,1)}, bf16[256,1024]{1,0:T(8,128)(2,1)S(1)}, u32[]{:S(2)}, u32[]{:S(2)}) collective-permute-start(bf16[256,1024]{1,0:T(8,128)(2,1)} %collective-permute-done.7.refs_8_), channel_id=1, source_target_pairs={{0,8},{8,0},{16,24},{24,16},{32,40},{40,32},{48,56},{56,48},{64,72... | collective-permute-start | bytes 1572872 | tf_op jit(solution)/shard_map/ppermute | solution.py:645
  53.2 4.7 %collective-permute-start.12 = (bf16[176,1024]{1,0:T(8,128)(2,1)}, bf16[176,1024]{1,0:T(8,128)(2,1)S(1)}, u32[]{:S(2)}, u32[]{:S(2)}) collective-permute-start(bf16[176,1024]{1,0:T(8,128)(2,1)} %collective-permute-done.11.refs_12_), channel_id=1, source_target_pairs={{0,8},{8,0},{16,24},{24,16},{32,40},{40,32},{48,56},{56,48},{64,72... | collective-permute-start | bytes 1081352 | tf_op jit(solution)/shard_map/ppermute | solution.py:645
  53.2 4.7 %collective-permute-start.14 = (bf16[176,1024]{1,0:T(8,128)(2,1)}, bf16[176,1024]{1,0:T(8,128)(2,1)S(1)}, u32[]{:S(2)}, u32[]{:S(2)}) collective-permute-start(bf16[176,1024]{1,0:T(8,128)(2,1)} %collective-permute-done.13.refs_14_), channel_id=1, source_target_pairs={{0,8},{8,0},{16,24},{24,16},{32,40},{40,32},{48,56},{56,48},{64,72... | collective-permute-start | bytes 1081352 | tf_op jit(solution)/shard_map/ppermute | solution.py:645
  53.7 4.2 %collective-permute-start.16 = (bf16[160,1024]{1,0:T(8,128)(2,1)}, bf16[160,1024]{1,0:T(8,128)(2,1)S(1)}, u32[]{:S(2)}, u32[]{:S(2)}) collective-permute-start(bf16[160,1024]{1,0:T(8,128)(2,1)} %collective-permute-done.15.refs_16_), channel_id=1, source_target_pairs={{0,8},{8,0},{16,24},{24,16},{32,40},{40,32},{48,56},{56,48},{64,72... | collective-permute-start | bytes 983048 | tf_op jit(solution)/shard_map/ppermute | solution.py:645
  53.8 20.0 %all-to-all-start.1 = ((bf16[16,128,256]{2,1,0:T(8,128)(2,1)}), bf16[16,128,256]{2,1,0:T(8,128)(2,1)S(1)}, u32[]{:S(2)}, u32[]{:S(2)}) async-start(bf16[16,128,256]{2,1,0:T(8,128)(2,1)} %bitcast.28), calls=%async_computation.1 | async-start | bytes 2097152 | tf_op jit(solution)/shard_map/all_to_all | solution.py:704
  57.9 0.7 copy-start.11
  57.9 0.9 copy-start.9
  58.0 0.9 copy-start.10
  58.0 1.1 copy-start.7
  58.0 1.3 %copy-start.8 = (bf16[256,1024]{1,0:T(8,128)(2,1)}, bf16[256,1024]{1,0:T(8,128)(2,1)S(1)}, u32[]{:S(2)}) copy-start(bf16[256,1024]{1,0:T(8,128)(2,1)S(1)} %collective-permute-done.8.refs_9_) | copy-start | bytes 1572868
  73.8 19.3 %copy-start = (bf16[16,128,256]{2,1,0:T(8,128)(2,1)}, bf16[16,128,256]{2,1,0:T(8,128)(2,1)S(1)}, u32[]{:S(2)}) copy-start(bf16[16,128,256]{2,1,0:T(8,128)(2,1)S(1)} %all-to-all-done.1) | copy-start | bytes 3145732
  73.8 29.1 %all-to-all-start.2 = ((bf16[8,832,128]{2,1,0:T(8,128)(2,1)}), bf16[8,832,128]{2,1,0:T(8,128)(2,1)S(1)}, u32[]{:S(2)}, u32[]{:S(2)}) async-start(bf16[8,832,128]{2,1,0:T(8,128)(2,1)} %weight_grads.1), calls=%async_computation.2 | async-start | bytes 3407872 | tf_op jit(solution)/shard_map/all_to_all | solution.py:710

commit v6 on v5

--- a/solution.py
+++ b/solution.py
@@ -127,64 +127,62 @@
     )(x, dy, gain, bias, w_gate, w_up, w_down)
 
 
-def heads_kernel(
-    order, x, dy, w_q, w_k, w_v, w_o, b_q, b_k, b_v, gain, bias,
-    table, out, hid, cosine, sine,
-):
+def heads_kernel(order, x, dy, w_in, w_out_in, b_qkv, gain, bias, table, out, *scratch):
+    w, w_out, cosine, sine, sems = scratch
     lanes = 2 * HEAD_DIM
+    groups = ((0, 256), (256, 512), (512, 1024))
+    copies = []
+    for i, (lo, hi) in enumerate(groups):
+        pairs = [(w_out_in.at[lo:hi, :], w_out.at[lo:hi, :])]
+        for j in range(3):
+            part = slice(j * WIDTH + lo, j * WIDTH + hi)
+            pairs.append((w_in.at[:, part], w.at[:, part]))
+        copies.append([pltpu.make_async_copy(*pair, sems.at[i, j]) for j, pair in enumerate(pairs)])
+        for copy in copies[i]:
+            copy.start()
     lane = lax.broadcasted_iota(jnp.int32, (1, lanes), 1)
     low = lane % HEAD_DIM < ROT // 2
     scale = jnp.where(lane < HEAD_DIM, HEAD_DIM**-0.5, 1.0)
-
-    @pl.when(pl.program_id(0) == 0)
-    def _():
-        unit, _ = normalise(x[...])
-        hid[...] = (unit * gain[...] + bias[...]).astype(bf16)
-        for g in range(HERE // GROUP):
-            rows = slice(g * GROUP, (g + 1) * GROUP)
-            group = order[lax.axis_index("seq") * (HERE // GROUP) + g]
-            cosine[rows, :], sine[rows, :] = group_rotation(table, group)
-
-    q = dot_nn(hid[...], w_q[...]) + b_q[...]
-    k = dot_nn(hid[...], w_k[...]) + b_k[...]
-    v = dot_nn(hid[...], w_v[...]) + b_v[...]
-    grad_att = dot_nt(dy[...], w_o[...])
-    for h in range(BLOCK // HEAD_DIM):
-        part = slice(h * HEAD_DIM, (h + 1) * HEAD_DIM)
-        raw = jnp.concatenate([q[:, part], k[:, part]], 1)
-        before, after = pltpu.roll(raw, ROT // 2, 1), pltpu.roll(raw, lanes - ROT // 2, 1)
-        turned = (raw * cosine[...] + jnp.where(low, -after, before) * sine[...]) * scale
-        rows = slice(h * HERE, (h + 1) * HERE)
-        out[rows, :lanes] = turned.astype(bf16)
-        out[rows, lanes:] = jnp.concatenate([v[:, part], grad_att[:, part]], 1).astype(bf16)
+    for g in range(HERE // GROUP):
+        rows = slice(g * GROUP, (g + 1) * GROUP)
+        group = order[lax.axis_index("seq") * (HERE // GROUP) + g]
+        cosine[rows, :], sine[rows, :] = group_rotation(table, group)
+    unit, _ = normalise(x[...])
+    hid = (unit * gain[...] + bias[...]).astype(bf16)
+    for i, (lo, hi) in enumerate(groups):
+        for copy in copies[i]:
+            copy.wait()
+        parts = [slice(j * WIDTH + lo, j * WIDTH + hi) for j in range(3)]
+        q, k, v = (dot_nn(hid, w[:, part]) + b_qkv[:, part] for part in parts)
+        grad_att = dot_nt(dy[...], w_out[lo:hi, :])
+        for h in range((hi - lo) // HEAD_DIM):
+            part = slice(h * HEAD_DIM, (h + 1) * HEAD_DIM)
+            raw = jnp.concatenate([q[:, part], k[:, part]], 1)
+            before, after = pltpu.roll(raw, ROT // 2, 1), pltpu.roll(raw, lanes - ROT // 2, 1)
+            turned = (raw * cosine[...] + jnp.where(low, -after, before) * sine[...]) * scale
+            at = lo // HEAD_DIM + h
+            rows = slice(at * HERE, (at + 1) * HERE)
+            out[rows, :lanes] = turned.astype(bf16)
+            out[rows, lanes:] = jnp.concatenate([v[:, part], grad_att[:, part]], 1).astype(bf16)
 
 
 def own_heads(order, x, dy, w_qkv, w_out, b_qkv, gain, bias, table):
-    fixed = lambda shape: pl.BlockSpec(shape, lambda j: (0,) * len(shape))
-    own, vector = fixed((HERE, WIDTH)), fixed((1, WIDTH))
-    steps = WIDTH // BLOCK
-
-    def part(rows, i):
-        return pl.BlockSpec((rows, BLOCK), lambda j: (0, i * steps + j))
-
     return pl.pallas_call(
         heads_kernel,
-        grid=(steps,),
         out_shape=jax.ShapeDtypeStruct((LENGTH, 4 * HEAD_DIM), bf16),
-        in_specs=[SMEM]
-        + [own, own, part(WIDTH, 0), part(WIDTH, 1), part(WIDTH, 2)]
-        + [pl.BlockSpec((BLOCK, WIDTH), lambda j: (j, 0)), part(1, 0), part(1, 1), part(1, 2)]
-        + [vector, vector, fixed(table.shape)],
-        out_specs=pl.BlockSpec((4 * HERE, 4 * HEAD_DIM), lambda j: (j, 0)),
+        in_specs=[SMEM] + [VMEM] * 2 + [ANY] * 2 + [VMEM] * 4,
+        out_specs=VMEM,
         scratch_shapes=[
-            pltpu.VMEM((HERE, WIDTH), bf16),
+            pltpu.VMEM((WIDTH, 3 * WIDTH), bf16),
+            pltpu.VMEM((WIDTH, WIDTH), bf16),
             pltpu.VMEM((HERE, 2 * HEAD_DIM), f32),
             pltpu.VMEM((HERE, 2 * HEAD_DIM), f32),
+            pltpu.SemaphoreType.DMA((3, 4)),
         ],
         compiler_params=params(60),
         cost_estimate=cost(1.1, 9),
         name="own_heads",
-    )(order, x, dy, w_qkv, w_qkv, w_qkv, w_out, b_qkv, b_qkv, b_qkv, gain, bias, table)
+    )(order, x, dy, w_qkv, w_out, b_qkv, gain, bias, table)
 
 
 def attention_kernel(*refs):

time: 116 us -> 116 us (level)
  no operation moved by 1% of the time
where the time goes in v6:
time: 116 us
  Pallas kernels  63.6 us (55%)
  starting transfers between devices  30.9 us (27%)
  blocking collectives  10.9 us (9%)
  waiting for transfers between devices  5.02 us (4%)
  local copies, waits for them, and re-layouts  2.29 us (2%)
  other arithmetic  1.83 us (2%)
    ppermute x17, starting transfers between devices, send(): return lax.ppermute(value, 'seq', to)  14.8 us
    pallas_call x1, Pallas kernels, weight_grads(): pl.pallas_call(lambda *refs: weights_kernel(pieces, len(arrays), *refs),...  13.2 us
    pallas_call x1, Pallas kernels, own_rows(): pl.pallas_call(own_kernel, out_shape=[jax.ShapeDtypeStruct((HERE, WIDTH),...  12.1 us
    all_to_all x1, blocking collectives, shards(): mine = lax.all_to_all(outgoing, 'seq', 0, 0, tiled=True)  10.9 us
    pallas_call x1, Pallas kernels, attention(): pl.pallas_call(attention_kernel, out_shape=jax.ShapeDtypeStruct((LENGTH,...  10.9 us
    pallas_call x1, Pallas kernels, final_rows(): pl.pallas_call(final_kernel, grid=(WIDTH // BLOCK,), out_shape=[jax.Shape...  8.02 us
    pallas_call x1, Pallas kernels, first_half(): pl.pallas_call(lambda *refs: first_kernel(pieces, len(arrays), *refs), ou...  7.3 us
    all_to_all x1, starting transfers between devices, shards(): got = lax.all_to_all(block, 'rows', 0, 0, tiled=True)  7.22 us
  transfers between devices with their start and end apart: 20, of which 4 were waited for; matrix products, arithmetic and copies ran while one was open for 1% of the time, Pallas kernels for 54%

profile of v6, /device:TPU:1, one launch (start us, length us, event | category | flops | bytes accessed | tf_op | source)
XLA Modules:
  0.0 115.5 jit_solution(17095016281220117716)
XLA Ops:
  0.6 1.1 pad_maximum_fusion.refs_0_
  1.7 2.2 %collective-permute-start.1 = (bf16[256,1024]{1,0:T(8,128)(2,1)S(1)}, bf16[256,1024]{1,0:T(8,128)(2,1)S(1)}, u32[]{:S(2)}, u32[]{:S(2)}) collective-permute-start(bf16[256,1024]{1,0:T(8,128)(2,1)S(1)} %pad_maximum_fusion.refs_0_), channel_id=1, source_target_pairs={{0,32},{8,40},{16,48},{24,56},{32,64},{40,72},{48,80},{56,88},{64,... | collective-permute-start | bytes 1572872 | tf_op jit(solution)/shard_map/ppermute | solution.py:643
  3.9 1.5 %collective-permute-start.3 = (bf16[256,1024]{1,0:T(8,128)(2,1)S(1)}, bf16[256,1024]{1,0:T(8,128)(2,1)S(1)}, u32[]{:S(2)}, u32[]{:S(2)}) collective-permute-start(bf16[256,1024]{1,0:T(8,128)(2,1)S(1)} %pad_maximum_fusion.refs_0_), channel_id=1, source_target_pairs={{0,96},{8,104},{16,112},{24,120},{32,0},{40,8},{48,16},{56,24},{64... | collective-permute-start | bytes 1572872 | tf_op jit(solution)/shard_map/ppermute | solution.py:643
  5.4 1.2 %collective-permute-start.5 = (bf16[256,1024]{1,0:T(8,128)(2,1)S(1)}, bf16[256,1024]{1,0:T(8,128)(2,1)S(1)}, u32[]{:S(2)}, u32[]{:S(2)}) collective-permute-start(bf16[256,1024]{1,0:T(8,128)(2,1)S(1)} %pad_maximum_fusion.refs_0_), channel_id=1, source_target_pairs={{0,16},{8,24},{16,0},{24,8},{32,48},{40,56},{48,32},{56,40},{64,80... | collective-permute-start | bytes 1572872 | tf_op jit(solution)/shard_map/ppermute | solution.py:643
  6.6 6.8 %own_heads.1 = bf16[2048,256]{1,0:T(8,128)(2,1)} custom-call(s32[32]{0:T(128)} %refs_4_.1, bf16[128,1024]{1,0:T(8,128)(2,1)} %bitcast.23, bf16[128,1024]{1,0:T(8,128)(2,1)} %bitcast.19, bf16[1024,3072]{1,0:T(8,128)(2,1)} %w_qkv.3, bf16[1024,1024]{1,0:T(8,128)(2,1)} %w_out.1, f32[1,3072]{1,0:T(1,128)} %bitcast.39, f32[1,1024]{1,0:T(1,128)} %bitcast.30, ...), custom_call_target="tpu_custom_call" | custom-call | flops 1100000000 | bytes 9437184 | tf_op jit(solution)/shard_map/own_heads/pallas_call | solution.py:170
  13.4 4.8 %all-to-all-start = ((bf16[16,128,256]{2,1,0:T(8,128)(2,1)}), bf16[16,128,256]{2,1,0:T(8,128)(2,1)S(1)}, u32[]{:S(2)}, u32[]{:S(2)}) async-start(bf16[16,128,256]{2,1,0:T(8,128)(2,1)} %bitcast.26), calls=%async_computation | async-start | bytes 2097152 | tf_op jit(solution)/shard_map/all_to_all | solution.py:692
  18.3 0.3 collective-permute-start
  18.6 0.0 collective-permute-done.1.refs_2_
  18.6 0.3 collective-permute-start.2
  18.9 0.2 collective-permute-start.4
  19.1 0.7 collective-permute-start.6
  19.8 3.6 %cut_weights.1 = (bf16[192,1024]{1,0:T(8,128)(2,1)}, bf16[352,1024]{1,0:T(8,128)(2,1)}) custom-call(bf16[1024,3072]{1,0:T(8,128)(2,1)} %w_qkv.3, bf16[1024,2816]{1,0:T(8,128)(2,1)} %wg_in.1, bf16[1024,2816]{1,0:T(8,128)(2,1)} %wu_in.1), custom_call_target="tpu_custom_call" | custom-call | flops 1000000 | bytes 1048 | tf_op jit(solution)/shard_map/cut_weights/pallas_call | solution.py:301
  23.4 2.4 %collective-permute-start.11 = (bf16[176,1024]{1,0:T(8,128)(2,1)S(1)}, bf16[176,1024]{1,0:T(8,128)(2,1)}, u32[]{:S(2)}, u32[]{:S(2)}) collective-permute-start(bf16[176,1024]{1,0:T(8,128)(2,1)S(1)} %slice.12), channel_id=1, source_target_pairs={{0,96},{8,104},{16,112},{24,120},{32,0},{40,8},{48,16},{56,24},{64... | collective-permute-start | bytes 1081352 | tf_op jit(solution)/shard_map/ppermute | solution.py:643
  25.8 0.8 pad_maximum_fusion.1
  26.6 0.0 collective-permute-done.refs_1_
  26.6 0.0 collective-permute-start.13
  26.6 1.3 %collective-permute-start.15 = (bf16[160,1024]{1,0:T(8,128)(2,1)}, bf16[160,1024]{1,0:T(8,128)(2,1)}, u32[]{:S(2)}, u32[]{:S(2)}) collective-permute-start(bf16[160,1024]{1,0:T(8,128)(2,1)} %pad_maximum_fusion.1), channel_id=1, source_target_pairs={{0,16},{8,24},{16,0},{24,8},{32,48},{40,56},{48,32},{56,40},{64,80... | collective-permute-start | bytes 983048 | tf_op jit(solution)/shard_map/ppermute | solution.py:643
  27.9 0.0 collective-permute-done.4.refs_5_
  27.9 2.6 %collective-permute-start.9 = (bf16[256,1024]{1,0:T(8,128)(2,1)S(1)}, bf16[256,1024]{1,0:T(8,128)(2,1)}, u32[]{:S(2)}, u32[]{:S(2)}) collective-permute-start(bf16[256,1024]{1,0:T(8,128)(2,1)S(1)} %collective-permute-done.3.refs_4_), channel_id=1, source_target_pairs={{0,112},{8,120},{16,96},{24,104},{32,16},{40,24},{48,0},{56,8},{64... | collective-permute-start | bytes 1572872 | tf_op jit(solution)/shard_map/ppermute | solution.py:643
  30.5 0.0 collective-permute-start.7
  30.5 7.3 %first_half.1 = (bf16[1024,1024]{1,0:T(8,128)(2,1)}, bf16[176,1024]{1,0:T(8,128)(2,1)}, bf16[352,1024]{1,0:T(8,128)(2,1)}, f32[352,128]{1,0:T(8,128)}) custom-call(bf16[256,1024]{1,0:T(8,128)(2,1)} %copy-done.1, bf16[256,1024]{1,0:T(8,128)(2,1)} %copy-done.6, bf16[256,1024]{1,0:T(8,128)(2,1)} %copy-done.4, bf16[256,1024]{1,0:T(8,128)(2,1)} %collective-permute-done.2.refs_3_, ...), custom_call_target="tpu_custom_call" | custom-call | flops 1000000 | bytes 1048 | tf_op jit(solution)/shard_map/first_half/pallas_call | solution.py:383
  37.8 1.0 copy-done.3
  38.8 10.9 %attention.1.refs_18_ = bf16[2048,256]{1,0:T(8,128)(2,1)} custom-call(bf16[1024,1024]{1,0:T(8,128)(2,1)} %get-tuple-element.41.refs_0_.refs_24_, bf16[176,1024]{1,0:T(8,128)(2,1)} %get-tuple-element.42.refs_1_.refs_25_, bf16[352,1024]{1,0:T(8,128)(2,1)} %get-tuple-element.43.refs_2_.refs_26_, f32[352,128]{1,0:T(8,128)} %get-tuple-element.44.refs_3_.refs_27_, ...), custom_call_target="tpu_custom_call" | custom-call | flops 15000000512 | bytes 8388608 | tf_op jit(solution)/shard_map/attention/pallas_call | solution.py:257
  49.7 1.6 %collective-permute-done.9.refs_10_ = bf16[256,1024]{1,0:T(8,128)(2,1)} collective-permute-done((bf16[256,1024]{1,0:T(8,128)(2,1)S(1)}, bf16[256,1024]{1,0:T(8,128)(2,1)}, u32[]{:S(2)}, u32[]{:S(2)}) %collective-permute-start.9) | collective-permute-done | bytes 524320 | tf_op jit(solution)/shard_map/ppermute | solution.py:643
  51.3 0.9 collective-permute-start.10
  52.2 0.3 collective-permute-done.7.refs_8_
  52.4 0.7 collective-permute-start.8
  53.1 0.0 collective-permute-start.12
  53.1 0.5 collective-permute-start.14
  53.6 0.0 collective-permute-done.15.refs_16_
  53.6 0.1 collective-permute-start.16
  53.7 4.1 %all-to-all-start.1 = ((bf16[16,128,256]{2,1,0:T(8,128)(2,1)}), bf16[16,128,256]{2,1,0:T(8,128)(2,1)S(1)}, u32[]{:S(2)}, u32[]{:S(2)}) async-start(bf16[16,128,256]{2,1,0:T(8,128)(2,1)} %bitcast.28), calls=%async_computation.1 | async-start | bytes 2097152 | tf_op jit(solution)/shard_map/all_to_all | solution.py:702
  57.8 0.0 collective-permute-done.16.refs_17_
  57.8 0.0 collective-permute-done.14.refs_15_
  57.9 0.6 copy-done.11
  58.5 0.1 copy-done.9
  58.7 0.1 copy-done.10
  58.8 0.2 copy-done.7
  59.0 0.2 copy-done.8
  59.1 13.2 %weight_grads.1 = bf16[8,832,128]{2,1,0:T(8,128)(2,1)} custom-call(bf16[256,1024]{1,0:T(8,128)(2,1)} %copy-done.1, bf16[256,1024]{1,0:T(8,128)(2,1)} %copy-done.6, bf16[256,1024]{1,0:T(8,128)(2,1)} %copy-done.4, bf16[256,1024]{1,0:T(8,128)(2,1)} %collective-permute-done.2.refs_3_, bf16[256,1024]{1,0:T(8,128)(2,1)} %copy-done.5, ...), custom_call_target="tpu_custom_call" | custom-call | flops 8000000000 | bytes 20971520 | tf_op jit(solution)/shard_map/weight_grads/pallas_call | solution.py:493
  72.3 1.4 %all-to-all-done.1 = bf16[16,128,256]{2,1,0:T(8,128)(2,1)S(1)} async-done(((bf16[16,128,256]{2,1,0:T(8,128)(2,1)}), bf16[16,128,256]{2,1,0:T(8,128)(2,1)S(1)}, u32[]{:S(2)}, u32[]{:S(2)}) %all-to-all-start.1) | async-done | bytes 1048608 | tf_op jit(solution)/shard_map/all_to_all | solution.py:702
  73.7 7.2 %all-to-all-start.2 = ((bf16[8,832,128]{2,1,0:T(8,128)(2,1)}), bf16[8,832,128]{2,1,0:T(8,128)(2,1)S(1)}, u32[]{:S(2)}, u32[]{:S(2)}) async-start(bf16[8,832,128]{2,1,0:T(8,128)(2,1)} %weight_grads.1), calls=%async_computation.2 | async-start | bytes 3407872 | tf_op jit(solution)/shard_map/all_to_all | solution.py:708
  80.9 12.1 %own_rows.1 = (f32[128,1024]{1,0:T(8,128)}, f32[128,1024]{1,0:T(8,128)}) custom-call(bf16[128,1024]{1,0:T(8,128)(2,1)} %bitcast.24, bf16[128,1024]{1,0:T(8,128)(2,1)} %bitcast.20, f32[1,1024]{1,0:T(1,128)} %bitcast.33, f32[1,1024]{1,0:T(1,128)} %bitcast.38, bf16[1024,2816]{1,0:T(8,128)(2,1)} %wg_in.1, bf16[1024,2816]{1,0:T(8,128)(2,1)} %wu_in.1, ...), custom_call_target="tpu_custom_call" | custom-call | flops 4499999744 | bytes 18874368 | tf_op jit(solution)/shard_map/own_rows/pallas_call | solution.py:113
  93.0 8.0 %final_rows.1 = (bf16[128,1024]{1,0:T(8,128)(2,1)}, bf16[128,1024]{1,0:T(8,128)(2,1)}) custom-call(bf16[2048,256]{1,0:T(8,128)(2,1)} %bitcast.27, bf16[128,1024]{1,0:T(8,128)(2,1)} %bitcast.25, bf16[128,1024]{1,0:T(8,128)(2,1)} %bitcast.21, f32[128,1024]{1,0:T(8,128)} %get-tuple-element.54.part, f32[128,1024]{1,0:T(8,128)} %get-tuple-element.55.grad, ...), custom_call_target="tpu_custom_call" | custom-call | flops 1100000000 | bytes 10485760 | tf_op jit(solution)/shard_map/final_rows/pallas_call | solution.py:550
  101.0 1.8 %all-to-all-done.2.got = bf16[8,832,128]{2,1,0:T(8,128)(2,1)S(1)} async-done(((bf16[8,832,128]{2,1,0:T(8,128)(2,1)}), bf16[8,832,128]{2,1,0:T(8,128)(2,1)S(1)}, u32[]{:S(2)}, u32[]{:S(2)}) %all-to-all-start.2) | async-done | bytes 1703968 | tf_op jit(solution)/shard_map/all_to_all | solution.py:708
  102.8 1.0 sum_rows.1
  103.8 10.9 %all_to_all.39 = bf16[16,8,640]{2,1,0:T(8,128)(2,1)S(1)} all-to-all(bf16[16,8,640]{2,1,0:T(8,128)(2,1)S(1)} %bitcast.17), channel_id=1, replica_groups=mesh['seq'=16,'rows'=8] {'seq'}, dimensions={0} | all-to-all | bytes 327680 | tf_op jit(solution)/shard_map/all_to_all | solution.py:714
  114.7 0.8 last_layout.1
  (31 shorter events, 0.1 us)
Async XLA Ops:
  1.7 16.6 %copy-start.1 = (bf16[256,1024]{1,0:T(8,128)(2,1)}, bf16[256,1024]{1,0:T(8,128)(2,1)S(1)}, u32[]{:S(2)}) copy-start(bf16[256,1024]{1,0:T(8,128)(2,1)S(1)} %pad_maximum_fusion.refs_0_) | copy-start | bytes 1572868
  1.7 16.9 %collective-permute-start.1 = (bf16[256,1024]{1,0:T(8,128)(2,1)S(1)}, bf16[256,1024]{1,0:T(8,128)(2,1)S(1)}, u32[]{:S(2)}, u32[]{:S(2)}) collective-permute-start(bf16[256,1024]{1,0:T(8,128)(2,1)S(1)} %pad_maximum_fusion.refs_0_), channel_id=1, source_target_pairs={{0,32},{8,40},{16,48},{24,56},{32,64},{40,72},{48,80},{56,88},{64,... | collective-permute-start | bytes 1572872 | tf_op jit(solution)/shard_map/ppermute | solution.py:643
  3.9 15.0 %collective-permute-start.3 = (bf16[256,1024]{1,0:T(8,128)(2,1)S(1)}, bf16[256,1024]{1,0:T(8,128)(2,1)S(1)}, u32[]{:S(2)}, u32[]{:S(2)}) collective-permute-start(bf16[256,1024]{1,0:T(8,128)(2,1)S(1)} %pad_maximum_fusion.refs_0_), channel_id=1, source_target_pairs={{0,96},{8,104},{16,112},{24,120},{32,0},{40,8},{48,16},{56,24},{64... | collective-permute-start | bytes 1572872 | tf_op jit(solution)/shard_map/ppermute | solution.py:643
  5.4 13.7 %collective-permute-start.5 = (bf16[256,1024]{1,0:T(8,128)(2,1)S(1)}, bf16[256,1024]{1,0:T(8,128)(2,1)S(1)}, u32[]{:S(2)}, u32[]{:S(2)}) collective-permute-start(bf16[256,1024]{1,0:T(8,128)(2,1)S(1)} %pad_maximum_fusion.refs_0_), channel_id=1, source_target_pairs={{0,16},{8,24},{16,0},{24,8},{32,48},{40,56},{48,32},{56,40},{64,80... | collective-permute-start | bytes 1572872 | tf_op jit(solution)/shard_map/ppermute | solution.py:643
  13.4 24.4 %all-to-all-start = ((bf16[16,128,256]{2,1,0:T(8,128)(2,1)}), bf16[16,128,256]{2,1,0:T(8,128)(2,1)S(1)}, u32[]{:S(2)}, u32[]{:S(2)}) async-start(bf16[16,128,256]{2,1,0:T(8,128)(2,1)} %bitcast.26), calls=%async_computation | async-start | bytes 2097152 | tf_op jit(solution)/shard_map/all_to_all | solution.py:692
  18.3 8.3 %collective-permute-start = (bf16[256,1024]{1,0:T(8,128)(2,1)S(1)}, bf16[256,1024]{1,0:T(8,128)(2,1)S(1)}, u32[]{:S(2)}, u32[]{:S(2)}) collective-permute-start(bf16[256,1024]{1,0:T(8,128)(2,1)S(1)} %pad_maximum_fusion.refs_0_), channel_id=1, source_target_pairs={{0,8},{8,0},{16,24},{24,16},{32,40},{40,32},{48,56},{56,48},{64,72... | collective-permute-start | bytes 1572872 | tf_op jit(solution)/shard_map/ppermute | solution.py:643
  18.6 11.9 %copy-start.4 = (bf16[256,1024]{1,0:T(8,128)(2,1)}, bf16[256,1024]{1,0:T(8,128)(2,1)S(1)}, u32[]{:S(2)}) copy-start(bf16[256,1024]{1,0:T(8,128)(2,1)S(1)} %collective-permute-done.1.refs_2_) | copy-start | bytes 1572868
  18.6 8.0 %collective-permute-start.2 = (bf16[256,1024]{1,0:T(8,128)(2,1)S(1)}, bf16[256,1024]{1,0:T(8,128)(2,1)}, u32[]{:S(2)}, u32[]{:S(2)}) collective-permute-start(bf16[256,1024]{1,0:T(8,128)(2,1)S(1)} %collective-permute-done.1.refs_2_), channel_id=1, source_target_pairs={{0,8},{8,0},{16,24},{24,16},{32,40},{40,32},{48,56},{56,48},{64,72... | collective-permute-start | bytes 1572872 | tf_op jit(solution)/shard_map/ppermute | solution.py:643
  18.9 9.0 %copy-start.5 = (bf16[256,1024]{1,0:T(8,128)(2,1)}, bf16[256,1024]{1,0:T(8,128)(2,1)S(1)}, u32[]{:S(2)}) copy-start(bf16[256,1024]{1,0:T(8,128)(2,1)S(1)} %collective-permute-done.3.refs_4_) | copy-start | bytes 1572868
  18.9 9.0 %collective-permute-start.4 = (bf16[256,1024]{1,0:T(8,128)(2,1)S(1)}, bf16[256,1024]{1,0:T(8,128)(2,1)}, u32[]{:S(2)}, u32[]{:S(2)}) collective-permute-start(bf16[256,1024]{1,0:T(8,128)(2,1)S(1)} %collective-permute-done.3.refs_4_), channel_id=1, source_target_pairs={{0,8},{8,0},{16,24},{24,16},{32,40},{40,32},{48,56},{56,48},{64,72... | collective-permute-start | bytes 1572872 | tf_op jit(solution)/shard_map/ppermute | solution.py:643
  19.1 4.3 %copy-start.2 = (bf16[256,1024]{1,0:T(8,128)(2,1)}, bf16[256,1024]{1,0:T(8,128)(2,1)S(1)}, u32[]{:S(2)}) copy-start(bf16[256,1024]{1,0:T(8,128)(2,1)S(1)} %collective-permute-done.5.refs_6_) | copy-start | bytes 1572868
  19.1 11.4 %collective-permute-start.6 = (bf16[256,1024]{1,0:T(8,128)(2,1)S(1)}, bf16[256,1024]{1,0:T(8,128)(2,1)}, u32[]{:S(2)}, u32[]{:S(2)}) collective-permute-start(bf16[256,1024]{1,0:T(8,128)(2,1)S(1)} %collective-permute-done.5.refs_6_), channel_id=1, source_target_pairs={{0,8},{8,0},{16,24},{24,16},{32,40},{40,32},{48,56},{56,48},{64,72... | collective-permute-start | bytes 1572872 | tf_op jit(solution)/shard_map/ppermute | solution.py:643
  23.4 29.7 %collective-permute-start.11 = (bf16[176,1024]{1,0:T(8,128)(2,1)S(1)}, bf16[176,1024]{1,0:T(8,128)(2,1)}, u32[]{:S(2)}, u32[]{:S(2)}) collective-permute-start(bf16[176,1024]{1,0:T(8,128)(2,1)S(1)} %slice.12), channel_id=1, source_target_pairs={{0,96},{8,104},{16,112},{24,120},{32,0},{40,8},{48,16},{56,24},{64... | collective-permute-start | bytes 1081352 | tf_op jit(solution)/shard_map/ppermute | solution.py:643
  26.6 3.9 %copy-start.6 = (bf16[256,1024]{1,0:T(8,128)(2,1)}, bf16[256,1024]{1,0:T(8,128)(2,1)S(1)}, u32[]{:S(2)}) copy-start(bf16[256,1024]{1,0:T(8,128)(2,1)S(1)} %collective-permute-done.refs_1_) | copy-start | bytes 1572868
  26.6 26.5 %collective-permute-start.13 = (bf16[176,1024]{1,0:T(8,128)(2,1)S(1)}, bf16[176,1024]{1,0:T(8,128)(2,1)}, u32[]{:S(2)}, u32[]{:S(2)}) collective-permute-start(bf16[176,1024]{1,0:T(8,128)(2,1)S(1)} %slice.12), channel_id=1, source_target_pairs={{0,32},{8,40},{16,48},{24,56},{32,64},{40,72},{48,80},{56,88},{64,... | collective-permute-start | bytes 1081352 | tf_op jit(solution)/shard_map/ppermute | solution.py:643
  26.6 27.0 %collective-permute-start.15 = (bf16[160,1024]{1,0:T(8,128)(2,1)}, bf16[160,1024]{1,0:T(8,128)(2,1)}, u32[]{:S(2)}, u32[]{:S(2)}) collective-permute-start(bf16[160,1024]{1,0:T(8,128)(2,1)} %pad_maximum_fusion.1), channel_id=1, source_target_pairs={{0,16},{8,24},{16,0},{24,8},{32,48},{40,56},{48,32},{56,40},{64,80... | collective-permute-start | bytes 983048 | tf_op jit(solution)/shard_map/ppermute | solution.py:643
  27.9 23.4 %collective-permute-start.9 = (bf16[256,1024]{1,0:T(8,128)(2,1)S(1)}, bf16[256,1024]{1,0:T(8,128)(2,1)}, u32[]{:S(2)}, u32[]{:S(2)}) collective-permute-start(bf16[256,1024]{1,0:T(8,128)(2,1)S(1)} %collective-permute-done.3.refs_4_), channel_id=1, source_target_pairs={{0,112},{8,120},{16,96},{24,104},{32,16},{40,24},{48,0},{56,8},{64... | collective-permute-start | bytes 1572872 | tf_op jit(solution)/shard_map/ppermute | solution.py:643
  30.5 21.9 %collective-permute-start.7 = (bf16[256,1024]{1,0:T(8,128)(2,1)S(1)}, bf16[256,1024]{1,0:T(8,128)(2,1)}, u32[]{:S(2)}, u32[]{:S(2)}) collective-permute-start(bf16[256,1024]{1,0:T(8,128)(2,1)S(1)} %collective-permute-done.1.refs_2_), channel_id=1, source_target_pairs={{0,32},{8,40},{16,48},{24,56},{32,64},{40,72},{48,80},{56,88},{64,... | collective-permute-start | bytes 1572872 | tf_op jit(solution)/shard_map/ppermute | solution.py:643
  37.8 1.0 copy-start.3
  51.3 6.6 %collective-permute-start.10 = (bf16[256,1024]{1,0:T(8,128)(2,1)}, bf16[256,1024]{1,0:T(8,128)(2,1)S(1)}, u32[]{:S(2)}, u32[]{:S(2)}) collective-permute-start(bf16[256,1024]{1,0:T(8,128)(2,1)} %collective-permute-done.9.refs_10_), channel_id=1, source_target_pairs={{0,8},{8,0},{16,24},{24,16},{32,40},{40,32},{48,56},{56,48},{64,72... | collective-permute-start | bytes 1572872 | tf_op jit(solution)/shard_map/ppermute | solution.py:643
  52.4 5.4 %collective-permute-start.8 = (bf16[256,1024]{1,0:T(8,128)(2,1)}, bf16[256,1024]{1,0:T(8,128)(2,1)S(1)}, u32[]{:S(2)}, u32[]{:S(2)}) collective-permute-start(bf16[256,1024]{1,0:T(8,128)(2,1)} %collective-permute-done.7.refs_8_), channel_id=1, source_target_pairs={{0,8},{8,0},{16,24},{24,16},{32,40},{40,32},{48,56},{56,48},{64,72... | collective-permute-start | bytes 1572872 | tf_op jit(solution)/shard_map/ppermute | solution.py:643
  53.1 4.7 %collective-permute-start.12 = (bf16[176,1024]{1,0:T(8,128)(2,1)}, bf16[176,1024]{1,0:T(8,128)(2,1)S(1)}, u32[]{:S(2)}, u32[]{:S(2)}) collective-permute-start(bf16[176,1024]{1,0:T(8,128)(2,1)} %collective-permute-done.11.refs_12_), channel_id=1, source_target_pairs={{0,8},{8,0},{16,24},{24,16},{32,40},{40,32},{48,56},{56,48},{64,72... | collective-permute-start | bytes 1081352 | tf_op jit(solution)/shard_map/ppermute | solution.py:643
  53.1 4.7 %collective-permute-start.14 = (bf16[176,1024]{1,0:T(8,128)(2,1)}, bf16[176,1024]{1,0:T(8,128)(2,1)S(1)}, u32[]{:S(2)}, u32[]{:S(2)}) collective-permute-start(bf16[176,1024]{1,0:T(8,128)(2,1)} %collective-permute-done.13.refs_14_), channel_id=1, source_target_pairs={{0,8},{8,0},{16,24},{24,16},{32,40},{40,32},{48,56},{56,48},{64,72... | collective-permute-start | bytes 1081352 | tf_op jit(solution)/shard_map/ppermute | solution.py:643
  53.6 4.2 %collective-permute-start.16 = (bf16[160,1024]{1,0:T(8,128)(2,1)}, bf16[160,1024]{1,0:T(8,128)(2,1)S(1)}, u32[]{:S(2)}, u32[]{:S(2)}) collective-permute-start(bf16[160,1024]{1,0:T(8,128)(2,1)} %collective-permute-done.15.refs_16_), channel_id=1, source_target_pairs={{0,8},{8,0},{16,24},{24,16},{32,40},{40,32},{48,56},{56,48},{64,72... | collective-permute-start | bytes 983048 | tf_op jit(solution)/shard_map/ppermute | solution.py:643
  53.7 20.0 %all-to-all-start.1 = ((bf16[16,128,256]{2,1,0:T(8,128)(2,1)}), bf16[16,128,256]{2,1,0:T(8,128)(2,1)S(1)}, u32[]{:S(2)}, u32[]{:S(2)}) async-start(bf16[16,128,256]{2,1,0:T(8,128)(2,1)} %bitcast.28), calls=%async_computation.1 | async-start | bytes 2097152 | tf_op jit(solution)/shard_map/all_to_all | solution.py:702
  57.8 0.7 copy-start.11
  57.8 0.9 copy-start.9
  57.8 0.9 copy-start.10
  57.9 1.1 copy-start.7
  57.9 1.3 %copy-start.8 = (bf16[256,1024]{1,0:T(8,128)(2,1)}, bf16[256,1024]{1,0:T(8,128)(2,1)S(1)}, u32[]{:S(2)}) copy-start(bf16[256,1024]{1,0:T(8,128)(2,1)S(1)} %collective-permute-done.8.refs_9_) | copy-start | bytes 1572868
  73.7 19.3 %copy-start = (bf16[16,128,256]{2,1,0:T(8,128)(2,1)}, bf16[16,128,256]{2,1,0:T(8,128)(2,1)S(1)}, u32[]{:S(2)}) copy-start(bf16[16,128,256]{2,1,0:T(8,128)(2,1)S(1)} %all-to-all-done.1) | copy-start | bytes 3145732
  73.7 29.1 %all-to-all-start.2 = ((bf16[8,832,128]{2,1,0:T(8,128)(2,1)}), bf16[8,832,128]{2,1,0:T(8,128)(2,1)S(1)}, u32[]{:S(2)}, u32[]{:S(2)}) async-start(bf16[8,832,128]{2,1,0:T(8,128)(2,1)} %weight_grads.1), calls=%async_computation.2 | async-start | bytes 3407872 | tf_op jit(solution)/shard_map/all_to_all | solution.py:708
